TPU v7x, 32 devices: a whole 2x2x4 slice. The times are simulated.
32 devices in a mesh: lat: 8 (over z, x), lon: 4 (over y, core).
Axes of the slice: x: 2, y: 2, z: 4, core: 2. Of those that a mesh axis runs over, the one named last changes fastest.
Arguments:
- state: float32 [128, 1440, 256], P('lat', 'lon'), may hold values from -6 to 6
- winds: bfloat16 [128, 1440, 128], P('lat', 'lon'), may hold values from -0.44921875 to 0.44921875
- decay: float32 [4], replicated, may hold values from 0.005 to 0.5
- widths: int32 [128], replicated, may hold values from 0 to 480, as said below
Outputs:
- advected: bfloat16 [128, 1440, 256], P('lat', 'lon')
Inputs may be any that keep to these rules, and one draw needn't show every extreme that they name: widths is 0 on rows 32 to 95 and at least 1 on the other rows; the first and last rows have exactly 480.
All inputs are finite; a program needn't handle non-finite values.
Results may differ from a plain program's by a relative error of at most 0.0075.
Values may be sent and summed in bfloat16 or wider, within the bound.
No kernel may reach another device: no remote copies, remote signals or barrier semaphores. Data moves between devices by JAX's collectives and lax.ppermute only.
A program may use at most 128 MiB of HBM per device.

v0:
```python
import functools

import jax
import jax.numpy as jnp
from jax import lax
from jax.experimental import pallas as pl
from jax.experimental.pallas import tpu as pltpu
from jax.sharding import PartitionSpec as P

ADV_STEPS = 4
REACH = 2 * ADV_STEPS
ROUND = 2
HALO = 2 * ROUND
HMAX = 480
LANES = 128
PIECES = 4
VMEM_LIMIT = 56 * 1024 * 1024
PAD = 8
COLS = 48


def tie(*values):
    return lax.optimization_barrier(values)


def round_up(value, unit):
    return -(-value // unit) * unit


def smooth_kernel(geo, first, info_ref, widths_ref, own_ref, sib_ref, opp_ref, diag_ref, q_ref, carry_ref, far_ref, scale_ref,
                  extra_ref, out_ref, cells, east_sum, west_sum):
    @pl.when(info_ref[1] == 1)
    def _():
        smooth_rows(geo, first, info_ref[0] == 1, widths_ref, own_ref, sib_ref, opp_ref, diag_ref,
                    q_ref, carry_ref, far_ref, scale_ref, out_ref, cells, east_sum, west_sum)
        rows = own_ref.shape[0]
        if out_ref.shape[0] > rows:
            out_ref[rows] = extra_ref[0]


def smooth_rows(geo, first, odd, widths_ref, own_ref, sib_ref, opp_ref, diag_ref, q_ref, carry_ref, far_ref, scale_ref,
                out_ref, cells, east_sum, west_sum):
    lon, back, span, seg, ext = geo
    rows, tiles = own_ref.shape[0], own_ref.shape[2] // LANES
    chains = [(r, t) for r in range(rows) for t in range(tiles)]

    def put(ref, start, begin, count):
        @pl.loop(0, rows)
        def _(r):
            for t in range(tiles):
                part = ref[r, pl.ds(begin, count), pl.ds(t * LANES, LANES)]
                cells[r * tiles + t, pl.ds(start, count), :] = part.astype(jnp.float32)

    head = back - lon
    put(opp_ref, 0, lon - head, head)
    put(own_ref, back, 0, lon)
    put(opp_ref, back + 2 * lon, 0, span - REACH - 2 * lon)

    @pl.when(odd)
    def _():
        put(sib_ref, back - lon, 0, lon)
        put(diag_ref, back + lon, 0, lon)

    @pl.when(jnp.logical_not(odd))
    def _():
        put(diag_ref, back - lon, 0, lon)
        put(sib_ref, back + lon, 0, lon)

    q = [jnp.broadcast_to(q_ref[0:1, t * LANES:(t + 1) * LANES], (8, LANES)) for t in range(tiles)]
    jump = [carry_ref[0:1, t * LANES:(t + 1) * LANES] for t in range(tiles)]
    zero = jnp.zeros((8, LANES), jnp.float32)
    none = jnp.zeros((1, LANES), jnp.float32)
    east_base = back - REACH

    for base, total, forward in ((east_base, east_sum, False), (0, west_sum, True)):
        def at(i, forward=forward):
            return i if forward else seg - 1 - i

        def totals(i, acc, base=base):
            return tuple(cells[r * tiles + t, pl.ds(base + at(i), 8, stride=seg), :] + q[t] * acc[n]
                         for n, (r, t) in enumerate(chains))

        acc = lax.fori_loop(0, seg, totals, (zero,) * len(chains), unroll=4)
        start = []
        for n, (r, t) in enumerate(chains):
            carry = none
            parts = [None] * 8
            for k in (range(8) if forward else range(7, -1, -1)):
                parts[k] = carry
                carry = acc[n][k:k + 1] + jump[t] * carry
            start.append(jnp.concatenate(parts, axis=0))

        def sums(i, acc, base=base, total=total):
            new = []
            for n, (r, t) in enumerate(chains):
                v = cells[r * tiles + t, pl.ds(base + at(i), 8, stride=seg), :] + q[t] * acc[n]
                total[r * tiles + t, pl.ds(at(i), 8, stride=seg), :] = v
                new.append(v)
            return tuple(new)

        lax.fori_loop(0, seg, sums, tuple(start), unroll=4)

    step = COLS

    @pl.loop(0, rows)
    def _(r):
        width = widths_ref[first + r]
        for t in range(tiles):
            n = r * tiles + t
            far = jnp.broadcast_to(far_ref[r, 0:1, t * LANES:(t + 1) * LANES], (step, LANES))
            scale = jnp.broadcast_to(scale_ref[r, 0:1, t * LANES:(t + 1) * LANES], (step, LANES))
            for c in range(0, ext, step):
                near = east_sum[n, pl.ds(c, step), :] + west_sum[n, pl.ds(back - REACH + c, step), :]
                cut = east_sum[n, pl.ds(c + 1 + width, step), :] + west_sum[n, pl.ds(back - REACH + c - 1 - width, step), :]
                mid = cells[n, pl.ds(back - REACH + c, step), :]
                out_ref[r, pl.ds(c, step), pl.ds(t * LANES, LANES)] = ((near - mid - far * cut) * scale).astype(jnp.bfloat16)


def smooth_chunk(first, rows, ext, info, widths, own, sib, opp, diag, q, carry, far, scale, extra):
    lon, channels = own.shape[1:]
    tiles = channels // LANES
    back = round_up(HMAX + 1 + REACH, 8)
    span = round_up(ext + HMAX + 1, 8)
    seg = max(back + ext - REACH, span) // 8
    geo = (lon, back, 8 * seg, seg, ext)
    more = 0 if extra is None else 1
    if extra is None:
        extra = jnp.zeros((1, ext, channels), jnp.bfloat16)
    smem, vmem = pl.BlockSpec(memory_space=pltpu.SMEM), pl.BlockSpec(memory_space=pltpu.VMEM)
    part = pl.BlockSpec((rows, lon, channels), lambda i: (first // rows, 0, 0))
    table = pl.BlockSpec((rows, 1, channels), lambda i: (first // rows, 0, 0))
    return pl.pallas_call(
        functools.partial(smooth_kernel, geo, first),
        grid=(1,),
        in_specs=[smem, smem, vmem, part, vmem, vmem, vmem, vmem, table, table, vmem],
        out_specs=pl.BlockSpec((rows + more, ext, channels), lambda i: (0, 0, 0)),
        out_shape=jax.ShapeDtypeStruct((rows + more, ext, channels), jnp.bfloat16),
        scratch_shapes=[
            pltpu.VMEM((rows * tiles, back - REACH + 8 * seg, LANES), jnp.float32),
            pltpu.VMEM((rows * tiles, 8 * seg, LANES), jnp.float32),
            pltpu.VMEM((rows * tiles, 8 * seg, LANES), jnp.float32),
        ],
        compiler_params=pltpu.CompilerParams(vmem_limit_bytes=VMEM_LIMIT),
        cost_estimate=pl.CostEstimate(flops=1000, bytes_accessed=1000, transcendentals=0),
        name="smooth",
    )(info, widths, own, sib, opp, diag, q, carry, far, scale, extra)


def update(src, r, t, c, count, u, v, zero):
    def at(dr, dc):
        return src[r + dr, t, pl.ds(PAD + c + dc + (zero if dc else 0), count), :]

    mid = at(0, 0)
    mid30 = 30.0 * mid
    e1, w1, e2, w2 = at(0, 1), at(0, -1), at(0, 2), at(0, -2)
    n1, s1, n2, s2 = at(1, 0), at(-1, 0), at(2, 0), at(-2, 0)
    first_x = (e2 - w2) - 8.0 * (e1 - w1)
    second_x = 16.0 * (e1 + w1) - (e2 + w2) - mid30
    first_y = (n2 - s2) - 8.0 * (n1 - s1)
    second_y = 16.0 * (n1 + s1) - (n2 + s2) - mid30
    change = u * (first_x + (6.0 * u) * second_x) + v * (first_y + (6.0 * v) * second_y)
    return mid + change


def put_rows(field, ref, base, count, ext):
    @pl.loop(0, count)
    def _(r):
        for t in range(field.shape[1]):
            field[base + r, t, pl.ds(PAD, ext), :] = ref[r, :, pl.ds(t * LANES, LANES)].astype(jnp.float32)


def step_rows(source, winds, zero, first, last, offset, start, stop, store):
    @pl.loop(first, last)
    def _(r):
        for c in range(start, stop, COLS):
            count = min(COLS, stop - c)
            u = winds[r + offset, pl.ds(c, count), pl.ds(0, LANES)].astype(jnp.float32) * (1.0 / 12.0)
            v = winds[r + offset, pl.ds(c, count), pl.ds(LANES, LANES)].astype(jnp.float32) * (1.0 / 12.0)
            for t in range(source.shape[1]):
                store(r, t, c, count, update(source, r + 2, t, c, count, u, v, zero))


class Copies:
    def __init__(self, sems):
        self.sems, self.used = sems, 0

    def start(self, source, target):
        copy = pltpu.make_async_copy(source, target, self.sems.at[self.used])
        self.used += 1
        copy.start()
        return copy

    def either(self, flag, source, other, target):
        sem = self.sems.at[self.used]
        self.used += 1

        @pl.when(flag)
        def _():
            pltpu.make_async_copy(source, target, sem).start()

        @pl.when(jnp.logical_not(flag))
        def _():
            pltpu.make_async_copy(other, target, sem).start()

        return pltpu.make_async_copy(source, target, sem)


def store_in(field):
    def store(r, t, c, count, value):
        field[r, t, pl.ds(PAD + c, count), :] = value

    return store


def store_out(ref):
    def store(r, t, c, count, value):
        ref[r, pl.ds(c - REACH, count), pl.ds(t * LANES, LANES)] = value.astype(jnp.bfloat16)

    return store


def start_own_rows(geo, polar, state_ref, smooth_refs, staged, field, base, first, count, sems):
    lon, part = geo[0], count // len(smooth_refs)

    @pl.when(polar)
    def _():
        for i, ref in enumerate(smooth_refs):
            pltpu.make_async_copy(ref.at[pl.ds(0, part)], staged.at[pl.ds(i * part, part)], sems.at[i]).start()

    @pl.when(jnp.logical_not(polar))
    def _():
        for t in range(field.shape[1]):
            pltpu.make_async_copy(
                state_ref.at[pl.ds(first, count), :, pl.ds(t * LANES, LANES)],
                field.at[pl.ds(base, count), t, pl.ds(PAD + REACH, lon), :], sems.at[t]).start()


def finish_own_rows(geo, polar, state_ref, edge_w_ref, edge_e_ref, smooth_refs, staged, field, base, first, count, sems):
    lon, ext = geo
    part = count // len(smooth_refs)

    @pl.when(polar)
    def _():
        for i, ref in enumerate(smooth_refs):
            pltpu.make_async_copy(ref.at[pl.ds(0, part)], staged.at[pl.ds(i * part, part)], sems.at[i]).wait()
            put_rows(field, staged.at[pl.ds(i * part, part)], base + i * part, part, ext)

    @pl.when(jnp.logical_not(polar))
    def _():
        @pl.loop(0, count)
        def _(r):
            for t in range(field.shape[1]):
                lanes = pl.ds(t * LANES, LANES)
                field[base + r, t, pl.ds(PAD, REACH), :] = edge_w_ref[first + r, :, lanes].astype(jnp.float32)
                field[base + r, t, pl.ds(PAD + REACH + lon, REACH), :] = edge_e_ref[first + r, :, lanes].astype(jnp.float32)

        for t in range(field.shape[1]):
            pltpu.make_async_copy(
                state_ref.at[pl.ds(first, count), :, pl.ds(t * LANES, LANES)],
                field.at[pl.ds(base, count), t, pl.ds(PAD + REACH, lon), :], sems.at[t]).wait()


def border_kernel(north, rows, lon, ext, info_ref, state_ref, edge_w_ref, edge_e_ref, winds_ref, beyond_ref, raw_ref, late_ref,
                  smooth_a_ref, smooth_b_ref, border_ref, level_ref, field_a, field_b, halo_rows, staged, winds, own_sem, sems):
    halo, own, first = (2 * HALO, 0, rows - 2 * HALO) if north else (0, HALO, 0)
    polar, zero = info_ref[1] == 1, info_ref[4]
    smooth_refs = smooth_a_ref, smooth_b_ref
    copies = Copies(sems)
    start_own_rows((lon, ext), polar, state_ref, smooth_refs, staged, field_a, own, first, 2 * HALO, own_sem)
    halo_copy = copies.either(info_ref[3 if north else 2] == 1, late_ref.at[pl.ds(0, HALO)], raw_ref.at[pl.ds(0, HALO)], halo_rows)
    wind_copies = [
        copies.start(winds_ref.at[pl.ds(first + 2 if north else 0, HALO + 2)], winds.at[pl.ds(0 if north else 2, HALO + 2)]),
        copies.start(beyond_ref, winds.at[pl.ds(HALO + 2 if north else 0, 2)]),
    ]
    finish_own_rows((lon, ext), polar, state_ref, edge_w_ref, edge_e_ref, smooth_refs, staged, field_a, own, first, 2 * HALO,
                    own_sem)
    halo_copy.wait()
    put_rows(field_a, halo_rows, halo, HALO, ext)
    for copy in wind_copies:
        copy.wait()
    step_rows(field_a, winds, zero, 0, 2 * HALO, 0, 0, ext, store_in(field_b))

    def store(r, t, c, count, value):
        level_ref[r, t, pl.ds(c, count), :] = value
        border_ref[r, pl.ds(c, count), pl.ds(t * LANES, LANES)] = value.astype(jnp.bfloat16)

    step_rows(field_b, winds, zero, 0, HALO, 2, 0, ext, store)


def border_rows(north, info, state, edges, winds, beyond, raw, late, smooths):
    rows, lon, channels = state.shape
    ext = winds.shape[1]
    tiles = channels // LANES
    vmem, hbm = pl.BlockSpec(memory_space=pltpu.VMEM), pl.BlockSpec(memory_space=pl.ANY)
    operands = [info, state, *edges, winds, beyond, raw, late, *smooths]
    return pl.pallas_call(
        functools.partial(border_kernel, north, rows, lon, ext),
        in_specs=[pl.BlockSpec(memory_space=pltpu.SMEM), hbm, vmem, vmem] + [hbm] * (len(operands) - 4),
        out_specs=[vmem, vmem],
        out_shape=[jax.ShapeDtypeStruct((HALO, ext, channels), jnp.bfloat16),
                   jax.ShapeDtypeStruct((HALO, tiles, ext, LANES), jnp.float32)],
        scratch_shapes=[
            cells_of(3 * HALO, tiles, ext), cells_of(2 * HALO, tiles, ext),
            half_of(HALO, ext, channels), half_of(2 * HALO, ext, channels), half_of(2 * HALO, ext, channels),
            pltpu.SemaphoreType.DMA((2,)), pltpu.SemaphoreType.DMA((3,)),
        ],
        compiler_params=pltpu.CompilerParams(vmem_limit_bytes=VMEM_LIMIT),
        cost_estimate=pl.CostEstimate(flops=1000, bytes_accessed=1000, transcendentals=0),
        name="border_north" if north else "border_south",
    )(*operands)


def interior_kernel(rows, lon, ext, info_ref, state_ref, edge_w_ref, edge_e_ref, winds_ref, level_s_ref, level_n_ref, *rest):
    smooth_refs, rest = rest[:PIECES], rest[PIECES:]
    out_ref, third_s_ref, third_n_ref, field_a, field_b, field_c, part_ref, staged, winds, sem, in_sem, out_sem = rest
    inner = rows - 4
    polar, zero = info_ref[1] == 1, info_ref[4]
    copies = Copies(in_sem)
    start_own_rows((lon, ext), polar, state_ref, smooth_refs, staged, field_a, 0, 0, rows, sem)
    wind_copy = copies.start(winds_ref.at[pl.ds(2, inner)], winds)

    def strip(field, base):
        return field.at[pl.ds(base, HALO), :, pl.ds(PAD, ext), :]

    incoming = [copies.start(ref, strip(field_c, base)) for ref, base in ((level_s_ref, 0), (level_n_ref, rows - HALO))]
    finish_own_rows((lon, ext), polar, state_ref, edge_w_ref, edge_e_ref, smooth_refs, staged, field_a, 0, 0, rows, sem)
    wind_copy.wait()
    step_rows(field_a, winds, zero, 0, inner, 0, 0, ext, store_in(field_b))

    def store(r, t, c, count, value):
        field_c[HALO + r, t, pl.ds(PAD + c, count), :] = value

    step_rows(field_b, winds, zero, 0, inner - 4, 2, 0, ext, store)
    for copy in incoming:
        copy.wait()
    step_rows(field_c, winds, zero, 0, inner, 0, 0, ext, store_in(field_b))
    outgoing = [pltpu.make_async_copy(strip(field_b, base), ref, out_sem.at[i])
                for i, (ref, base) in enumerate(((third_s_ref, 0), (third_n_ref, inner - HALO)))]
    for copy in outgoing:
        copy.start()
    step_rows(field_b, winds, zero, 0, inner - 4, 2, REACH, REACH + lon, store_out(part_ref))
    outgoing.append(pltpu.make_async_copy(part_ref, out_ref.at[pl.ds(HALO, rows - 2 * HALO)], out_sem.at[2]))
    outgoing[2].start()
    for copy in outgoing:
        copy.wait()


def interior(info, state, edges, winds, levels, smooths):
    rows, lon, channels = state.shape
    ext = winds.shape[1]
    tiles = channels // LANES
    vmem, hbm = pl.BlockSpec(memory_space=pltpu.VMEM), pl.BlockSpec(memory_space=pl.ANY)
    third = jax.ShapeDtypeStruct((HALO, tiles, ext, LANES), jnp.float32)
    return pl.pallas_call(
        functools.partial(interior_kernel, rows, lon, ext),
        in_specs=[pl.BlockSpec(memory_space=pltpu.SMEM), hbm, vmem, vmem] + [hbm] * (3 + len(smooths)),
        out_specs=[hbm, hbm, hbm],
        out_shape=[jax.ShapeDtypeStruct((rows, lon, channels), jnp.bfloat16), third, third],
        scratch_shapes=[
            cells_of(rows, tiles, ext), cells_of(rows - 4, tiles, ext), cells_of(rows, tiles, ext),
            half_of(rows - 2 * HALO, lon, channels), half_of(rows, ext, channels), half_of(rows - 4, ext, channels),
            pltpu.SemaphoreType.DMA((len(smooths),)), pltpu.SemaphoreType.DMA((3,)), pltpu.SemaphoreType.DMA((3,)),
        ],
        compiler_params=pltpu.CompilerParams(vmem_limit_bytes=VMEM_LIMIT),
        cost_estimate=pl.CostEstimate(flops=1000, bytes_accessed=1000, transcendentals=0),
        name="interior",
    )(info, state, *edges, winds, *levels, *smooths)


def finish_kernel(rows, lon, ext, _, info_ref, winds_ref, *rest):
    sides, (out_ref, field_a, field_b, winds, halo_rows, part_ref, in_sem, out_sem) = rest[:8], rest[8:]
    zero = info_ref[4]
    incoming, outgoing = [], []
    copies = Copies(in_sem)
    for side in range(2):
        beyond_ref, border_ref, level_ref, third_ref = sides[4 * side:4 * side + 4]
        mine, other = (0, HALO) if side else (HALO, 0)
        wind = winds.at[side]
        incoming.append([
            copies.start(border_ref, halo_rows.at[side]),
            copies.start(level_ref, field_a.at[side, pl.ds(mine, HALO), :, pl.ds(PAD, ext), :]),
            copies.start(third_ref, field_b.at[side, pl.ds(mine, HALO), :, pl.ds(PAD, ext), :]),
            copies.start(winds_ref.at[pl.ds(rows - HALO if side else 0, HALO)], wind.at[pl.ds(0 if side else 2, HALO)]),
            copies.start(beyond_ref, wind.at[pl.ds(HALO if side else 0, 2)]),
        ])
    for side in range(2):
        near, last, wind = field_a.at[side], field_b.at[side], winds.at[side]
        mine, other = (0, HALO) if side else (HALO, 0)
        incoming[side][0].wait()
        put_rows(near, halo_rows.at[side], other, HALO, ext)
        for copy in incoming[side][1:]:
            copy.wait()

        def store(r, t, c, count, value, last=last, base=other):
            last[r + base, t, pl.ds(PAD + c, count), :] = value

        step_rows(near, wind, zero, 0, HALO, 2 if side else 0, 0, ext, store)
        step_rows(last, wind, zero, 0, HALO, 0 if side else 2, REACH, REACH + lon, store_out(part_ref.at[side]))
        place = out_ref.at[pl.ds(rows - HALO if side else 0, HALO)]
        outgoing.append(pltpu.make_async_copy(part_ref.at[side], place, out_sem.at[side]))
        outgoing[-1].start()
    for copy in outgoing:
        copy.wait()


def finish(info, out, winds, south, north):
    rows, lon, channels = out.shape
    ext = winds.shape[1]
    tiles = channels // LANES
    hbm = pl.BlockSpec(memory_space=pl.ANY)
    side = pltpu.VMEM((2, 2 * HALO, tiles, ext + 2 * PAD, LANES), jnp.float32)
    return pl.pallas_call(
        functools.partial(finish_kernel, rows, lon, ext),
        in_specs=[hbm, pl.BlockSpec(memory_space=pltpu.SMEM)] + [hbm] * 9,
        out_specs=hbm,
        out_shape=jax.ShapeDtypeStruct(out.shape, out.dtype),
        input_output_aliases={0: 0},
        scratch_shapes=[
            side, side,
            pltpu.VMEM((2, HALO + 2, ext, channels), jnp.bfloat16),
            pltpu.VMEM((2, HALO, ext, channels), jnp.bfloat16),
            pltpu.VMEM((2, HALO, lon, channels), jnp.bfloat16),
            pltpu.SemaphoreType.DMA((10,)),
            pltpu.SemaphoreType.DMA((2,)),
        ],
        compiler_params=pltpu.CompilerParams(vmem_limit_bytes=VMEM_LIMIT),
        cost_estimate=pl.CostEstimate(flops=1000, bytes_accessed=1000, transcendentals=0),
        name="finish",
    )(out, info, winds, *south, *north)


def half_of(rows, ext, channels):
    return pltpu.VMEM((rows, ext, channels), jnp.bfloat16)


def cells_of(rows, tiles, ext):
    return pltpu.VMEM((rows, tiles, ext + 2 * PAD, LANES), jnp.float32)


def per_device(state, winds, decay, widths):
    rows, lon, channels = state.shape
    fields = decay.shape[0]
    bands, tiles = lax.axis_size("lat"), lax.axis_size("lon")
    lat, lon_at = lax.axis_index("lat"), lax.axis_index("lon")
    quarter = bands // 4
    ext = round_up(lon + 2 * REACH, 16)
    fill = ext - lon - 2 * REACH
    axes = ("lat", "lon")

    def is_polar(band):
        return band < quarter or band >= bands - quarter

    def polar_at(band):
        return ((band >= 0) & (band < quarter)) | ((band >= bands - quarter) & (band < bands))

    info = jnp.stack([lon_at % 2, polar_at(lat), polar_at(lat - 1), polar_at(lat + 1), lat < 0]).astype(jnp.int32)

    def over_lon(flip):
        return [(b * tiles + l, b * tiles + (l ^ flip)) for b in range(bands) if is_polar(b) for l in range(tiles)]

    def over_lat(shift, wanted=lambda band: True):
        return [(b * tiles + l, (b + shift) * tiles + l)
                for b in range(bands) if 0 <= b + shift < bands and wanted(b) for l in range(tiles)]

    def move(cells, pairs):
        return lax.ppermute(cells, axes, pairs)

    count = rows // PIECES
    circle_rows = [0, rows - count, count, rows - 2 * count]

    def joined(cols):
        return jnp.concatenate([state[:, cols].astype(jnp.bfloat16), winds[:, cols]], axis=2)

    east = [(l, (l + 1) % tiles) for l in range(tiles)]
    west = [((l + 1) % tiles, l) for l in range(tiles)]
    head, rear, cells = tie(joined(slice(0, REACH)), joined(slice(lon - REACH, lon)), state)
    from_east = lax.ppermute(head, "lon", west)
    from_west = lax.ppermute(rear, "lon", east)

    def piece(first):
        return lax.slice_in_dim(cells, first, first + count).astype(jnp.bfloat16)

    opp, late, smooths = [None] * PIECES, [None] * 2, {}
    circles = [piece(circle_rows[0])]
    circles[0], cells = tie(circles[0], cells)
    opp[0] = move(circles[0], over_lon(2))
    circles += [piece(f) for f in circle_rows[1:]]
    edge_w, edge_e = from_west[:, :, :channels], from_east[:, :, :channels]

    def extend(inner, before, after):
        parts = [before, inner, after, jnp.zeros((inner.shape[0], fill, inner.shape[2]), inner.dtype)]
        return jnp.concatenate(parts, axis=1)

    winds_ext = extend(winds, from_west[:, :, channels:], from_east[:, :, channels:])

    def border(first, wind_first):
        of = slice(first, first + HALO)
        wind = [winds_ext[wind_first + i:wind_first + i + 1] for i in range(2)]
        ends = extend(cells[of].astype(jnp.bfloat16), edge_w[of], edge_e[of])
        return jnp.concatenate([ends, jnp.concatenate(wind, axis=2)], axis=0)

    def is_plain(band):
        return not is_polar(band)

    north_rows, south_rows = border(rows - HALO, rows - 2), border(0, 0)
    raw_s = move(north_rows, over_lat(1, is_plain))
    raw_n = move(south_rows, over_lat(-1, is_plain))
    behind = (south_rows[HALO:], north_rows[HALO:], None, None)

    def spread(wind):
        half = wind.shape[-1] // 2
        return jnp.concatenate([wind[..., :half]] * 2 + [wind[..., half:]] * 2, axis=-1)

    winds_all = spread(winds_ext)

    def beyond(is_late, late_rows, raw_rows):
        both = jnp.where(is_late, late_rows[HALO], raw_rows[HALO])
        return spread(jnp.stack([both[:, :LANES], both[:, LANES:]]))

    sib = move(cells.astype(jnp.bfloat16), over_lon(1))
    circles[1], winds_ext = tie(circles[1], winds_ext)
    opp[1] = move(circles[1], over_lon(2))

    own_widths = lax.dynamic_slice_in_dim(widths, lat * rows, rows)
    rate = jnp.repeat(decay, channels // fields)[None, :]
    reach = own_widths.astype(jnp.float32)[:, None]
    q = jnp.exp(-rate)
    back = round_up(HMAX + 1 + REACH, 8)
    seg = max(back + ext - REACH, round_up(ext + HMAX + 1, 8)) // 8
    carry = jnp.exp(-rate * seg)
    far = jnp.exp(-rate * (reach + 1.0))[:, None, :]
    total = (-jnp.expm1(-rate * (reach + 1.0)) - q * jnp.expm1(-rate * reach)) / -jnp.expm1(-rate)
    scale = (1.0 / total)[:, None, :]

    edges = edge_w, edge_e
    for i, f in enumerate(circle_rows):
        if i == 1:
            opp[i], raw_n, winds_all = tie(opp[i], raw_n, winds_all)
        if i == 2:
            opp[i], late[0], raw_s = tie(opp[i], late[0], raw_s)
        if i == 3:
            opp[i], late[1] = tie(opp[i], late[1])
        if i + 2 < PIECES:
            opp[i], circles[i + 2] = tie(opp[i], circles[i + 2])
            opp[i + 2] = move(circles[i + 2], over_lon(2))
        diag = move(opp[i], over_lon(1))
        smooth = smooth_chunk(f, count, ext, info, own_widths, circles[i], sib, opp[i], diag,
                              q, carry, far, scale, behind[i])
        smooths[f] = smooth
        if i + 1 < PIECES:
            smooth, opp[i + 1] = tie(smooth, opp[i + 1])
        if i < 2:
            late[i] = move(smooths[f], over_lat((-1, 1)[i], is_polar))
        if i == 2:
            wind_s = beyond(polar_at(lat - 1), late[1], raw_s)
            low_rows, level_s = border_rows(False, info, state, edges, winds_all, wind_s, raw_s, late[1],
                                            (smooths[0], smooths[f]))
            to_south = move(low_rows, over_lat(-1))

    smooths = [smooths[f] for f in sorted(smooths)]
    wind_n = beyond(polar_at(lat + 1), late[0], raw_n)
    top_rows, level_n = border_rows(True, info, state, edges, winds_all, wind_n, raw_n, late[0], smooths[2:])
    to_north = move(top_rows, over_lat(1))
    level_s, to_south, level_n = tie(level_s, to_south, level_n)
    out, third_s, third_n = interior(info, state, edges, winds_all, (level_s, level_n), smooths)
    return finish(info, out, winds_all, (wind_s, to_north, level_s, third_s), (wind_n, to_south, level_n, third_n))


def solution(mesh):
    in_specs = (P("lat", "lon", None), P("lat", "lon", None), P(), P())
    out_specs = P("lat", "lon", None)
    return jax.shard_map(
        per_device, mesh=mesh, in_specs=in_specs, out_specs=out_specs, check_vma=False
    )
```

profile of v0, /device:TPU:23, one launch (start us, length us, event | category | flops | bytes accessed | tf_op | source)
XLA Modules:
  0.0 167.6 jit_solution(1390614801561608167)
XLA Ops:
  0.8 3.1 %convert.15 = bf16[16,360,256]{2,1,0:T(8,128)(2,1)S(1)} convert(f32[16,360,256]{2,1,0:T(8,128)} %state_ref.5) | non-fusion elementwise | flops 1474560 | bytes 8847360 | tf_op jit(solution)/shard_map/convert.10
  6.1 1.6 collective-permute-start.3
  7.8 1.9 %convert_element_type.4 = bf16[16,360,256]{2,1,0:T(8,128)(2,1)} convert(f32[16,360,256]{2,1,0:T(8,128)S(1)} %copy-done) | non-fusion elementwise | flops 1474560 | bytes 8847360 | tf_op jit(solution)/shard_map/convert_element_type | solution.py:520
  11.4 3.2 %fusion.13 = (bf16[4,360,256]{2,1,0:T(8,128)(2,1)}, bf16[4,360,256]{2,1,0:T(8,128)(2,1)S(1)}, bf16[4,360,256]{2,1,0:T(8,128)(2,1)S(1)}, bf16[4,360,256]{2,1,0:T(8,128)(2,1)}) fusion(bf16[16,360,256]{2,1,0:T(8,128)(2,1)} %convert_element_type.4), kind=kLoop, calls=%fused_computation.37 | loop fusion | bytes 5898240 | tf_op jit(solution)/shard_map/slice | solution.py:481
  16.3 1.7 %maximum_maximum_fusion.1 = (bf16[5,384,256]{2,1,0:T(8,128)(2,1)}, bf16[5,384,256]{2,1,0:T(8,128)(2,1)}) fusion(bf16[1,384,128]{2,1,0:T(8,128)(2,1)S(1)} %get-tuple-element.74, bf16[1,384,128]{2,1,0:T(8,128)(2,1)S(1)} %get-tuple-element.73, bf16[4,8,256]{2,1,0:T(8,128)(2,1)S(1)} %get-tuple-element.87, bf16[4,360,256]{2,1,0:T(8,128)(2,1)S(1)} %get-tuple-element.41.own_ref, ...), kind=kLoop, calls=%fused_computation.4 | loop fusion | flops 11304960 | bytes 3903232 | tf_op jit(solution)/shard_map/concatenate | solution.py:500
  18.1 3.1 %collective-permute-start.6 = (bf16[5,384,256]{2,1,0:T(8,128)(2,1)}, bf16[5,384,256]{2,1,0:T(8,128)(2,1)}, u32[]{:S(2)}, u32[]{:S(2)}) collective-permute-start(bf16[5,384,256]{2,1,0:T(8,128)(2,1)} %get-tuple-element.90), channel_id=1, source_target_pairs={{8,4},{9,5},{10,6},{11,7},{12,8},{13,9},{14,10},{15,11},{16,12},{1... | collective-permute-start | bytes 2949128 | tf_op jit(solution)/shard_map/ppermute | solution.py:466
  26.1 7.3 %collective-permute-start.11 = (bf16[5,384,256]{2,1,0:T(8,128)(2,1)}, bf16[5,384,256]{2,1,0:T(8,128)(2,1)S(1)}, u32[]{:S(2)}, u32[]{:S(2)}) collective-permute-start(bf16[5,384,256]{2,1,0:T(8,128)(2,1)} %get-tuple-element.89), channel_id=1, source_target_pairs={{8,12},{9,13},{10,14},{11,15},{12,16},{13,17},{14,18},{15,19},{16,... | collective-permute-start | bytes 2949128 | tf_op jit(solution)/shard_map/ppermute | solution.py:466
  35.0 2.6 %fusion.16 = (bf16[16,384,64]{2,1,0:T(8,128)(2,1)S(1)}, bf16[16,384,64]{2,1,0:T(8,128)(2,1)S(1)}) fusion(bf16[16,384,128]{2,1,0:T(8,128)(2,1)} %copy-done.2), kind=kLoop, calls=%fused_computation.40 | loop fusion | bytes 3145728 | tf_op jit(solution)/shard_map/slice | solution.py:512
  37.6 4.5 %pad_maximum_fusion.winds_ref = bf16[16,384,256]{2,1,0:T(8,128)(2,1)} fusion(bf16[16,384,64]{2,1,0:T(8,128)(2,1)S(1)} %get-tuple-element.78, bf16[16,8,128]{2,1,0:T(8,128)(2,1)S(1)} %broadcast_in_dim.16, bf16[16,8,128]{2,1,0:T(8,128)(2,1)S(1)} %slice.162, bf16[16,360,128]{2,1,0:T(8,128)(2,1)S(1)} %copy-done.5, bf16[16,8,128]{2,1,0:T(8,128)(2,1)S(1)} %slice.161, ...), kind=kLoop, calls=%fused_computation | loop fusion | flops 18874368 | bytes 6291456 | tf_op jit(solution)/shard_map/concatenate | solution.py:512
  43.0 1.0 copy-done.1
  44.0 2.9 %smooth.4.smooth_a_ref.rest_0_ = bf16[5,384,256]{2,1,0:T(8,128)(2,1)} custom-call(s32[5]{0:T(128)} %stack.57.info_ref, s32[16]{0:T(128)} %copy-done.22, bf16[4,360,256]{2,1,0:T(8,128)(2,1)} %slice.200.own_ref, bf16[16,360,256]{2,1,0:T(8,128)(2,1)} %copy-done.1, bf16[4,360,256]{2,1,0:T(8,128)(2,1)} %collective-permute-done.3.opp_ref, ...), custom_call_target="tpu_custom_call" | custom-call | flops 1000 | bytes 1000 | tf_op jit(solution)/shard_map/smooth/pallas_call | solution.py:132
  46.8 1.3 collective-permute-start.10
  48.1 13.2 %collective-permute-done.6.raw_ref = bf16[5,384,256]{2,1,0:T(8,128)(2,1)} collective-permute-done((bf16[5,384,256]{2,1,0:T(8,128)(2,1)}, bf16[5,384,256]{2,1,0:T(8,128)(2,1)}, u32[]{:S(2)}, u32[]{:S(2)}) %collective-permute-start.6) | collective-permute-done | bytes 983072 | tf_op jit(solution)/shard_map/ppermute | solution.py:466
  64.4 2.8 %smooth.5.smooth_b_ref.rest_3_ = bf16[5,384,256]{2,1,0:T(8,128)(2,1)} custom-call(s32[5]{0:T(128)} %stack.57.info_ref, s32[16]{0:T(128)} %copy-done.22, bf16[4,360,256]{2,1,0:T(8,128)(2,1)} %copy-done.3, bf16[16,360,256]{2,1,0:T(8,128)(2,1)} %copy-done.1, bf16[4,360,256]{2,1,0:T(8,128)(2,1)} %copy-done.13, bf16[4,360,256]{2,1,0:T(8,128)(2,1)} %copy-done.19, ...), custom_call_target="tpu_custom_call" | custom-call | flops 1000 | bytes 1000 | tf_op jit(solution)/shard_map/smooth/pallas_call | solution.py:132
  67.9 6.5 %collective-permute-done.10.late_ref = bf16[5,384,256]{2,1,0:T(8,128)(2,1)S(1)} collective-permute-done((bf16[5,384,256]{2,1,0:T(8,128)(2,1)}, bf16[5,384,256]{2,1,0:T(8,128)(2,1)S(1)}, u32[]{:S(2)}, u32[]{:S(2)}) %collective-permute-start.10) | collective-permute-done | bytes 983072 | tf_op jit(solution)/shard_map/ppermute | solution.py:466
  79.1 2.8 %smooth.6.smooth_b_ref.rest_1_ = bf16[4,384,256]{2,1,0:T(8,128)(2,1)} custom-call(s32[5]{0:T(128)} %stack.57.info_ref, s32[16]{0:T(128)} %copy-done.22, bf16[4,360,256]{2,1,0:T(8,128)(2,1)} %get-tuple-element.46.own_ref, bf16[16,360,256]{2,1,0:T(8,128)(2,1)} %copy-done.1, bf16[4,360,256]{2,1,0:T(8,128)(2,1)} %copy-done.15, bf16[4,360,256]{2,1,0:T(8,128)(2,1)} %copy-done.17, ...), custom_call_target="tpu_custom_call" | custom-call | flops 1000 | bytes 1000 | tf_op jit(solution)/shard_map/smooth/pallas_call | solution.py:132
  83.6 9.6 %border_south.1 = (bf16[4,384,256]{2,1,0:T(8,128)(2,1)}, f32[4,2,384,128]{3,2,1,0:T(8,128)}) custom-call(s32[5]{0:T(128)} %stack.57.info_ref, f32[16,360,256]{2,1,0:T(8,128)} %state_ref.5, bf16[16,8,256]{2,1,0:T(8,128)(2,1)} %slice.157.edge_w_ref, bf16[16,8,256]{2,1,0:T(8,128)(2,1)} %slice.158.edge_e_ref, bf16[16,384,256]{2,1,0:T(8,128)(2,1)} %pad_maximum_fusion.winds_ref, ...), custom_call_target="tpu_custom_call" | custom-call | flops 1000 | bytes 1000 | tf_op jit(solution)/shard_map/border_south/pallas_call | solution.py:296
  93.3 1.9 %collective-permute-start.13 = (bf16[4,384,256]{2,1,0:T(8,128)(2,1)}, bf16[4,384,256]{2,1,0:T(8,128)(2,1)S(1)}, u32[]{:S(2)}, u32[]{:S(2)}) collective-permute-start(bf16[4,384,256]{2,1,0:T(8,128)(2,1)} %get-tuple-element.51), channel_id=1, source_target_pairs={{4,0},{5,1},{6,2},{7,3},{8,4},{9,5},{10,6},{11,7},{12,8},{13,9},{1... | collective-permute-start | bytes 2359304 | tf_op jit(solution)/shard_map/ppermute | solution.py:466
  95.2 1.0 fusion.7.beyond_ref.rest_4_
  97.1 2.8 %smooth.7.smooth_a_ref.rest_2_ = bf16[4,384,256]{2,1,0:T(8,128)(2,1)} custom-call(s32[5]{0:T(128)} %stack.57.info_ref, s32[16]{0:T(128)} %copy-done.22, bf16[4,360,256]{2,1,0:T(8,128)(2,1)} %get-tuple-element.54.own_ref, bf16[16,360,256]{2,1,0:T(8,128)(2,1)} %copy-done.1, bf16[4,360,256]{2,1,0:T(8,128)(2,1)} %copy-done.14, bf16[4,360,256]{2,1,0:T(8,128)(2,1)} %copy-done.16, ...), custom_call_target="tpu_custom_call" | custom-call | flops 1000 | bytes 1000 | tf_op jit(solution)/shard_map/smooth/pallas_call | solution.py:132
  99.8 9.6 %border_north.1 = (bf16[4,384,256]{2,1,0:T(8,128)(2,1)}, f32[4,2,384,128]{3,2,1,0:T(8,128)}) custom-call(s32[5]{0:T(128)} %stack.57.info_ref, f32[16,360,256]{2,1,0:T(8,128)} %state_ref.5, bf16[16,8,256]{2,1,0:T(8,128)(2,1)} %slice.157.edge_w_ref, bf16[16,8,256]{2,1,0:T(8,128)(2,1)} %slice.158.edge_e_ref, bf16[16,384,256]{2,1,0:T(8,128)(2,1)} %pad_maximum_fusion.winds_ref, ...), custom_call_target="tpu_custom_call" | custom-call | flops 1000 | bytes 1000 | tf_op jit(solution)/shard_map/border_north/pallas_call | solution.py:296
  109.4 25.4 %collective-permute-start.16 = (bf16[4,384,256]{2,1,0:T(8,128)(2,1)}, bf16[4,384,256]{2,1,0:T(8,128)(2,1)S(1)}, u32[]{:S(2)}, u32[]{:S(2)}) collective-permute-start(bf16[4,384,256]{2,1,0:T(8,128)(2,1)} %get-tuple-element.61), channel_id=1, source_target_pairs={{0,4},{1,5},{2,6},{3,7},{4,8},{5,9},{6,10},{7,11},{8,12},{9,13},{1... | collective-permute-start | bytes 2359304 | tf_op jit(solution)/shard_map/ppermute | solution.py:466
  134.9 21.3 %interior.1 = (bf16[16,360,256]{2,1,0:T(8,128)(2,1)}, f32[4,2,384,128]{3,2,1,0:T(8,128)}, f32[4,2,384,128]{3,2,1,0:T(8,128)}) custom-call(s32[5]{0:T(128)} %stack.57.info_ref, f32[16,360,256]{2,1,0:T(8,128)} %state_ref.5, bf16[16,8,256]{2,1,0:T(8,128)(2,1)} %slice.157.edge_w_ref, bf16[16,8,256]{2,1,0:T(8,128)(2,1)} %slice.158.edge_e_ref, ...), custom_call_target="tpu_custom_call" | custom-call | flops 1000 | bytes 1000 | tf_op jit(solution)/shard_map/interior/pallas_call | solution.py:354
  157.1 10.4 %finish.1 = bf16[16,360,256]{2,1,0:T(8,128)(2,1)} custom-call(bf16[16,360,256]{2,1,0:T(8,128)(2,1)} %get-tuple-element.60._, s32[5]{0:T(128)} %stack.57.info_ref, bf16[16,384,256]{2,1,0:T(8,128)(2,1)} %pad_maximum_fusion.winds_ref, bf16[2,384,256]{2,1,0:T(8,128)(2,1)} %fusion.5.beyond_ref.rest_0_, ...), custom_call_target="tpu_custom_call", output_to_operand_aliasing={{}: (0, {})} | custom-call | flops 1000 | bytes 1000 | tf_op jit(solution)/shard_map/finish/pallas_call | solution.py:412
  (112 shorter events, 25.5 us)
Async XLA Ops:
  3.9 10.8 %collective-permute-start = (bf16[16,8,384]{2,1,0:T(8,128)(2,1)S(1)}, bf16[16,8,384]{2,1,0:T(8,128)(2,1)S(1)}, u32[]{:S(2)}, u32[]{:S(2)}) collective-permute-start(bf16[16,8,384]{2,1,0:T(8,128)(2,1)S(1)} %get-tuple-element.35), channel_id=1, source_target_pairs={{0,1},{1,2},{2,3},{3,0},{4,5},{5,6},{6,7},{7,4},{8,9},{9,10},{10,1... | collective-permute-start | bytes 294920 | tf_op jit(solution)/shard_map/ppermute | solution.py:478
  4.8 9.9 %collective-permute-start.1 = (bf16[16,8,384]{2,1,0:T(8,128)(2,1)S(1)}, bf16[16,8,384]{2,1,0:T(8,128)(2,1)S(1)}, u32[]{:S(2)}, u32[]{:S(2)}) collective-permute-start(bf16[16,8,384]{2,1,0:T(8,128)(2,1)S(1)} %get-tuple-element.36), channel_id=1, source_target_pairs={{1,0},{2,1},{3,2},{0,3},{5,4},{6,5},{7,6},{4,7},{9,8},{10,9},{11,1... | collective-permute-start | bytes 294920 | tf_op jit(solution)/shard_map/ppermute | solution.py:477
  6.1 28.0 %collective-permute-start.3 = (bf16[4,360,256]{2,1,0:T(8,128)(2,1)}, bf16[4,360,256]{2,1,0:T(8,128)(2,1)}, u32[]{:S(2)}, u32[]{:S(2)}) collective-permute-start(bf16[4,360,256]{2,1,0:T(8,128)(2,1)} %slice.200.own_ref), channel_id=1, source_target_pairs={{0,2},{1,3},{2,0},{3,1},{4,6},{5,7},{6,4},{7,5},{24,26},{25,27},{2... | collective-permute-start | bytes 2211848 | tf_op jit(solution)/shard_map/ppermute | solution.py:466
  9.6 32.5 %collective-permute-start.2 = (bf16[16,360,256]{2,1,0:T(8,128)(2,1)}, bf16[16,360,256]{2,1,0:T(8,128)(2,1)S(1)}, u32[]{:S(2)}, u32[]{:S(2)}) collective-permute-start(bf16[16,360,256]{2,1,0:T(8,128)(2,1)} %convert_element_type.4), channel_id=1, source_target_pairs={{0,1},{1,0},{2,3},{3,2},{4,5},{5,4},{6,7},{7,6},{24,25},{25,24},{2... | collective-permute-start | bytes 8847368 | tf_op jit(solution)/shard_map/ppermute | solution.py:466
  18.1 43.3 %collective-permute-start.6 = (bf16[5,384,256]{2,1,0:T(8,128)(2,1)}, bf16[5,384,256]{2,1,0:T(8,128)(2,1)}, u32[]{:S(2)}, u32[]{:S(2)}) collective-permute-start(bf16[5,384,256]{2,1,0:T(8,128)(2,1)} %get-tuple-element.90), channel_id=1, source_target_pairs={{8,4},{9,5},{10,6},{11,7},{12,8},{13,9},{14,10},{15,11},{16,12},{1... | collective-permute-start | bytes 2949128 | tf_op jit(solution)/shard_map/ppermute | solution.py:466
  25.4 22.7 %collective-permute-start.5 = (bf16[4,360,256]{2,1,0:T(8,128)(2,1)}, bf16[4,360,256]{2,1,0:T(8,128)(2,1)S(1)}, u32[]{:S(2)}, u32[]{:S(2)}) collective-permute-start(bf16[4,360,256]{2,1,0:T(8,128)(2,1)} %copy-done.3), channel_id=1, source_target_pairs={{0,2},{1,3},{2,0},{3,1},{4,6},{5,7},{6,4},{7,5},{24,26},{25,27},{2... | collective-permute-start | bytes 2211848 | tf_op jit(solution)/shard_map/ppermute | solution.py:466
  26.1 41.8 %collective-permute-start.11 = (bf16[5,384,256]{2,1,0:T(8,128)(2,1)}, bf16[5,384,256]{2,1,0:T(8,128)(2,1)S(1)}, u32[]{:S(2)}, u32[]{:S(2)}) collective-permute-start(bf16[5,384,256]{2,1,0:T(8,128)(2,1)} %get-tuple-element.89), channel_id=1, source_target_pairs={{8,12},{9,13},{10,14},{11,15},{12,16},{13,17},{14,18},{15,19},{16,... | collective-permute-start | bytes 2949128 | tf_op jit(solution)/shard_map/ppermute | solution.py:466
  34.1 8.0 %collective-permute-start.4 = (bf16[4,360,256]{2,1,0:T(8,128)(2,1)}, bf16[4,360,256]{2,1,0:T(8,128)(2,1)S(1)}, u32[]{:S(2)}, u32[]{:S(2)}) collective-permute-start(bf16[4,360,256]{2,1,0:T(8,128)(2,1)} %collective-permute-done.3.opp_ref), channel_id=1, source_target_pairs={{0,1},{1,0},{2,3},{3,2},{4,5},{5,4},{6,7},{7,6},{24,25},{25,24},{2... | collective-permute-start | bytes 2211848 | tf_op jit(solution)/shard_map/ppermute | solution.py:466
  44.0 18.1 %copy-start.7 = (bf16[4,360,256]{2,1,0:T(8,128)(2,1)S(1)}, bf16[4,360,256]{2,1,0:T(8,128)(2,1)}, u32[]{:S(2)}) copy-start(bf16[4,360,256]{2,1,0:T(8,128)(2,1)} %get-tuple-element.46.own_ref) | copy-start | bytes 2211844
  46.8 27.6 %collective-permute-start.10 = (bf16[5,384,256]{2,1,0:T(8,128)(2,1)}, bf16[5,384,256]{2,1,0:T(8,128)(2,1)S(1)}, u32[]{:S(2)}, u32[]{:S(2)}) collective-permute-start(bf16[5,384,256]{2,1,0:T(8,128)(2,1)} %smooth.4.smooth_a_ref.rest_0_), channel_id=1, source_target_pairs={{4,0},{5,1},{6,2},{7,3},{24,20},{25,21},{26,22},{27,23},{28,24},{2... | collective-permute-start | bytes 2949128 | tf_op jit(solution)/shard_map/ppermute | solution.py:466
  48.1 15.4 %copy-start.13 = (bf16[4,360,256]{2,1,0:T(8,128)(2,1)}, bf16[4,360,256]{2,1,0:T(8,128)(2,1)S(1)}, u32[]{:S(2)}) copy-start(bf16[4,360,256]{2,1,0:T(8,128)(2,1)S(1)} %collective-permute-done.5.opp_ref) | copy-start | bytes 2211844
  61.4 2.1 %collective-permute-start.7 = (bf16[4,360,256]{2,1,0:T(8,128)(2,1)S(1)}, bf16[4,360,256]{2,1,0:T(8,128)(2,1)S(1)}, u32[]{:S(2)}, u32[]{:S(2)}) collective-permute-start(bf16[4,360,256]{2,1,0:T(8,128)(2,1)S(1)} %collective-permute-done.5.opp_ref), channel_id=1, source_target_pairs={{0,1},{1,0},{2,3},{3,2},{4,5},{5,4},{6,7},{7,6},{24,25},{25,24},{2... | collective-permute-start | bytes 2211848 | tf_op jit(solution)/shard_map/ppermute | solution.py:466
  62.1 5.8 %collective-permute-start.9 = (bf16[4,360,256]{2,1,0:T(8,128)(2,1)S(1)}, bf16[4,360,256]{2,1,0:T(8,128)(2,1)S(1)}, u32[]{:S(2)}, u32[]{:S(2)}) collective-permute-start(bf16[4,360,256]{2,1,0:T(8,128)(2,1)S(1)} %copy-done.7), channel_id=1, source_target_pairs={{0,2},{1,3},{2,0},{3,1},{4,6},{5,7},{6,4},{7,5},{24,26},{25,27},{2... | collective-permute-start | bytes 2211848 | tf_op jit(solution)/shard_map/ppermute | solution.py:466
  63.5 11.6 %copy-start.6 = (bf16[4,360,256]{2,1,0:T(8,128)(2,1)S(1)}, bf16[4,360,256]{2,1,0:T(8,128)(2,1)}, u32[]{:S(2)}) copy-start(bf16[4,360,256]{2,1,0:T(8,128)(2,1)} %get-tuple-element.54.own_ref) | copy-start | bytes 2211844
  63.5 13.0 %copy-start.21 = (bf16[16,8,384]{2,1,0:T(8,128)(2,1)S(1)}, bf16[16,8,384]{2,1,0:T(8,128)(2,1)}, u32[]{:S(2)}) copy-start(bf16[16,8,384]{2,1,0:T(8,128)(2,1)} %copy-done.20) | copy-start | bytes 294916
  67.2 14.7 %collective-permute-start.8 = (bf16[5,384,256]{2,1,0:T(8,128)(2,1)}, bf16[5,384,256]{2,1,0:T(8,128)(2,1)S(1)}, u32[]{:S(2)}, u32[]{:S(2)}) collective-permute-start(bf16[5,384,256]{2,1,0:T(8,128)(2,1)} %smooth.5.smooth_b_ref.rest_3_), channel_id=1, source_target_pairs={{0,4},{1,5},{2,6},{3,7},{4,8},{5,9},{6,10},{7,11},{24,28},{25,29},... | collective-permute-start | bytes 2949128 | tf_op jit(solution)/shard_map/ppermute | solution.py:466
  67.9 14.7 %copy-start.8 = (bf16[5,384,256]{2,1,0:T(8,128)(2,1)}, bf16[5,384,256]{2,1,0:T(8,128)(2,1)S(1)}, u32[]{:S(2)}) copy-start(bf16[5,384,256]{2,1,0:T(8,128)(2,1)S(1)} %collective-permute-done.11.raw_ref) | copy-start | bytes 2949124
  74.4 3.7 %collective-permute-start.12 = (bf16[4,360,256]{2,1,0:T(8,128)(2,1)S(1)}, bf16[4,360,256]{2,1,0:T(8,128)(2,1)S(1)}, u32[]{:S(2)}, u32[]{:S(2)}) collective-permute-start(bf16[4,360,256]{2,1,0:T(8,128)(2,1)S(1)} %collective-permute-done.9.opp_ref), channel_id=1, source_target_pairs={{0,1},{1,0},{2,3},{3,2},{4,5},{5,4},{6,7},{7,6},{24,25},{25,24},{2... | collective-permute-start | bytes 2211848 | tf_op jit(solution)/shard_map/ppermute | solution.py:466
  75.1 6.7 %collective-permute-start.14 = (bf16[4,360,256]{2,1,0:T(8,128)(2,1)S(1)}, bf16[4,360,256]{2,1,0:T(8,128)(2,1)S(1)}, u32[]{:S(2)}, u32[]{:S(2)}) collective-permute-start(bf16[4,360,256]{2,1,0:T(8,128)(2,1)S(1)} %copy-done.6), channel_id=1, source_target_pairs={{0,2},{1,3},{2,0},{3,1},{4,6},{5,7},{6,4},{7,5},{24,26},{25,27},{2... | collective-permute-start | bytes 2211848 | tf_op jit(solution)/shard_map/ppermute | solution.py:466
  81.9 11.4 %copy-start.14 = (bf16[4,360,256]{2,1,0:T(8,128)(2,1)}, bf16[4,360,256]{2,1,0:T(8,128)(2,1)S(1)}, u32[]{:S(2)}) copy-start(bf16[4,360,256]{2,1,0:T(8,128)(2,1)S(1)} %collective-permute-done.14.opp_ref) | copy-start | bytes 2211844
  81.9 14.3 %collective-permute-start.15 = (bf16[4,360,256]{2,1,0:T(8,128)(2,1)S(1)}, bf16[4,360,256]{2,1,0:T(8,128)(2,1)S(1)}, u32[]{:S(2)}, u32[]{:S(2)}) collective-permute-start(bf16[4,360,256]{2,1,0:T(8,128)(2,1)S(1)} %collective-permute-done.14.opp_ref), channel_id=1, source_target_pairs={{0,1},{1,0},{2,3},{3,2},{4,5},{5,4},{6,7},{7,6},{24,25},{25,24},{2... | collective-permute-start | bytes 2211848 | tf_op jit(solution)/shard_map/ppermute | solution.py:466
  93.3 41.6 %collective-permute-start.13 = (bf16[4,384,256]{2,1,0:T(8,128)(2,1)}, bf16[4,384,256]{2,1,0:T(8,128)(2,1)S(1)}, u32[]{:S(2)}, u32[]{:S(2)}) collective-permute-start(bf16[4,384,256]{2,1,0:T(8,128)(2,1)} %get-tuple-element.51), channel_id=1, source_target_pairs={{4,0},{5,1},{6,2},{7,3},{8,4},{9,5},{10,6},{11,7},{12,8},{13,9},{1... | collective-permute-start | bytes 2359304 | tf_op jit(solution)/shard_map/ppermute | solution.py:466
  109.4 46.8 %collective-permute-start.16 = (bf16[4,384,256]{2,1,0:T(8,128)(2,1)}, bf16[4,384,256]{2,1,0:T(8,128)(2,1)S(1)}, u32[]{:S(2)}, u32[]{:S(2)}) collective-permute-start(bf16[4,384,256]{2,1,0:T(8,128)(2,1)} %get-tuple-element.61), channel_id=1, source_target_pairs={{0,4},{1,5},{2,6},{3,7},{4,8},{5,9},{6,10},{7,11},{8,12},{9,13},{1... | collective-permute-start | bytes 2359304 | tf_op jit(solution)/shard_map/ppermute | solution.py:466
  134.9 21.3 %copy-start.11 = (bf16[4,384,256]{2,1,0:T(8,128)(2,1)}, bf16[4,384,256]{2,1,0:T(8,128)(2,1)S(1)}, u32[]{:S(2)}) copy-start(bf16[4,384,256]{2,1,0:T(8,128)(2,1)S(1)} %collective-permute-done.13.rest_5_) | copy-start | bytes 2359300
  (18 other events, 55.6 us)
where the time goes:
time: 169 us; the launch traced here: 168 us
  Pallas kernels  62.1 us (37%)
  starting transfers between devices  48.1 us (28%)
  local copies, waits for them, and re-layouts  19.8 us (12%)
  waiting for transfers between devices  19.8 us (12%)
  other arithmetic  17.2 us (10%)
    ppermute x15, starting transfers between devices, move(): return lax.ppermute(cells, axes, pairs)  47.3 us
    pallas_call x1, Pallas kernels, interior(): pl.pallas_call(functools.partial(interior_kernel, rows, lon, ext), in_spe...  21.3 us
    ppermute x15, waiting for transfers between devices, move(): return lax.ppermute(cells, axes, pairs)  19.8 us
    pallas_call x2, Pallas kernels, border_rows(): pl.pallas_call(functools.partial(border_kernel, north, rows, lon, ext), i...  19.2 us
    pallas_call x4, Pallas kernels, smooth_chunk(): pl.pallas_call(functools.partial(smooth_kernel, geo, first), grid=(1,), i...  11.2 us
    pallas_call x1, Pallas kernels, finish(): pl.pallas_call(functools.partial(finish_kernel, rows, lon, ext), in_specs...  10.4 us
    concatenate x3, other arithmetic, spread(): jnp.concatenate([wind[..., :half]] * 2 + [wind[..., half:]] * 2, axis=-1)  6.41 us
    unnamed x50, local copies, waits for them, and re-layouts  5.64 us
  transfers between devices with their start and end apart: 17, of which 2 were waited for; matrix products, arithmetic and copies ran while one was open for 16% of the time, Pallas kernels for 31%

commit v1 on v0

v1 whole, which is shorter than its diff:
```python
import functools

import jax
import jax.numpy as jnp
from jax import lax
from jax.experimental import pallas as pl
from jax.experimental.pallas import tpu as pltpu
from jax.sharding import PartitionSpec as P

ADV_STEPS = 4
REACH = 2 * ADV_STEPS
ROUND = 2
HALO = 2 * ROUND
HMAX = 480
LANES = 128
VMEM_LIMIT = 56 * 1024 * 1024
PAD = 8
COLS = 48


def tie(*values):
    return lax.optimization_barrier(values)


def round_up(value, unit):
    return -(-value // unit) * unit


def smooth_kernel(geo, sends, info_ref, widths_ref, *refs):
    ins, extra_refs, outs, scratch = refs[:8], refs[8:8 + sends], refs[8 + sends:9 + 2 * sends], refs[9 + 2 * sends:]

    @pl.when(info_ref[1] == 1)
    def _():
        smooth_rows(geo, info_ref[0] == 1, widths_ref, *ins, *outs[:1], outs[1:], *scratch)
        for ref, extra_ref in zip(outs[1:], extra_refs):
            ref[HALO] = extra_ref[0]


def smooth_rows(geo, odd, widths_ref, own_ref, sib_ref, opp_ref, diag_ref, q_ref, carry_ref, far_ref, scale_ref,
                level_ref, border_refs, cells, east_sum, west_sum):
    lon, back, span, seg, ext = geo
    rows, tiles = own_ref.shape[0], own_ref.shape[2] // LANES
    chains = [(r, t) for r in range(rows) for t in range(tiles)]

    def put(ref, start, begin, count):
        @pl.loop(0, rows)
        def _(r):
            for t in range(tiles):
                part = ref[r, pl.ds(begin, count), pl.ds(t * LANES, LANES)]
                cells[r * tiles + t, pl.ds(start, count), :] = part.astype(jnp.float32)

    head = back - lon
    put(opp_ref, 0, lon - head, head)
    put(own_ref, back, 0, lon)
    put(opp_ref, back + 2 * lon, 0, span - REACH - 2 * lon)

    @pl.when(odd)
    def _():
        put(sib_ref, back - lon, 0, lon)
        put(diag_ref, back + lon, 0, lon)

    @pl.when(jnp.logical_not(odd))
    def _():
        put(diag_ref, back - lon, 0, lon)
        put(sib_ref, back + lon, 0, lon)

    q = [jnp.broadcast_to(q_ref[0:1, t * LANES:(t + 1) * LANES], (8, LANES)) for t in range(tiles)]
    jump = [carry_ref[0:1, t * LANES:(t + 1) * LANES] for t in range(tiles)]
    zero = jnp.zeros((8, LANES), jnp.float32)
    none = jnp.zeros((1, LANES), jnp.float32)
    east_base = back - REACH

    for base, total, forward in ((east_base, east_sum, False), (0, west_sum, True)):
        def at(i, forward=forward):
            return i if forward else seg - 1 - i

        def totals(i, acc, base=base):
            return tuple(cells[r * tiles + t, pl.ds(base + at(i), 8, stride=seg), :] + q[t] * acc[n]
                         for n, (r, t) in enumerate(chains))

        acc = lax.fori_loop(0, seg, totals, (zero,) * len(chains), unroll=4)
        start = []
        for n, (r, t) in enumerate(chains):
            carry = none
            parts = [None] * 8
            for k in (range(8) if forward else range(7, -1, -1)):
                parts[k] = carry
                carry = acc[n][k:k + 1] + jump[t] * carry
            start.append(jnp.concatenate(parts, axis=0))

        def sums(i, acc, base=base, total=total):
            new = []
            for n, (r, t) in enumerate(chains):
                v = cells[r * tiles + t, pl.ds(base + at(i), 8, stride=seg), :] + q[t] * acc[n]
                total[r * tiles + t, pl.ds(at(i), 8, stride=seg), :] = v
                new.append(v)
            return tuple(new)

        lax.fori_loop(0, seg, sums, tuple(start), unroll=4)

    step = COLS

    def one_row(r, border_ref, border_row):
        width = widths_ref[r]
        for t in range(tiles):
            n = r * tiles + t
            far = jnp.broadcast_to(far_ref[r, 0:1, t * LANES:(t + 1) * LANES], (step, LANES))
            scale = jnp.broadcast_to(scale_ref[r, 0:1, t * LANES:(t + 1) * LANES], (step, LANES))
            for c in range(0, ext, step):
                near = east_sum[n, pl.ds(c, step), :] + west_sum[n, pl.ds(back - REACH + c, step), :]
                cut = east_sum[n, pl.ds(c + 1 + width, step), :] + west_sum[n, pl.ds(back - REACH + c - 1 - width, step), :]
                mid = cells[n, pl.ds(back - REACH + c, step), :]
                value = ((near - mid - far * cut) * scale).astype(jnp.bfloat16)
                level_ref[r, t, pl.ds(c, step), :] = value.astype(jnp.float32)
                if border_ref is not None:
                    border_ref[border_row, pl.ds(c, step), pl.ds(t * LANES, LANES)] = value

    if border_refs:
        for i, ref in enumerate(border_refs):
            @pl.loop(0, HALO)
            def _(r, i=i, ref=ref):
                one_row(i * HALO + r, ref, r)
    else:
        @pl.loop(0, rows)
        def _(r):
            one_row(r, None, None)


def smooth_piece(first, rows, ext, info, widths, own, sib, opp, diag, q, carry, far, scale, extras):
    lon, channels = own.shape[1:]
    tiles = channels // LANES
    back = round_up(HMAX + 1 + REACH, 8)
    span = round_up(ext + HMAX + 1, 8)
    seg = max(back + ext - REACH, span) // 8
    geo = (lon, back, 8 * seg, seg, ext)
    smem, vmem = pl.BlockSpec(memory_space=pltpu.SMEM), pl.BlockSpec(memory_space=pltpu.VMEM)
    part = pl.BlockSpec((rows, lon, channels), lambda i: (first // rows, 0, 0))
    table = pl.BlockSpec((rows, 1, channels), lambda i: (first // rows, 0, 0))
    border = jax.ShapeDtypeStruct((HALO + 1, ext, channels), jnp.bfloat16)
    of_rows = slice(first, first + rows)
    return pl.pallas_call(
        functools.partial(smooth_kernel, geo, len(extras)),
        grid=(1,),
        in_specs=[smem, smem, vmem, part, vmem, vmem, vmem, vmem, table, table] + [vmem] * len(extras),
        out_specs=[vmem] * (1 + len(extras)),
        out_shape=[jax.ShapeDtypeStruct((rows, tiles, ext, LANES), jnp.float32)] + [border] * len(extras),
        scratch_shapes=[
            pltpu.VMEM((rows * tiles, back - REACH + 8 * seg, LANES), jnp.float32),
            pltpu.VMEM((rows * tiles, 8 * seg, LANES), jnp.float32),
            pltpu.VMEM((rows * tiles, 8 * seg, LANES), jnp.float32),
        ],
        compiler_params=pltpu.CompilerParams(vmem_limit_bytes=VMEM_LIMIT),
        cost_estimate=pl.CostEstimate(flops=1000, bytes_accessed=1000, transcendentals=0),
        name="smooth",
    )(info, widths[of_rows], own, sib, opp, diag, q, carry, far, scale, *extras)


def update(src, r, t, c, count, u, v, zero):
    def at(dr, dc):
        return src[r + dr, t, pl.ds(PAD + c + dc + (zero if dc else 0), count), :]

    mid = at(0, 0)
    mid30 = 30.0 * mid
    e1, w1, e2, w2 = at(0, 1), at(0, -1), at(0, 2), at(0, -2)
    n1, s1, n2, s2 = at(1, 0), at(-1, 0), at(2, 0), at(-2, 0)
    first_x = (e2 - w2) - 8.0 * (e1 - w1)
    second_x = 16.0 * (e1 + w1) - (e2 + w2) - mid30
    first_y = (n2 - s2) - 8.0 * (n1 - s1)
    second_y = 16.0 * (n1 + s1) - (n2 + s2) - mid30
    change = u * (first_x + (6.0 * u) * second_x) + v * (first_y + (6.0 * v) * second_y)
    return mid + change


def put_rows(field, ref, base, count, ext):
    @pl.loop(0, count)
    def _(r):
        for t in range(field.shape[1]):
            field[base + r, t, pl.ds(PAD, ext), :] = ref[r, :, pl.ds(t * LANES, LANES)].astype(jnp.float32)


def step_rows(source, winds, zero, first, last, offset, start, stop, store):
    @pl.loop(first, last)
    def _(r):
        for c in range(start, stop, COLS):
            count = min(COLS, stop - c)
            u = winds[r + offset, pl.ds(c, count), pl.ds(0, LANES)].astype(jnp.float32) * (1.0 / 12.0)
            v = winds[r + offset, pl.ds(c, count), pl.ds(LANES, LANES)].astype(jnp.float32) * (1.0 / 12.0)
            for t in range(source.shape[1]):
                store(r, t, c, count, update(source, r + 2, t, c, count, u, v, zero))


class Copies:
    def __init__(self, sems):
        self.sems, self.used = sems, 0

    def start(self, source, target):
        copy = pltpu.make_async_copy(source, target, self.sems.at[self.used])
        self.used += 1
        copy.start()
        return copy

    def either(self, flag, source, other, target):
        sem = self.sems.at[self.used]
        self.used += 1

        @pl.when(flag)
        def _():
            pltpu.make_async_copy(source, target, sem).start()

        @pl.when(jnp.logical_not(flag))
        def _():
            pltpu.make_async_copy(other, target, sem).start()

        return pltpu.make_async_copy(source, target, sem)


def store_in(field):
    def store(r, t, c, count, value):
        field[r, t, pl.ds(PAD + c, count), :] = value

    return store


def store_out(ref):
    def store(r, t, c, count, value):
        ref[r, pl.ds(c - REACH, count), pl.ds(t * LANES, LANES)] = value.astype(jnp.bfloat16)

    return store


class OwnRows:
    def __init__(self, polar, lon, ext, state_ref, edge_w_ref, edge_e_ref, parts, field, base, first, sems):
        tiles, count = field.shape[1], HALO * len(parts)
        self.polar, self.edges = polar, (edge_w_ref, edge_e_ref)
        self.place = (field, base, first, count, lon)
        self.smooth, self.plain = [], []
        for i, (ref, start) in enumerate(parts):
            target = field.at[pl.ds(base + i * HALO, HALO), :, pl.ds(PAD, ext), :]
            self.smooth.append(pltpu.make_async_copy(ref.at[pl.ds(start, HALO)], target, sems.at[i]))
        for t in range(tiles):
            self.plain.append(pltpu.make_async_copy(
                state_ref.at[pl.ds(first, count), :, pl.ds(t * LANES, LANES)],
                field.at[pl.ds(base, count), t, pl.ds(PAD + REACH, lon), :], sems.at[t]))
        self.each(lambda copy: copy.start())

    def each(self, act):
        @pl.when(self.polar)
        def _():
            for copy in self.smooth:
                act(copy)

        @pl.when(jnp.logical_not(self.polar))
        def _():
            for copy in self.plain:
                act(copy)

    def wait(self):
        field, base, first, count, lon = self.place
        edge_w_ref, edge_e_ref = self.edges

        @pl.when(jnp.logical_not(self.polar))
        def _():
            @pl.loop(0, count)
            def _(r):
                for t in range(field.shape[1]):
                    lanes = pl.ds(t * LANES, LANES)
                    field[base + r, t, pl.ds(PAD, REACH), :] = edge_w_ref[first + r, :, lanes].astype(jnp.float32)
                    field[base + r, t, pl.ds(PAD + REACH + lon, REACH), :] = edge_e_ref[first + r, :, lanes].astype(jnp.float32)

        self.each(lambda copy: copy.wait())


def strip(field, base, ext):
    return field.at[pl.ds(base, HALO), :, pl.ds(PAD, ext), :]


def border_kernel(north, rows, lon, ext, info_ref, state_ref, edge_w_ref, edge_e_ref, winds_ref, beyond_ref, raw_ref, late_ref,
                  smooth_a_ref, smooth_b_ref, border_ref, level_ref, one_ref, field_a, field_b, halo_rows, winds, own_sem, sems):
    halo, own, first = (2 * HALO, 0, rows - 2 * HALO) if north else (0, HALO, 0)
    zero = info_ref[4]
    parts = ((smooth_b_ref, 0), (smooth_a_ref, HALO)) if north else ((smooth_a_ref, 0), (smooth_b_ref, 0))
    copies = Copies(sems)
    halo_copy = copies.either(info_ref[3 if north else 2] == 1, late_ref.at[pl.ds(0, HALO)], raw_ref.at[pl.ds(0, HALO)], halo_rows)
    mine = OwnRows(info_ref[1] == 1, lon, ext, state_ref, edge_w_ref, edge_e_ref, parts, field_a, own, first, own_sem)
    wind_copies = [
        copies.start(winds_ref.at[pl.ds(first + 2 if north else 0, HALO + 2)], winds.at[pl.ds(0 if north else 2, HALO + 2)]),
        copies.start(beyond_ref, winds.at[pl.ds(HALO + 2 if north else 0, 2)]),
    ]
    halo_copy.wait()
    put_rows(field_a, halo_rows, halo, HALO, ext)
    mine.wait()
    for copy in wind_copies:
        copy.wait()
    step_rows(field_a, winds, zero, 0, 2 * HALO, 0, 0, ext, store_in(field_b))
    one_copy = copies.start(strip(field_b, 0 if north else HALO, ext), one_ref)

    def store(r, t, c, count, value):
        level_ref[r, t, pl.ds(c, count), :] = value
        border_ref[r, pl.ds(c, count), pl.ds(t * LANES, LANES)] = value.astype(jnp.bfloat16)

    step_rows(field_b, winds, zero, 0, HALO, 2, 0, ext, store)
    one_copy.wait()


def border_rows(north, info, state, edges, winds, beyond, raw, late, smooths):
    rows, lon, channels = state.shape
    ext = winds.shape[1]
    tiles = channels // LANES
    vmem, hbm = pl.BlockSpec(memory_space=pltpu.VMEM), pl.BlockSpec(memory_space=pl.ANY)
    level = jax.ShapeDtypeStruct((HALO, tiles, ext, LANES), jnp.float32)
    return pl.pallas_call(
        functools.partial(border_kernel, north, rows, lon, ext),
        in_specs=[pl.BlockSpec(memory_space=pltpu.SMEM), hbm, vmem, vmem] + [hbm] * 6,
        out_specs=[vmem, vmem, hbm],
        out_shape=[jax.ShapeDtypeStruct((HALO, ext, channels), jnp.bfloat16), level, level],
        scratch_shapes=[
            cells_of(3 * HALO, tiles, ext), cells_of(2 * HALO, tiles, ext),
            half_of(HALO, ext, channels), half_of(2 * HALO, ext, channels),
            pltpu.SemaphoreType.DMA((2,)), pltpu.SemaphoreType.DMA((4,)),
        ],
        compiler_params=pltpu.CompilerParams(vmem_limit_bytes=VMEM_LIMIT),
        cost_estimate=pl.CostEstimate(flops=1000, bytes_accessed=1000, transcendentals=0),
        name="border_north" if north else "border_south",
    )(info, state, *edges, winds, beyond, raw, late, *smooths)


def interior_kernel(rows, lon, ext, info_ref, state_ref, edge_w_ref, edge_e_ref, winds_ref, level_s_ref, level_n_ref,
                    one_s_ref, one_n_ref, smooth_s_ref, smooth_n_ref, out_ref, third_s_ref, third_n_ref,
                    field_a, field_b, field_c, part_ref, winds, sem, in_sem, out_sem):
    inner = rows - 4
    zero = info_ref[4]
    copies = Copies(in_sem)
    mine = OwnRows(info_ref[1] == 1, lon, ext, state_ref, edge_w_ref, edge_e_ref,
                   ((smooth_s_ref, 0), (smooth_n_ref, 0)), field_a, 0, HALO, sem)
    wind_copy = copies.start(winds_ref.at[pl.ds(2, inner)], winds)
    incoming = [copies.start(ref, strip(field, base, ext)) for ref, field, base in (
        (one_s_ref, field_b, 0), (one_n_ref, field_b, inner - HALO), (level_s_ref, field_c, 0), (level_n_ref, field_c, rows - HALO))]
    mine.wait()
    wind_copy.wait()

    def store(r, t, c, count, value):
        field_b[HALO + r, t, pl.ds(PAD + c, count), :] = value

    step_rows(field_a, winds, zero, 0, inner - 2 * HALO, HALO, 0, ext, store)
    for copy in incoming:
        copy.wait()

    def store(r, t, c, count, value):
        field_c[HALO + r, t, pl.ds(PAD + c, count), :] = value

    step_rows(field_b, winds, zero, 0, inner - 4, 2, 0, ext, store)
    step_rows(field_c, winds, zero, 0, inner, 0, 0, ext, store_in(field_b))
    outgoing = [pltpu.make_async_copy(strip(field_b, base, ext), ref, out_sem.at[i])
                for i, (ref, base) in enumerate(((third_s_ref, 0), (third_n_ref, inner - HALO)))]
    for copy in outgoing:
        copy.start()
    step_rows(field_b, winds, zero, 0, inner - 4, 2, REACH, REACH + lon, store_out(part_ref))
    outgoing.append(pltpu.make_async_copy(part_ref, out_ref.at[pl.ds(HALO, rows - 2 * HALO)], out_sem.at[2]))
    outgoing[2].start()
    for copy in outgoing:
        copy.wait()


def interior(info, state, edges, winds, levels, ones, smooths):
    rows, lon, channels = state.shape
    ext = winds.shape[1]
    tiles = channels // LANES
    vmem, hbm = pl.BlockSpec(memory_space=pltpu.VMEM), pl.BlockSpec(memory_space=pl.ANY)
    third = jax.ShapeDtypeStruct((HALO, tiles, ext, LANES), jnp.float32)
    return pl.pallas_call(
        functools.partial(interior_kernel, rows, lon, ext),
        in_specs=[pl.BlockSpec(memory_space=pltpu.SMEM), hbm, vmem, vmem] + [hbm] * 7,
        out_specs=[hbm, hbm, hbm],
        out_shape=[jax.ShapeDtypeStruct((rows, lon, channels), jnp.bfloat16), third, third],
        scratch_shapes=[
            cells_of(rows - 2 * HALO, tiles, ext), cells_of(rows - 4, tiles, ext), cells_of(rows, tiles, ext),
            half_of(rows - 2 * HALO, lon, channels), half_of(rows - 4, ext, channels),
            pltpu.SemaphoreType.DMA((2,)), pltpu.SemaphoreType.DMA((5,)), pltpu.SemaphoreType.DMA((3,)),
        ],
        compiler_params=pltpu.CompilerParams(vmem_limit_bytes=VMEM_LIMIT),
        cost_estimate=pl.CostEstimate(flops=1000, bytes_accessed=1000, transcendentals=0),
        name="interior",
    )(info, state, *edges, winds, *levels, *ones, *smooths)


def finish_kernel(north, rows, lon, ext, _, info_ref, winds_ref, beyond_ref, border_ref, level_ref, third_ref,
                  out_ref, near, last, winds, halo_rows, part_ref, in_sem, out_sem):
    zero = info_ref[4]
    mine, other = (0, HALO) if north else (HALO, 0)
    copies = Copies(in_sem)
    halo_copy = copies.start(border_ref, halo_rows)
    incoming = [
        copies.start(level_ref, strip(near, mine, ext)),
        copies.start(third_ref, strip(last, mine, ext)),
        copies.start(winds_ref.at[pl.ds(rows - HALO if north else 0, HALO)], winds.at[pl.ds(0 if north else 2, HALO)]),
        copies.start(beyond_ref, winds.at[pl.ds(HALO if north else 0, 2)]),
    ]
    halo_copy.wait()
    put_rows(near, halo_rows, other, HALO, ext)
    for copy in incoming:
        copy.wait()

    def store(r, t, c, count, value):
        last[r + other, t, pl.ds(PAD + c, count), :] = value

    step_rows(near, winds, zero, 0, HALO, 2 if north else 0, 0, ext, store)
    step_rows(last, winds, zero, 0, HALO, 0 if north else 2, REACH, REACH + lon, store_out(part_ref))
    copy = pltpu.make_async_copy(part_ref, out_ref.at[pl.ds(rows - HALO if north else 0, HALO)], out_sem.at[0])
    copy.start()
    copy.wait()


def finish(north, info, out, winds, beyond, border, level, third):
    rows, lon, channels = out.shape
    ext = winds.shape[1]
    tiles = channels // LANES
    hbm = pl.BlockSpec(memory_space=pl.ANY)
    return pl.pallas_call(
        functools.partial(finish_kernel, north, rows, lon, ext),
        in_specs=[hbm, pl.BlockSpec(memory_space=pltpu.SMEM)] + [hbm] * 5,
        out_specs=hbm,
        out_shape=jax.ShapeDtypeStruct(out.shape, out.dtype),
        input_output_aliases={0: 0},
        scratch_shapes=[
            cells_of(2 * HALO, tiles, ext), cells_of(2 * HALO, tiles, ext),
            half_of(HALO + 2, ext, channels), half_of(HALO, ext, channels), half_of(HALO, lon, channels),
            pltpu.SemaphoreType.DMA((5,)),
            pltpu.SemaphoreType.DMA((1,)),
        ],
        compiler_params=pltpu.CompilerParams(vmem_limit_bytes=VMEM_LIMIT),
        cost_estimate=pl.CostEstimate(flops=1000, bytes_accessed=1000, transcendentals=0),
        name="finish_north" if north else "finish_south",
    )(out, info, winds, beyond, border, level, third)


def half_of(rows, ext, channels):
    return pltpu.VMEM((rows, ext, channels), jnp.bfloat16)


def cells_of(rows, tiles, ext):
    return pltpu.VMEM((rows, tiles, ext + 2 * PAD, LANES), jnp.float32)


def per_device(state, winds, decay, widths):
    rows, lon, channels = state.shape
    fields = decay.shape[0]
    bands, tiles = lax.axis_size("lat"), lax.axis_size("lon")
    lat, lon_at = lax.axis_index("lat"), lax.axis_index("lon")
    quarter = bands // 4
    ext = round_up(lon + 2 * REACH, 16)
    fill = ext - lon - 2 * REACH
    axes = ("lat", "lon")

    def is_polar(band):
        return band < quarter or band >= bands - quarter

    def polar_at(band):
        return ((band >= 0) & (band < quarter)) | ((band >= bands - quarter) & (band < bands))

    info = jnp.stack([lon_at % 2, polar_at(lat), polar_at(lat - 1), polar_at(lat + 1), lat < 0]).astype(jnp.int32)

    def over_lon(flip):
        return [(b * tiles + l, b * tiles + (l ^ flip)) for b in range(bands) if is_polar(b) for l in range(tiles)]

    def over_lat(shift, wanted=lambda band: True):
        return [(b * tiles + l, (b + shift) * tiles + l)
                for b in range(bands) if 0 <= b + shift < bands and wanted(b) for l in range(tiles)]

    def move(cells, pairs):
        return lax.ppermute(cells, axes, pairs)

    inner = rows - 2 * HALO
    order = [(0, HALO), (rows - HALO, HALO), (HALO, inner)]
    sizes = [2 * HALO, inner // 2, inner // 2]
    starts = [0, 2 * HALO, 2 * HALO + inner // 2]

    def ordered(values):
        return jnp.concatenate([values[f:f + n] for f, n in order], axis=0)

    def joined(cols):
        return jnp.concatenate([state[:, cols].astype(jnp.bfloat16), winds[:, cols]], axis=2)

    east = [(l, (l + 1) % tiles) for l in range(tiles)]
    west = [((l + 1) % tiles, l) for l in range(tiles)]
    head, rear, cells = tie(joined(slice(0, REACH)), joined(slice(lon - REACH, lon)), state)
    from_east = lax.ppermute(head, "lon", west)
    from_west = lax.ppermute(rear, "lon", east)

    opp = [None] * len(sizes)
    circles = [ordered(cells)[:2 * HALO].astype(jnp.bfloat16)]
    circles[0], cells = tie(circles[0], cells)
    opp[0] = move(circles[0], over_lon(2))
    low = ordered(cells).astype(jnp.bfloat16)
    circles += [low[f:f + n] for f, n in zip(starts[1:], sizes[1:])]

    edge_w, edge_e = from_west[:, :, :channels], from_east[:, :, :channels]

    def extend(inner, before, after):
        parts = [before, inner, after, jnp.zeros((inner.shape[0], fill, inner.shape[2]), inner.dtype)]
        return jnp.concatenate(parts, axis=1)

    winds_ext = extend(winds, from_west[:, :, channels:], from_east[:, :, channels:])

    def border(first, wind_first):
        of = slice(first, first + HALO)
        wind = [winds_ext[wind_first + i:wind_first + i + 1] for i in range(2)]
        ends = extend(cells[of].astype(jnp.bfloat16), edge_w[of], edge_e[of])
        return jnp.concatenate([ends, jnp.concatenate(wind, axis=2)], axis=0)

    def is_plain(band):
        return not is_polar(band)

    north_rows, south_rows = border(rows - HALO, rows - 2), border(0, 0)
    raw_s = move(north_rows, over_lat(1, is_plain))
    raw_n = move(south_rows, over_lat(-1, is_plain))
    behind = south_rows[HALO:], north_rows[HALO:]

    def spread(wind):
        half = wind.shape[-1] // 2
        return jnp.concatenate([wind[..., :half]] * 2 + [wind[..., half:]] * 2, axis=-1)

    winds_all = spread(winds_ext)

    def beyond(is_late, late_rows, raw_rows):
        both = jnp.where(is_late, late_rows[HALO], raw_rows[HALO])
        return spread(jnp.stack([both[:, :LANES], both[:, LANES:]]))

    sib = move(low, over_lon(1))
    circles[1], winds_ext = tie(circles[1], winds_ext)
    opp[1] = move(circles[1], over_lon(2))

    own_widths = ordered(lax.dynamic_slice_in_dim(widths, lat * rows, rows))
    rate = jnp.repeat(decay, channels // fields)[None, :]
    reach = own_widths.astype(jnp.float32)[:, None]
    q = jnp.exp(-rate)
    back = round_up(HMAX + 1 + REACH, 8)
    seg = max(back + ext - REACH, round_up(ext + HMAX + 1, 8)) // 8
    carry = jnp.exp(-rate * seg)
    far = jnp.exp(-rate * (reach + 1.0))[:, None, :]
    total = (-jnp.expm1(-rate * (reach + 1.0)) - q * jnp.expm1(-rate * reach)) / -jnp.expm1(-rate)
    scale = (1.0 / total)[:, None, :]

    edges = edge_w, edge_e
    smooths = []
    for i, (f, n) in enumerate(zip(starts, sizes)):
        if i == 0:
            opp[i], raw_n = tie(opp[i], raw_n)
        if i == 1:
            opp[i], raw_s, winds_all = tie(opp[i], raw_s, winds_all)
        if i == 2:
            opp[i], late_s, late_n = tie(opp[i], late_s, late_n)
        if i + 1 < len(sizes) and opp[i + 1] is None:
            opp[i], circles[i + 1] = tie(opp[i], circles[i + 1])
            opp[i + 1] = move(circles[i + 1], over_lon(2))
        diag = move(opp[i], over_lon(1))
        smooth, *ends = smooth_piece(f, n, ext, info, own_widths, circles[i], sib, opp[i], diag,
                                     q, carry, far, scale, behind if i == 0 else ())
        smooths.append(smooth)
        if i + 1 < len(sizes):
            smooth, opp[i + 1] = tie(smooth, opp[i + 1])
        if i == 0:
            late_n, late_s = move(ends[0], over_lat(-1, is_polar)), move(ends[1], over_lat(1, is_polar))
        if i == 1:
            wind_s = beyond(polar_at(lat - 1), late_s, raw_s)
            low_rows, level_s, one_s = border_rows(False, info, state, edges, winds_all, wind_s, raw_s, late_s, smooths[:2])
            to_south = move(low_rows, over_lat(-1))

    wind_n = beyond(polar_at(lat + 1), late_n, raw_n)
    top_rows, level_n, one_n = border_rows(True, info, state, edges, winds_all, wind_n, raw_n, late_n, (smooths[0], smooths[2]))
    to_north = move(top_rows, over_lat(1))
    level_s, to_south, level_n = tie(level_s, to_south, level_n)
    out, third_s, third_n = interior(info, state, edges, winds_all, (level_s, level_n), (one_s, one_n), smooths[1:])
    out = finish(True, info, out, winds_all, wind_n, to_south, level_n, third_n)
    return finish(False, info, out, winds_all, wind_s, to_north, level_s, third_s)


def solution(mesh):
    in_specs = (P("lat", "lon", None), P("lat", "lon", None), P(), P())
    out_specs = P("lat", "lon", None)
    return jax.shard_map(
        per_device, mesh=mesh, in_specs=in_specs, out_specs=out_specs, check_vma=False
    )
```

time: 169 us -> 193 us (1.14)
  the two profiles are of different devices: /device:TPU:23 before, /device:TPU:21 now
where the time goes in v1:
time: 193 us; the launch traced here: 191 us
  Pallas kernels  62.2 us (32%)
  starting transfers between devices  48.6 us (25%)
  waiting for transfers between devices  42.9 us (22%)
  other arithmetic  21.2 us (11%)
  local copies, waits for them, and re-layouts  15.1 us (8%)
    ppermute x13, starting transfers between devices, move(): return lax.ppermute(cells, axes, pairs)  47.8 us
    ppermute x13, waiting for transfers between devices, move(): return lax.ppermute(cells, axes, pairs)  42.9 us
    pallas_call x2, Pallas kernels, border_rows(): pl.pallas_call(functools.partial(border_kernel, north, rows, lon, ext), i...  19.2 us
    pallas_call x1, Pallas kernels, interior(): pl.pallas_call(functools.partial(interior_kernel, rows, lon, ext), in_spe...  17.5 us
    pallas_call x2, Pallas kernels, finish(): pl.pallas_call(functools.partial(finish_kernel, north, rows, lon, ext), i...  14.2 us
    pallas_call x3, Pallas kernels, smooth_piece(): pl.pallas_call(functools.partial(smooth_kernel, geo, len(extras)), grid=(...  11.3 us
    concatenate x3, other arithmetic, spread(): jnp.concatenate([wind[..., :half]] * 2 + [wind[..., half:]] * 2, axis=-1)  7.21 us
    unnamed x64, local copies, waits for them, and re-layouts  6.62 us
  transfers between devices with their start and end apart: 15, of which 3 were waited for; matrix products, arithmetic and copies ran while one was open for 13% of the time, Pallas kernels for 29%

profile of v1, /device:TPU:21, one launch (start us, length us, event | category | flops | bytes accessed | tf_op | source)
XLA Modules:
  0.0 190.7 jit_solution(9413706660132811944)
XLA Ops:
  0.8 3.1 %convert.24 = bf16[16,360,256]{2,1,0:T(8,128)(2,1)S(1)} convert(f32[16,360,256]{2,1,0:T(8,128)} %state_ref.5) | non-fusion elementwise | flops 1474560 | bytes 8847360 | tf_op jit(solution)/shard_map/convert.13
  6.9 1.8 collective-permute-start.3
  10.7 1.9 pad_maximum_fusion.1
  14.4 1.7 maximum_maximum_fusion.1
  16.1 3.0 %collective-permute-start.4 = (bf16[5,384,256]{2,1,0:T(8,128)(2,1)}, bf16[5,384,256]{2,1,0:T(8,128)(2,1)}, u32[]{:S(2)}, u32[]{:S(2)}) collective-permute-start(bf16[5,384,256]{2,1,0:T(8,128)(2,1)} %get-tuple-element.96), channel_id=1, source_target_pairs={{8,4},{9,5},{10,6},{11,7},{12,8},{13,9},{14,10},{15,11},{16,12},{1... | collective-permute-start | bytes 2949128 | tf_op jit(solution)/shard_map/ppermute | solution.py:470
  19.9 20.5 %collective-permute-done.4.raw_ref = bf16[5,384,256]{2,1,0:T(8,128)(2,1)} collective-permute-done((bf16[5,384,256]{2,1,0:T(8,128)(2,1)}, bf16[5,384,256]{2,1,0:T(8,128)(2,1)}, u32[]{:S(2)}, u32[]{:S(2)}) %collective-permute-start.4) | collective-permute-done | bytes 983072 | tf_op jit(solution)/shard_map/ppermute | solution.py:470
  40.3 1.8 collective-permute-start.5
  45.9 2.3 %fusion.13 = (bf16[4,360,256]{2,1,0:T(8,128)(2,1)S(1)}, bf16[4,360,256]{2,1,0:T(8,128)(2,1)}) fusion(bf16[16,360,256]{2,1,0:T(8,128)(2,1)} %copy-done.4), kind=kLoop, calls=%fused_computation.42 | loop fusion | bytes 2949120 | tf_op jit(solution)/shard_map/slice | solution.py:494
  48.2 1.9 %collective-permute-start.7 = (bf16[5,384,256]{2,1,0:T(8,128)(2,1)}, bf16[5,384,256]{2,1,0:T(8,128)(2,1)}, u32[]{:S(2)}, u32[]{:S(2)}) collective-permute-start(bf16[5,384,256]{2,1,0:T(8,128)(2,1)} %get-tuple-element.95), channel_id=1, source_target_pairs={{8,12},{9,13},{10,14},{11,15},{12,16},{13,17},{14,18},{15,19},{16,... | collective-permute-start | bytes 2949128 | tf_op jit(solution)/shard_map/ppermute | solution.py:470
  50.2 1.5 collective-permute-start.6
  53.8 1.6 copy-done.1
  55.4 5.2 %smooth.3 = (f32[8,2,384,128]{3,2,1,0:T(8,128)}, bf16[5,384,256]{2,1,0:T(8,128)(2,1)}, bf16[5,384,256]{2,1,0:T(8,128)(2,1)}) custom-call(s32[5]{0:T(128)} %stack.57.info_ref, s32[8]{0:T(128)} %pad_add_fusion.widths_ref, bf16[8,360,256]{2,1,0:T(8,128)(2,1)} %pad_maximum_fusion.3.refs_0_, bf16[16,360,256]{2,1,0:T(8,128)(2,1)} %copy-done.1, ...), custom_call_target="tpu_custom_call" | custom-call | flops 1000 | bytes 1000 | tf_op jit(solution)/shard_map/smooth/pallas_call | solution.py:141
  61.3 5.3 %pad_maximum_fusion.winds_ref = bf16[16,384,256]{2,1,0:T(8,128)(2,1)} fusion(bf16[16,384,64]{2,1,0:T(8,128)(2,1)S(1)} %get-tuple-element.80, bf16[16,8,128]{2,1,0:T(8,128)(2,1)} %copy-done.25, bf16[16,8,128]{2,1,0:T(8,128)(2,1)} %copy-done.24, bf16[16,360,128]{2,1,0:T(8,128)(2,1)S(1)} %copy-done.6, bf16[16,8,128]{2,1,0:T(8,128)(2,1)} %copy-done.23, ...), kind=kLoop, calls=%fused_computation | loop fusion | flops 18874368 | bytes 6291456 | tf_op jit(solution)/shard_map/concatenate | solution.py:520
  66.7 5.8 %collective-permute-done.7.raw_ref = bf16[5,384,256]{2,1,0:T(8,128)(2,1)} collective-permute-done((bf16[5,384,256]{2,1,0:T(8,128)(2,1)}, bf16[5,384,256]{2,1,0:T(8,128)(2,1)}, u32[]{:S(2)}, u32[]{:S(2)}) %collective-permute-start.7) | collective-permute-done | bytes 983072 | tf_op jit(solution)/shard_map/ppermute | solution.py:470
  76.8 3.1 %smooth.4.smooth_b_ref.smooth_s_ref = f32[4,2,384,128]{3,2,1,0:T(8,128)} custom-call(s32[5]{0:T(128)} %stack.57.info_ref, s32[4]{0:T(128)} %get-tuple-element.102.widths_ref, bf16[4,360,256]{2,1,0:T(8,128)(2,1)} %get-tuple-element.44.refs_0_, bf16[16,360,256]{2,1,0:T(8,128)(2,1)} %copy-done.1, bf16[4,360,256]{2,1,0:T(8,128)(2,1)} %collective-permute-done.6.refs_2_, ...), custom_call_target="tpu_custom_call" | custom-call | flops 1000 | bytes 1000 | tf_op jit(solution)/shard_map/smooth/pallas_call | solution.py:141
  82.8 9.6 %border_south.1 = (bf16[4,384,256]{2,1,0:T(8,128)(2,1)}, f32[4,2,384,128]{3,2,1,0:T(8,128)}, f32[4,2,384,128]{3,2,1,0:T(8,128)}) custom-call(s32[5]{0:T(128)} %stack.57.info_ref, f32[16,360,256]{2,1,0:T(8,128)} %state_ref.5, bf16[16,8,256]{2,1,0:T(8,128)(2,1)} %slice.192.edge_w_ref, bf16[16,8,256]{2,1,0:T(8,128)(2,1)} %slice.193.edge_e_ref, ...), custom_call_target="tpu_custom_call" | custom-call | flops 1000 | bytes 1000 | tf_op jit(solution)/shard_map/border_south/pallas_call | solution.py:311
  92.4 3.9 %collective-permute-start.10 = (bf16[4,384,256]{2,1,0:T(8,128)(2,1)}, bf16[4,384,256]{2,1,0:T(8,128)(2,1)S(1)}, u32[]{:S(2)}, u32[]{:S(2)}) collective-permute-start(bf16[4,384,256]{2,1,0:T(8,128)(2,1)} %get-tuple-element.52), channel_id=1, source_target_pairs={{4,0},{5,1},{6,2},{7,3},{8,4},{9,5},{10,6},{11,7},{12,8},{13,9},{1... | collective-permute-start | bytes 2359304 | tf_op jit(solution)/shard_map/ppermute | solution.py:470
  99.2 3.0 %smooth.5.smooth_b_ref.smooth_n_ref = f32[4,2,384,128]{3,2,1,0:T(8,128)} custom-call(s32[5]{0:T(128)} %stack.57.info_ref, s32[4]{0:T(128)} %get-tuple-element.101.widths_ref, bf16[4,360,256]{2,1,0:T(8,128)(2,1)} %copy-done.7, bf16[16,360,256]{2,1,0:T(8,128)(2,1)} %copy-done.1, bf16[4,360,256]{2,1,0:T(8,128)(2,1)} %copy-done.20, ...), custom_call_target="tpu_custom_call" | custom-call | flops 1000 | bytes 1000 | tf_op jit(solution)/shard_map/smooth/pallas_call | solution.py:141
  102.2 9.6 %border_north.1 = (bf16[4,384,256]{2,1,0:T(8,128)(2,1)}, f32[4,2,384,128]{3,2,1,0:T(8,128)}, f32[4,2,384,128]{3,2,1,0:T(8,128)}) custom-call(s32[5]{0:T(128)} %stack.57.info_ref, f32[16,360,256]{2,1,0:T(8,128)} %state_ref.5, bf16[16,8,256]{2,1,0:T(8,128)(2,1)} %slice.192.edge_w_ref, bf16[16,8,256]{2,1,0:T(8,128)(2,1)} %slice.193.edge_e_ref, ...), custom_call_target="tpu_custom_call" | custom-call | flops 1000 | bytes 1000 | tf_op jit(solution)/shard_map/border_north/pallas_call | solution.py:311
  111.8 29.4 %collective-permute-start.14 = (bf16[4,384,256]{2,1,0:T(8,128)(2,1)}, bf16[4,384,256]{2,1,0:T(8,128)(2,1)S(1)}, u32[]{:S(2)}, u32[]{:S(2)}) collective-permute-start(bf16[4,384,256]{2,1,0:T(8,128)(2,1)} %get-tuple-element.67), channel_id=1, source_target_pairs={{0,4},{1,5},{2,6},{3,7},{4,8},{5,9},{6,10},{7,11},{8,12},{9,13},{1... | collective-permute-start | bytes 2359304 | tf_op jit(solution)/shard_map/ppermute | solution.py:470
  141.3 16.6 %collective-permute-done.10.border_ref = bf16[4,384,256]{2,1,0:T(8,128)(2,1)S(1)} collective-permute-done((bf16[4,384,256]{2,1,0:T(8,128)(2,1)}, bf16[4,384,256]{2,1,0:T(8,128)(2,1)S(1)}, u32[]{:S(2)}, u32[]{:S(2)}) %collective-permute-start.10) | collective-permute-done | bytes 786464 | tf_op jit(solution)/shard_map/ppermute | solution.py:470
  157.9 17.5 %interior.1 = (bf16[16,360,256]{2,1,0:T(8,128)(2,1)}, f32[4,2,384,128]{3,2,1,0:T(8,128)}, f32[4,2,384,128]{3,2,1,0:T(8,128)}) custom-call(s32[5]{0:T(128)} %stack.57.info_ref, f32[16,360,256]{2,1,0:T(8,128)} %state_ref.5, bf16[16,8,256]{2,1,0:T(8,128)(2,1)} %slice.192.edge_w_ref, bf16[16,8,256]{2,1,0:T(8,128)(2,1)} %slice.193.edge_e_ref, ...), custom_call_target="tpu_custom_call" | custom-call | flops 1000 | bytes 1000 | tf_op jit(solution)/shard_map/interior/pallas_call | solution.py:370
  175.4 7.2 %finish_north.1._ = bf16[16,360,256]{2,1,0:T(8,128)(2,1)} custom-call(bf16[16,360,256]{2,1,0:T(8,128)(2,1)} %get-tuple-element.64._, s32[5]{0:T(128)} %stack.57.info_ref, bf16[16,384,256]{2,1,0:T(8,128)(2,1)} %pad_maximum_fusion.winds_ref, bf16[2,384,256]{2,1,0:T(8,128)(2,1)} %fusion.7.beyond_ref, ...), custom_call_target="tpu_custom_call", output_to_operand_aliasing={{}: (0, {})} | custom-call | flops 1000 | bytes 1000 | tf_op jit(solution)/shard_map/finish_north/pallas_call | solution.py:418
  183.4 7.1 %finish_south.1 = bf16[16,360,256]{2,1,0:T(8,128)(2,1)} custom-call(bf16[16,360,256]{2,1,0:T(8,128)(2,1)} %finish_north.1._, s32[5]{0:T(128)} %stack.57.info_ref, bf16[16,384,256]{2,1,0:T(8,128)(2,1)} %pad_maximum_fusion.winds_ref, bf16[2,384,256]{2,1,0:T(8,128)(2,1)} %fusion.5.beyond_ref, ...), custom_call_target="tpu_custom_call", output_to_operand_aliasing={{}: (0, {})} | custom-call | flops 1000 | bytes 1000 | tf_op jit(solution)/shard_map/finish_south/pallas_call | solution.py:418
  (129 shorter events, 25.5 us)
Async XLA Ops:
  3.9 9.6 %collective-permute-start = (bf16[16,8,384]{2,1,0:T(8,128)(2,1)S(1)}, bf16[16,8,384]{2,1,0:T(8,128)(2,1)S(1)}, u32[]{:S(2)}, u32[]{:S(2)}) collective-permute-start(bf16[16,8,384]{2,1,0:T(8,128)(2,1)S(1)} %get-tuple-element.37), channel_id=1, source_target_pairs={{0,1},{1,2},{2,3},{3,0},{4,5},{5,6},{6,7},{7,4},{8,9},{9,10},{10,1... | collective-permute-start | bytes 294920 | tf_op jit(solution)/shard_map/ppermute | solution.py:487
  4.8 8.8 %collective-permute-start.1 = (bf16[16,8,384]{2,1,0:T(8,128)(2,1)S(1)}, bf16[16,8,384]{2,1,0:T(8,128)(2,1)S(1)}, u32[]{:S(2)}, u32[]{:S(2)}) collective-permute-start(bf16[16,8,384]{2,1,0:T(8,128)(2,1)S(1)} %get-tuple-element.38), channel_id=1, source_target_pairs={{1,0},{2,1},{3,2},{0,3},{5,4},{6,5},{7,6},{4,7},{9,8},{10,9},{11,1... | collective-permute-start | bytes 294920 | tf_op jit(solution)/shard_map/ppermute | solution.py:486
  6.9 33.4 %collective-permute-start.3 = (bf16[8,360,256]{2,1,0:T(8,128)(2,1)}, bf16[8,360,256]{2,1,0:T(8,128)(2,1)}, u32[]{:S(2)}, u32[]{:S(2)}) collective-permute-start(bf16[8,360,256]{2,1,0:T(8,128)(2,1)} %pad_maximum_fusion.3.refs_0_), channel_id=1, source_target_pairs={{0,2},{1,3},{2,0},{3,1},{4,6},{5,7},{6,4},{7,5},{24,26},{25,27},{2... | collective-permute-start | bytes 4423688 | tf_op jit(solution)/shard_map/ppermute | solution.py:470
  12.6 41.2 %collective-permute-start.2 = (bf16[16,360,256]{2,1,0:T(8,128)(2,1)}, bf16[16,360,256]{2,1,0:T(8,128)(2,1)S(1)}, u32[]{:S(2)}, u32[]{:S(2)}) collective-permute-start(bf16[16,360,256]{2,1,0:T(8,128)(2,1)} %pad_maximum_fusion.1), channel_id=1, source_target_pairs={{0,1},{1,0},{2,3},{3,2},{4,5},{5,4},{6,7},{7,6},{24,25},{25,24},{2... | collective-permute-start | bytes 8847368 | tf_op jit(solution)/shard_map/ppermute | solution.py:470
  16.1 24.2 %collective-permute-start.4 = (bf16[5,384,256]{2,1,0:T(8,128)(2,1)}, bf16[5,384,256]{2,1,0:T(8,128)(2,1)}, u32[]{:S(2)}, u32[]{:S(2)}) collective-permute-start(bf16[5,384,256]{2,1,0:T(8,128)(2,1)} %get-tuple-element.96), channel_id=1, source_target_pairs={{8,4},{9,5},{10,6},{11,7},{12,8},{13,9},{14,10},{15,11},{16,12},{1... | collective-permute-start | bytes 2949128 | tf_op jit(solution)/shard_map/ppermute | solution.py:470
  40.3 13.4 %collective-permute-start.5 = (bf16[8,360,256]{2,1,0:T(8,128)(2,1)}, bf16[8,360,256]{2,1,0:T(8,128)(2,1)}, u32[]{:S(2)}, u32[]{:S(2)}) collective-permute-start(bf16[8,360,256]{2,1,0:T(8,128)(2,1)} %collective-permute-done.3.refs_2_), channel_id=1, source_target_pairs={{0,1},{1,0},{2,3},{3,2},{4,5},{5,4},{6,7},{7,6},{24,25},{25,24},{2... | collective-permute-start | bytes 4423688 | tf_op jit(solution)/shard_map/ppermute | solution.py:470
  45.0 7.4 %copy-start.11 = (bf16[1,384,128]{2,1,0:T(8,128)(2,1)S(1)}, bf16[1,384,128]{2,1,0:T(8,128)(2,1)}, u32[]{:S(2)}) copy-start(bf16[1,384,128]{2,1,0:T(8,128)(2,1)} %copy-done.10) | copy-start | bytes 294916
  45.0 7.4 %copy-start.13 = (bf16[1,384,128]{2,1,0:T(8,128)(2,1)S(1)}, bf16[1,384,128]{2,1,0:T(8,128)(2,1)}, u32[]{:S(2)}) copy-start(bf16[1,384,128]{2,1,0:T(8,128)(2,1)} %copy-done.12) | copy-start | bytes 294916
  45.0 8.1 %copy-start.3 = (bf16[16,384,128]{2,1,0:T(8,128)(2,1)S(1)}, bf16[16,384,128]{2,1,0:T(8,128)(2,1)}, u32[]{:S(2)}) copy-start(bf16[16,384,128]{2,1,0:T(8,128)(2,1)} %copy-done.2) | copy-start | bytes 4718596
  48.2 24.9 %copy-start.7 = (bf16[4,360,256]{2,1,0:T(8,128)(2,1)}, bf16[4,360,256]{2,1,0:T(8,128)(2,1)S(1)}, u32[]{:S(2)}) copy-start(bf16[4,360,256]{2,1,0:T(8,128)(2,1)S(1)} %get-tuple-element.53.refs_0_) | copy-start | bytes 2211844
  48.2 24.2 %collective-permute-start.7 = (bf16[5,384,256]{2,1,0:T(8,128)(2,1)}, bf16[5,384,256]{2,1,0:T(8,128)(2,1)}, u32[]{:S(2)}, u32[]{:S(2)}) collective-permute-start(bf16[5,384,256]{2,1,0:T(8,128)(2,1)} %get-tuple-element.95), channel_id=1, source_target_pairs={{8,12},{9,13},{10,14},{11,15},{12,16},{13,17},{14,18},{15,19},{16,... | collective-permute-start | bytes 2949128 | tf_op jit(solution)/shard_map/ppermute | solution.py:470
  50.2 16.5 %collective-permute-start.6 = (bf16[4,360,256]{2,1,0:T(8,128)(2,1)}, bf16[4,360,256]{2,1,0:T(8,128)(2,1)}, u32[]{:S(2)}, u32[]{:S(2)}) collective-permute-start(bf16[4,360,256]{2,1,0:T(8,128)(2,1)} %get-tuple-element.44.refs_0_), channel_id=1, source_target_pairs={{0,2},{1,3},{2,0},{3,1},{4,6},{5,7},{6,4},{7,5},{24,26},{25,27},{2... | collective-permute-start | bytes 2211848 | tf_op jit(solution)/shard_map/ppermute | solution.py:470
  60.6 19.3 %collective-permute-start.8 = (bf16[5,384,256]{2,1,0:T(8,128)(2,1)}, bf16[5,384,256]{2,1,0:T(8,128)(2,1)S(1)}, u32[]{:S(2)}, u32[]{:S(2)}) collective-permute-start(bf16[5,384,256]{2,1,0:T(8,128)(2,1)} %get-tuple-element.47), channel_id=1, source_target_pairs={{0,4},{1,5},{2,6},{3,7},{4,8},{5,9},{6,10},{7,11},{24,28},{25,29},... | collective-permute-start | bytes 2949128 | tf_op jit(solution)/shard_map/ppermute | solution.py:470
  61.3 13.3 %copy-start.27 = (bf16[16,8,384]{2,1,0:T(8,128)(2,1)S(1)}, bf16[16,8,384]{2,1,0:T(8,128)(2,1)}, u32[]{:S(2)}) copy-start(bf16[16,8,384]{2,1,0:T(8,128)(2,1)} %copy-done.26) | copy-start | bytes 294916
  61.3 13.9 %copy-start.29 = (bf16[16,8,384]{2,1,0:T(8,128)(2,1)S(1)}, bf16[16,8,384]{2,1,0:T(8,128)(2,1)}, u32[]{:S(2)}) copy-start(bf16[16,8,384]{2,1,0:T(8,128)(2,1)} %copy-done.28) | copy-start | bytes 294916
  72.4 3.4 %collective-permute-start.9 = (bf16[4,360,256]{2,1,0:T(8,128)(2,1)}, bf16[4,360,256]{2,1,0:T(8,128)(2,1)S(1)}, u32[]{:S(2)}, u32[]{:S(2)}) collective-permute-start(bf16[4,360,256]{2,1,0:T(8,128)(2,1)} %collective-permute-done.6.refs_2_), channel_id=1, source_target_pairs={{0,1},{1,0},{2,3},{3,2},{4,5},{5,4},{6,7},{7,6},{24,25},{25,24},{2... | collective-permute-start | bytes 2211848 | tf_op jit(solution)/shard_map/ppermute | solution.py:470
  73.1 6.7 %collective-permute-start.11 = (bf16[4,360,256]{2,1,0:T(8,128)(2,1)S(1)}, bf16[4,360,256]{2,1,0:T(8,128)(2,1)S(1)}, u32[]{:S(2)}, u32[]{:S(2)}) collective-permute-start(bf16[4,360,256]{2,1,0:T(8,128)(2,1)S(1)} %get-tuple-element.53.refs_0_), channel_id=1, source_target_pairs={{0,2},{1,3},{2,0},{3,1},{4,6},{5,7},{6,4},{7,5},{24,26},{25,27},{2... | collective-permute-start | bytes 2211848 | tf_op jit(solution)/shard_map/ppermute | solution.py:470
  73.9 7.2 %collective-permute-start.12 = (bf16[5,384,256]{2,1,0:T(8,128)(2,1)}, bf16[5,384,256]{2,1,0:T(8,128)(2,1)S(1)}, u32[]{:S(2)}, u32[]{:S(2)}) collective-permute-start(bf16[5,384,256]{2,1,0:T(8,128)(2,1)} %get-tuple-element.55), channel_id=1, source_target_pairs={{4,0},{5,1},{6,2},{7,3},{24,20},{25,21},{26,22},{27,23},{28,24},{2... | collective-permute-start | bytes 2949128 | tf_op jit(solution)/shard_map/ppermute | solution.py:470
  79.8 12.6 %copy-start.20 = (bf16[4,360,256]{2,1,0:T(8,128)(2,1)}, bf16[4,360,256]{2,1,0:T(8,128)(2,1)S(1)}, u32[]{:S(2)}) copy-start(bf16[4,360,256]{2,1,0:T(8,128)(2,1)S(1)} %collective-permute-done.11.refs_2_) | copy-start | bytes 2211844
  81.1 15.3 %copy-start.8 = (bf16[5,384,256]{2,1,0:T(8,128)(2,1)}, bf16[5,384,256]{2,1,0:T(8,128)(2,1)S(1)}, u32[]{:S(2)}) copy-start(bf16[5,384,256]{2,1,0:T(8,128)(2,1)S(1)} %collective-permute-done.12.late_ref) | copy-start | bytes 2949124
  81.1 17.2 %collective-permute-start.13 = (bf16[4,360,256]{2,1,0:T(8,128)(2,1)S(1)}, bf16[4,360,256]{2,1,0:T(8,128)(2,1)S(1)}, u32[]{:S(2)}, u32[]{:S(2)}) collective-permute-start(bf16[4,360,256]{2,1,0:T(8,128)(2,1)S(1)} %collective-permute-done.11.refs_2_), channel_id=1, source_target_pairs={{0,1},{1,0},{2,3},{3,2},{4,5},{5,4},{6,7},{7,6},{24,25},{25,24},{2... | collective-permute-start | bytes 2211848 | tf_op jit(solution)/shard_map/ppermute | solution.py:470
  92.4 65.5 %collective-permute-start.10 = (bf16[4,384,256]{2,1,0:T(8,128)(2,1)}, bf16[4,384,256]{2,1,0:T(8,128)(2,1)S(1)}, u32[]{:S(2)}, u32[]{:S(2)}) collective-permute-start(bf16[4,384,256]{2,1,0:T(8,128)(2,1)} %get-tuple-element.52), channel_id=1, source_target_pairs={{4,0},{5,1},{6,2},{7,3},{8,4},{9,5},{10,6},{11,7},{12,8},{13,9},{1... | collective-permute-start | bytes 2359304 | tf_op jit(solution)/shard_map/ppermute | solution.py:470
  111.8 70.7 %collective-permute-start.14 = (bf16[4,384,256]{2,1,0:T(8,128)(2,1)}, bf16[4,384,256]{2,1,0:T(8,128)(2,1)S(1)}, u32[]{:S(2)}, u32[]{:S(2)}) collective-permute-start(bf16[4,384,256]{2,1,0:T(8,128)(2,1)} %get-tuple-element.67), channel_id=1, source_target_pairs={{0,4},{1,5},{2,6},{3,7},{4,8},{5,9},{6,10},{7,11},{8,12},{9,13},{1... | collective-permute-start | bytes 2359304 | tf_op jit(solution)/shard_map/ppermute | solution.py:470
  157.9 17.5 %copy-start.18 = (bf16[4,384,256]{2,1,0:T(8,128)(2,1)}, bf16[4,384,256]{2,1,0:T(8,128)(2,1)S(1)}, u32[]{:S(2)}) copy-start(bf16[4,384,256]{2,1,0:T(8,128)(2,1)S(1)} %collective-permute-done.10.border_ref) | copy-start | bytes 2359300
  (23 other events, 57.9 us)

commit v2 on v1

v2 whole, which is shorter than its diff:
```python
import functools

import jax
import jax.numpy as jnp
from jax import lax
from jax.experimental import pallas as pl
from jax.experimental.pallas import tpu as pltpu
from jax.sharding import PartitionSpec as P

ADV_STEPS = 4
REACH = 2 * ADV_STEPS
ROUND = 2
HALO = 2 * ROUND
HMAX = 480
LANES = 128
MIB = 1024 * 1024
ODD, POLAR, OUTER_LATE, INNER_LATE, ZERO, LOW_HALF, MIDDLE = range(7)
PAD = 8
COLS = 48


def tie(*values):
    return lax.optimization_barrier(values)


def round_up(value, unit):
    return -(-value // unit) * unit


def smooth_kernel(geo, sends, info_ref, widths_ref, *refs):
    ins, extra_refs, outs, scratch = refs[:8], refs[8:8 + sends], refs[8 + sends:9 + 2 * sends], refs[9 + 2 * sends:]

    @pl.when(info_ref[POLAR] == 1)
    def _():
        smooth_rows(geo, info_ref[ODD] == 1, widths_ref, *ins, *outs[:1], outs[1:], *scratch)
        for ref, extra_ref in zip(outs[1:], extra_refs):
            ref[HALO] = extra_ref[0]


def smooth_rows(geo, odd, widths_ref, own_ref, sib_ref, opp_ref, diag_ref, q_ref, carry_ref, far_ref, scale_ref,
                level_ref, border_refs, cells, east_sum, west_sum):
    lon, back, span, seg, ext = geo
    rows, tiles = own_ref.shape[0], own_ref.shape[2] // LANES
    chains = [(r, t) for r in range(rows) for t in range(tiles)]

    def put(ref, start, begin, count):
        @pl.loop(0, rows)
        def _(r):
            for t in range(tiles):
                part = ref[r, pl.ds(begin, count), pl.ds(t * LANES, LANES)]
                cells[r * tiles + t, pl.ds(start, count), :] = part.astype(jnp.float32)

    head = back - lon
    put(opp_ref, 0, lon - head, head)
    put(own_ref, back, 0, lon)
    put(opp_ref, back + 2 * lon, 0, span - REACH - 2 * lon)

    @pl.when(odd)
    def _():
        put(sib_ref, back - lon, 0, lon)
        put(diag_ref, back + lon, 0, lon)

    @pl.when(jnp.logical_not(odd))
    def _():
        put(diag_ref, back - lon, 0, lon)
        put(sib_ref, back + lon, 0, lon)

    q = [jnp.broadcast_to(q_ref[0:1, t * LANES:(t + 1) * LANES], (8, LANES)) for t in range(tiles)]
    jump = [carry_ref[0:1, t * LANES:(t + 1) * LANES] for t in range(tiles)]
    zero = jnp.zeros((8, LANES), jnp.float32)
    none = jnp.zeros((1, LANES), jnp.float32)
    east_base = back - REACH

    for base, total, forward in ((east_base, east_sum, False), (0, west_sum, True)):
        def at(i, forward=forward):
            return i if forward else seg - 1 - i

        def totals(i, acc, base=base):
            return tuple(cells[r * tiles + t, pl.ds(base + at(i), 8, stride=seg), :] + q[t] * acc[n]
                         for n, (r, t) in enumerate(chains))

        acc = lax.fori_loop(0, seg, totals, (zero,) * len(chains), unroll=4)
        start = []
        for n, (r, t) in enumerate(chains):
            carry = none
            parts = [None] * 8
            for k in (range(8) if forward else range(7, -1, -1)):
                parts[k] = carry
                carry = acc[n][k:k + 1] + jump[t] * carry
            start.append(jnp.concatenate(parts, axis=0))

        def sums(i, acc, base=base, total=total):
            new = []
            for n, (r, t) in enumerate(chains):
                v = cells[r * tiles + t, pl.ds(base + at(i), 8, stride=seg), :] + q[t] * acc[n]
                total[r * tiles + t, pl.ds(at(i), 8, stride=seg), :] = v
                new.append(v)
            return tuple(new)

        lax.fori_loop(0, seg, sums, tuple(start), unroll=4)

    step = COLS

    def one_row(r, border_ref, border_row):
        width = widths_ref[r]
        for t in range(tiles):
            n = r * tiles + t
            far = jnp.broadcast_to(far_ref[r, 0:1, t * LANES:(t + 1) * LANES], (step, LANES))
            scale = jnp.broadcast_to(scale_ref[r, 0:1, t * LANES:(t + 1) * LANES], (step, LANES))
            for c in range(0, ext, step):
                near = east_sum[n, pl.ds(c, step), :] + west_sum[n, pl.ds(back - REACH + c, step), :]
                cut = east_sum[n, pl.ds(c + 1 + width, step), :] + west_sum[n, pl.ds(back - REACH + c - 1 - width, step), :]
                mid = cells[n, pl.ds(back - REACH + c, step), :]
                value = ((near - mid - far * cut) * scale).astype(jnp.bfloat16)
                level_ref[r, t, pl.ds(c, step), :] = value.astype(jnp.float32)
                if border_ref is not None:
                    border_ref[border_row, pl.ds(c, step), pl.ds(t * LANES, LANES)] = value

    @pl.loop(0, rows)
    def _(r):
        one_row(r, border_refs[0] if border_refs else None, r)


def smooth_piece(piece, rows, ext, info, widths, own, sib, opp, diag, q, carry, far, scale, extras):
    lon, channels = own.shape[1:]
    tiles = channels // LANES
    back = round_up(HMAX + 1 + REACH, 8)
    span = round_up(ext + HMAX + 1, 8)
    seg = max(back + ext - REACH, span) // 8
    geo = (lon, back, 8 * seg, seg, ext)
    smem, vmem = pl.BlockSpec(memory_space=pltpu.SMEM), pl.BlockSpec(memory_space=pltpu.VMEM)
    part = pl.BlockSpec((rows, lon, channels), lambda i: (piece % 2, 0, 0))
    table = pl.BlockSpec((rows, 1, channels), lambda i: (piece, 0, 0))
    border = jax.ShapeDtypeStruct((HALO + 1, ext, channels), jnp.bfloat16)
    of_rows = slice(piece * rows, (piece + 1) * rows)
    return pl.pallas_call(
        functools.partial(smooth_kernel, geo, len(extras)),
        grid=(1,),
        in_specs=[smem, smem, vmem, part, vmem, vmem, vmem, vmem, table, table] + [vmem] * len(extras),
        out_specs=[vmem] * (1 + len(extras)),
        out_shape=[jax.ShapeDtypeStruct((rows, tiles, ext, LANES), jnp.float32)] + [border] * len(extras),
        scratch_shapes=[
            pltpu.VMEM((rows * tiles, back - REACH + 8 * seg, LANES), jnp.float32),
            pltpu.VMEM((rows * tiles, 8 * seg, LANES), jnp.float32),
            pltpu.VMEM((rows * tiles, 8 * seg, LANES), jnp.float32),
        ],
        compiler_params=pltpu.CompilerParams(vmem_limit_bytes=28 * MIB),
        cost_estimate=pl.CostEstimate(flops=1000, bytes_accessed=1000, transcendentals=0),
        name="smooth",
    )(info, widths[of_rows], own, sib, opp, diag, q, carry, far, scale, *extras)


def update(src, r, t, c, count, u, v, zero):
    def at(dr, dc):
        return src[r + dr, t, pl.ds(PAD + c + dc + (zero if dc else 0), count), :]

    mid = at(0, 0)
    mid30 = 30.0 * mid
    e1, w1, e2, w2 = at(0, 1), at(0, -1), at(0, 2), at(0, -2)
    n1, s1, n2, s2 = at(1, 0), at(-1, 0), at(2, 0), at(-2, 0)
    first_x = (e2 - w2) - 8.0 * (e1 - w1)
    second_x = 16.0 * (e1 + w1) - (e2 + w2) - mid30
    first_y = (n2 - s2) - 8.0 * (n1 - s1)
    second_y = 16.0 * (n1 + s1) - (n2 + s2) - mid30
    change = u * (first_x + (6.0 * u) * second_x) + v * (first_y + (6.0 * v) * second_y)
    return mid + change


def put_rows(field, ref, base, count, ext):
    @pl.loop(0, count)
    def _(r):
        for t in range(field.shape[1]):
            field[base + r, t, pl.ds(PAD, ext), :] = ref[r, :, pl.ds(t * LANES, LANES)].astype(jnp.float32)


def step_rows(source, winds, zero, first, last, offset, start, stop, store):
    half = LANES // 2
    eastward = lax.broadcasted_iota(jnp.int32, (COLS, LANES), 1) < half

    @pl.loop(first, last)
    def _(r):
        for c in range(start, stop, COLS):
            count = min(COLS, stop - c)
            both = winds[r + offset, pl.ds(c, count), :].astype(jnp.float32) * (1.0 / 12.0)
            swapped = pltpu.roll(both, half, 1)
            u = jnp.where(eastward[:count], both, swapped)
            v = jnp.where(eastward[:count], swapped, both)
            for t in range(source.shape[1]):
                store(r, t, c, count, update(source, r + 2, t, c, count, u, v, zero))


class Copies:
    def __init__(self, sems):
        self.sems, self.used = sems, 0

    def start(self, source, target):
        copy = pltpu.make_async_copy(source, target, self.sems.at[self.used])
        self.used += 1
        copy.start()
        return copy

    def either(self, flag, source, other, target):
        sem = self.sems.at[self.used]
        self.used += 1

        @pl.when(flag)
        def _():
            pltpu.make_async_copy(source, target, sem).start()

        @pl.when(jnp.logical_not(flag))
        def _():
            pltpu.make_async_copy(other, target, sem).start()

        return pltpu.make_async_copy(source, target, sem)


def store_in(field):
    def store(r, t, c, count, value):
        field[r, t, pl.ds(PAD + c, count), :] = value

    return store


def store_out(ref):
    def store(r, t, c, count, value):
        ref[r, pl.ds(c - REACH, count), pl.ds(t * LANES, LANES)] = value.astype(jnp.bfloat16)

    return store


class OwnRows:
    def __init__(self, polar, lon, ext, state_ref, edge_w_ref, edge_e_ref, parts, field, base, first, sems, started=False):
        tiles, count = field.shape[1], HALO * len(parts)
        self.polar, self.edges = polar, (edge_w_ref, edge_e_ref)
        self.place = (field, base, first, count, lon)
        self.smooth, self.plain = [], []
        for i, (ref, start) in enumerate(parts):
            target = field.at[pl.ds(base + i * HALO, HALO), :, pl.ds(PAD, ext), :]
            self.smooth.append(pltpu.make_async_copy(ref.at[pl.ds(start, HALO)], target, sems.at[i]))
        for t in range(tiles):
            self.plain.append(pltpu.make_async_copy(
                state_ref.at[pl.ds(first, count), :, pl.ds(t * LANES, LANES)],
                field.at[pl.ds(base, count), t, pl.ds(PAD + REACH, lon), :], sems.at[t]))
        if not started:
            self.each(lambda copy: copy.start())

    def each(self, act):
        @pl.when(self.polar)
        def _():
            for copy in self.smooth:
                act(copy)

        @pl.when(jnp.logical_not(self.polar))
        def _():
            for copy in self.plain:
                act(copy)

    def wait(self):
        field, base, first, count, lon = self.place
        edge_w_ref, edge_e_ref = self.edges

        @pl.when(jnp.logical_not(self.polar))
        def _():
            @pl.loop(0, count)
            def _(r):
                for t in range(field.shape[1]):
                    lanes = pl.ds(t * LANES, LANES)
                    field[base + r, t, pl.ds(PAD, REACH), :] = edge_w_ref[first + r, :, lanes].astype(jnp.float32)
                    field[base + r, t, pl.ds(PAD + REACH + lon, REACH), :] = edge_e_ref[first + r, :, lanes].astype(jnp.float32)

        self.each(lambda copy: copy.wait())


def strip(field, base, ext):
    return field.at[pl.ds(base, HALO), :, pl.ds(PAD, ext), :]


def winds_beyond(copies, is_late, late_ref, raw_ref, winds, row):
    def part(ref, i):
        return ref.at[HALO, :, pl.ds(i * LANES, LANES)]

    return [copies.either(is_late, part(late_ref, i), part(raw_ref, i), winds.at[row + i]) for i in range(2)]


def on_side(info_ref, outer, body):
    @pl.when(info_ref[LOW_HALF] == 1)
    def _():
        body(not outer)

    @pl.when(info_ref[LOW_HALF] == 0)
    def _():
        body(outer)


def border_kernel(outer, rows, lon, ext, info_ref, state_ref, edge_w_ref, edge_e_ref, winds_ref, raw_ref, late_ref,
                  near_ref, far_ref, border_ref, level_ref, one_ref, field_a, field_b, halo_rows, winds, own_sem, sems):
    zero = info_ref[ZERO]
    is_late = info_ref[OUTER_LATE if outer else INNER_LATE] == 1

    def store_both(r, t, c, count, value):
        level_ref[r, t, pl.ds(c, count), :] = value
        border_ref[r, pl.ds(c, count), pl.ds(t * LANES, LANES)] = value.astype(jnp.bfloat16)

    def body(north):
        halo, own, first = (2 * HALO, 0, rows - 2 * HALO) if north else (0, HALO, 0)
        parts = ((far_ref, 0), (near_ref, 0)) if north else ((near_ref, 0), (far_ref, 0))
        copies = Copies(sems)
        halo_copy = copies.either(is_late, late_ref.at[pl.ds(0, HALO)], raw_ref.at[pl.ds(0, HALO)], halo_rows)
        mine = OwnRows(info_ref[POLAR] == 1, lon, ext, state_ref, edge_w_ref, edge_e_ref, parts, field_a, own, first, own_sem)
        wind_copies = [
            copies.start(winds_ref.at[pl.ds(first + 2 if north else 0, HALO + 2)], winds.at[pl.ds(0 if north else 2, HALO + 2)]),
            *winds_beyond(copies, is_late, late_ref, raw_ref, winds, HALO + 2 if north else 0),
        ]
        halo_copy.wait()
        put_rows(field_a, halo_rows, halo, HALO, ext)
        mine.wait()
        for copy in wind_copies:
            copy.wait()

    def pass_on(north):
        pltpu.make_async_copy(strip(field_b, 0 if north else HALO, ext), one_ref, sems.at[4]).start()

    on_side(info_ref, outer, body)
    step_rows(field_a, winds, zero, 0, 2 * HALO, 0, 0, ext, store_in(field_b))
    on_side(info_ref, outer, pass_on)
    step_rows(field_b, winds, zero, 0, HALO, 2, 0, ext, store_both)
    pltpu.make_async_copy(strip(field_b, 0, ext), one_ref, sems.at[4]).wait()


def border_rows(outer, info, state, edges, winds, raw, late, near, far):
    rows, lon, channels = state.shape
    ext = winds.shape[1]
    tiles = channels // LANES
    vmem, hbm = pl.BlockSpec(memory_space=pltpu.VMEM), pl.BlockSpec(memory_space=pl.ANY)
    level = jax.ShapeDtypeStruct((HALO, tiles, ext, LANES), jnp.float32)
    return pl.pallas_call(
        functools.partial(border_kernel, outer, rows, lon, ext),
        in_specs=[pl.BlockSpec(memory_space=pltpu.SMEM), hbm, vmem, vmem] + [hbm] * 5,
        out_specs=[vmem, vmem, hbm],
        out_shape=[jax.ShapeDtypeStruct((HALO, ext, channels), jnp.bfloat16), level, level],
        scratch_shapes=[
            cells_of(3 * HALO, tiles, ext), cells_of(2 * HALO, tiles, ext),
            half_of(HALO, ext, channels), half_of(2 * HALO, ext, LANES),
            pltpu.SemaphoreType.DMA((2,)), pltpu.SemaphoreType.DMA((5,)),
        ],
        compiler_params=pltpu.CompilerParams(vmem_limit_bytes=20 * MIB),
        cost_estimate=pl.CostEstimate(flops=1000, bytes_accessed=1000, transcendentals=0),
        name="border_outer" if outer else "border_inner",
    )(info, state, *edges, winds, raw, late, near, far)


def interior_kernel(rows, lon, ext, info_ref, state_ref, edge_w_ref, edge_e_ref, winds_ref, level_o_ref, level_i_ref,
                    one_o_ref, one_i_ref, smooth_o_ref, smooth_i_ref, out_ref, third_o_ref, third_i_ref,
                    field_a, field_b, field_c, part_ref, winds, sem, in_sem, out_sem):
    inner = rows - 4
    zero, low_half = info_ref[ZERO], info_ref[LOW_HALF] == 1

    def start(south, north):
        OwnRows(info_ref[POLAR] == 1, lon, ext, state_ref, edge_w_ref, edge_e_ref,
                ((south[0], 0), (north[0], 0)), field_a, 0, HALO, sem)
        copies = Copies(in_sem)
        copies.start(winds_ref.at[pl.ds(2, inner)], winds)
        for one, two, at_one, at_two in ((south[1], south[2], 0, 0), (north[1], north[2], inner - HALO, rows - HALO)):
            copies.start(one, strip(field_b, at_one, ext))
            copies.start(two, strip(field_c, at_two, ext))

    outer_refs, inner_refs = (smooth_o_ref, one_o_ref, level_o_ref), (smooth_i_ref, one_i_ref, level_i_ref)

    @pl.when(low_half)
    def _():
        start(outer_refs, inner_refs)

    @pl.when(jnp.logical_not(low_half))
    def _():
        start(inner_refs, outer_refs)

    OwnRows(info_ref[POLAR] == 1, lon, ext, state_ref, edge_w_ref, edge_e_ref,
            ((smooth_o_ref, 0), (smooth_i_ref, 0)), field_a, 0, HALO, sem, started=True).wait()
    pltpu.make_async_copy(winds_ref.at[pl.ds(2, inner)], winds, in_sem.at[0]).wait()

    def store(r, t, c, count, value):
        field_b[HALO + r, t, pl.ds(PAD + c, count), :] = value

    step_rows(field_a, winds, zero, 0, inner - 2 * HALO, HALO, 0, ext, store)
    for i in range(4):
        pltpu.make_async_copy(one_o_ref, strip(field_b, 0, ext), in_sem.at[1 + i]).wait()

    def store(r, t, c, count, value):
        field_c[HALO + r, t, pl.ds(PAD + c, count), :] = value

    step_rows(field_b, winds, zero, 0, inner - 4, 2, 0, ext, store)
    step_rows(field_c, winds, zero, 0, inner, 0, 0, ext, store_in(field_b))

    def hand_on(south_ref, north_ref):
        for i, (ref, base) in enumerate(((south_ref, 0), (north_ref, inner - HALO))):
            pltpu.make_async_copy(strip(field_b, base, ext), ref, out_sem.at[i]).start()

    @pl.when(low_half)
    def _():
        hand_on(third_o_ref, third_i_ref)

    @pl.when(jnp.logical_not(low_half))
    def _():
        hand_on(third_i_ref, third_o_ref)

    step_rows(field_b, winds, zero, 0, inner - 4, 2, REACH, REACH + lon, store_out(part_ref))
    copy = pltpu.make_async_copy(part_ref, out_ref.at[pl.ds(HALO, rows - 2 * HALO)], out_sem.at[2])
    copy.start()
    for i in range(2):
        pltpu.make_async_copy(strip(field_b, 0, ext), third_o_ref, out_sem.at[i]).wait()
    copy.wait()


def interior(info, state, edges, winds, levels, ones, smooths):
    rows, lon, channels = state.shape
    ext = winds.shape[1]
    tiles = channels // LANES
    vmem, hbm = pl.BlockSpec(memory_space=pltpu.VMEM), pl.BlockSpec(memory_space=pl.ANY)
    third = jax.ShapeDtypeStruct((HALO, tiles, ext, LANES), jnp.float32)
    return pl.pallas_call(
        functools.partial(interior_kernel, rows, lon, ext),
        in_specs=[pl.BlockSpec(memory_space=pltpu.SMEM), hbm, vmem, vmem] + [hbm] * 7,
        out_specs=[hbm, hbm, hbm],
        out_shape=[jax.ShapeDtypeStruct((rows, lon, channels), jnp.bfloat16), third, third],
        scratch_shapes=[
            cells_of(rows - 2 * HALO, tiles, ext), cells_of(rows - 4, tiles, ext), cells_of(rows, tiles, ext),
            half_of(rows - 2 * HALO, lon, channels), half_of(rows - 4, ext, LANES),
            pltpu.SemaphoreType.DMA((2,)), pltpu.SemaphoreType.DMA((5,)), pltpu.SemaphoreType.DMA((3,)),
        ],
        compiler_params=pltpu.CompilerParams(vmem_limit_bytes=24 * MIB),
        cost_estimate=pl.CostEstimate(flops=1000, bytes_accessed=1000, transcendentals=0),
        name="interior",
    )(info, state, *edges, winds, *levels, *ones, *smooths)


def finish_kernel(outer, rows, lon, ext, _, info_ref, winds_ref, raw_ref, late_ref, border_ref, across_ref, level_ref, third_ref,
                  out_ref, near, last, winds, halo_rows, part_ref, in_sem, out_sem):
    zero = info_ref[ZERO]

    def body(north):
        mine, other = (0, HALO) if north else (HALO, 0)
        copies = Copies(in_sem)
        halo_copy = copies.either(info_ref[MIDDLE] == 1, across_ref, border_ref, halo_rows)
        incoming = [
            copies.start(level_ref, strip(near, mine, ext)),
            copies.start(third_ref, strip(last, mine, ext)),
            copies.start(winds_ref.at[pl.ds(rows - HALO if north else 0, HALO)], winds.at[pl.ds(0 if north else 2, HALO)]),
            *winds_beyond(copies, info_ref[OUTER_LATE if outer else INNER_LATE] == 1, late_ref, raw_ref, winds, HALO if north else 0),
        ]
        halo_copy.wait()
        put_rows(near, halo_rows, other, HALO, ext)
        for copy in incoming:
            copy.wait()

        def store(r, t, c, count, value):
            last[r + other, t, pl.ds(PAD + c, count), :] = value

        step_rows(near, winds, zero, 0, HALO, 2 if north else 0, 0, ext, store)
        step_rows(last, winds, zero, 0, HALO, 0 if north else 2, REACH, REACH + lon, store_out(part_ref))
        copy = pltpu.make_async_copy(part_ref, out_ref.at[pl.ds(rows - HALO if north else 0, HALO)], out_sem.at[0])
        copy.start()
        copy.wait()

    on_side(info_ref, outer, body)


def finish(outer, info, out, winds, raw, late, border, across, level, third):
    rows, lon, channels = out.shape
    ext = winds.shape[1]
    tiles = channels // LANES
    hbm = pl.BlockSpec(memory_space=pl.ANY)
    return pl.pallas_call(
        functools.partial(finish_kernel, outer, rows, lon, ext),
        in_specs=[hbm, pl.BlockSpec(memory_space=pltpu.SMEM)] + [hbm] * 7,
        out_specs=hbm,
        out_shape=jax.ShapeDtypeStruct(out.shape, out.dtype),
        input_output_aliases={0: 0},
        scratch_shapes=[
            cells_of(2 * HALO, tiles, ext), cells_of(2 * HALO, tiles, ext),
            half_of(HALO + 2, ext, LANES), half_of(HALO, ext, channels), half_of(HALO, lon, channels),
            pltpu.SemaphoreType.DMA((6,)),
            pltpu.SemaphoreType.DMA((1,)),
        ],
        compiler_params=pltpu.CompilerParams(vmem_limit_bytes=16 * MIB),
        cost_estimate=pl.CostEstimate(flops=1000, bytes_accessed=1000, transcendentals=0),
        name="finish_outer" if outer else "finish_inner",
    )(out, info, winds, raw, late, border, across, level, third)


def half_of(rows, ext, channels):
    return pltpu.VMEM((rows, ext, channels), jnp.bfloat16)


def cells_of(rows, tiles, ext):
    return pltpu.VMEM((rows, tiles, ext + 2 * PAD, LANES), jnp.float32)


def per_device(state, winds, decay, widths):
    rows, lon, channels = state.shape
    fields = decay.shape[0]
    bands, tiles = lax.axis_size("lat"), lax.axis_size("lon")
    lat, lon_at = lax.axis_index("lat"), lax.axis_index("lon")
    quarter = bands // 4
    ext = round_up(lon + 2 * REACH, 16)
    fill = ext - lon - 2 * REACH
    axes = ("lat", "lon")

    middle = bands // 2

    def is_polar(band):
        return band < quarter or band >= bands - quarter

    def is_plain(band):
        return not is_polar(band)

    def inward(band):
        return band + 1 if band < middle else band - 1

    def outward(band):
        return band - 1 if band < middle else band + 1

    def over_lon(flip):
        return [(b * tiles + l, b * tiles + (l ^ flip)) for b in range(bands) if is_polar(b) for l in range(tiles)]

    def over_lat(to, wanted=lambda band: True):
        return [(b * tiles + l, to(b) * tiles + l) for b in range(bands)
                if wanted(b) and 0 <= to(b) < bands and (to(b) < middle) == (b < middle) for l in range(tiles)]

    across = [(b * tiles + l, inward(b) * tiles + l) for b in (middle - 1, middle) for l in range(tiles)]

    def move(cells, pairs):
        return lax.ppermute(cells, axes, pairs)

    low_half = lat < middle
    at_middle = (lat == middle - 1) | (lat == middle)
    polar = (lat < quarter) | (lat >= bands - quarter)
    outer_late = (lat <= quarter) | (lat >= bands - quarter - 1)
    inner_late = (lat < quarter - 1) | (lat > bands - quarter)
    info = jnp.stack([lon_at % 2, polar, outer_late, inner_late, lat < 0, low_half, at_middle]).astype(jnp.int32)

    count = HALO
    starts = [jnp.where(low_half, f, rows - count - f) for f in (0, rows - count, count, rows - 2 * count)]

    def rows_of(values, i):
        return lax.dynamic_slice_in_dim(values, starts[i], count)

    def ordered(values):
        return jnp.concatenate([rows_of(values, i) for i in range(len(starts))], axis=0)

    def joined(cols):
        return jnp.concatenate([state[:, cols].astype(jnp.bfloat16), winds[:, cols]], axis=2)

    east = [(l, (l + 1) % tiles) for l in range(tiles)]
    west = [((l + 1) % tiles, l) for l in range(tiles)]
    head, rear, cells = tie(joined(slice(0, REACH)), joined(slice(lon - REACH, lon)), state)
    from_east = lax.ppermute(head, "lon", west)
    from_west = lax.ppermute(rear, "lon", east)

    opp = [None] * len(starts)
    circles = [rows_of(cells, 0).astype(jnp.bfloat16)]
    circles[0], cells = tie(circles[0], cells)
    opp[0] = move(circles[0], over_lon(2))
    circles += [rows_of(cells, i).astype(jnp.bfloat16) for i in range(1, len(starts))]

    edge_w, edge_e = from_west[:, :, :channels], from_east[:, :, :channels]

    def extend(inner, before, after):
        parts = [before, inner, after, jnp.zeros((inner.shape[0], fill, inner.shape[2]), inner.dtype)]
        return jnp.concatenate(parts, axis=1)

    winds_ext = extend(winds, from_west[:, :, channels:], from_east[:, :, channels:])

    def border(i, wind_first):
        wind = lax.dynamic_slice_in_dim(winds_ext, wind_first, 2)
        ends = extend(rows_of(cells, i).astype(jnp.bfloat16), rows_of(edge_w, i), rows_of(edge_e, i))
        return jnp.concatenate([ends, jnp.concatenate([wind[:1], wind[1:]], axis=2)], axis=0)

    outer_rows = border(0, jnp.where(low_half, 0, rows - 2))
    inner_rows = border(1, jnp.where(low_half, rows - 2, 0))
    raw_out = move(outer_rows, over_lat(outward, is_plain))
    raw_in = move(inner_rows, over_lat(inward, is_plain))
    raw_across = move(inner_rows, across)
    behind = outer_rows[HALO:], inner_rows[HALO:]

    circles[1], outer_rows = tie(circles[1], outer_rows)
    sib = [move(jnp.concatenate(circles[:2], axis=0), over_lon(1)), None]
    opp[1] = move(circles[1], over_lon(2))

    own_widths = ordered(lax.dynamic_slice_in_dim(widths, lat * rows, rows))
    rate = jnp.repeat(decay, channels // fields)[None, :]
    reach = own_widths.astype(jnp.float32)[:, None]
    q = jnp.exp(-rate)
    back = round_up(HMAX + 1 + REACH, 8)
    seg = max(back + ext - REACH, round_up(ext + HMAX + 1, 8)) // 8
    carry = jnp.exp(-rate * seg)
    far = jnp.exp(-rate * (reach + 1.0))[:, None, :]
    total = (-jnp.expm1(-rate * (reach + 1.0)) - q * jnp.expm1(-rate * reach)) / -jnp.expm1(-rate)
    scale = (1.0 / total)[:, None, :]

    edges = edge_w, edge_e
    smooths, late = [], []
    for i in range(len(starts)):
        if i == 1:
            opp[i], raw_out = tie(opp[i], raw_out)
        if i == 2:
            opp[i], late[0], raw_in = tie(opp[i], late[0], raw_in)
        if i == 3:
            opp[i], late[1] = tie(opp[i], late[1])
        if i + 2 < len(starts):
            opp[i], circles[i + 2] = tie(opp[i], circles[i + 2])
            opp[i + 2] = move(circles[i + 2], over_lon(2))
        diag = move(opp[i], over_lon(1))
        if i == 1:
            sib[1] = move(jnp.concatenate(circles[2:], axis=0), over_lon(1))
        smooth, *ends = smooth_piece(i, count, ext, info, own_widths, circles[i], sib[i // 2], opp[i], diag,
                                     q, carry, far, scale, behind[i:i + 1])
        smooths.append(smooth)
        if i + 1 < len(starts):
            smooth, opp[i + 1] = tie(smooth, opp[i + 1])
        if ends:
            late.append(move(ends[0], over_lat((outward, inward)[i], is_polar)))
        if i == 2:
            outer_rows, level_o, one_o = border_rows(
                True, info, state, edges, winds_ext, raw_in, late[1], smooths[0], smooths[2])
            going_out = move(outer_rows, over_lat(outward))

    raw_inner = jnp.where(at_middle, raw_across, raw_out)
    inner_rows, level_i, one_i = border_rows(
        False, info, state, edges, winds_ext, raw_inner, late[0], smooths[1], smooths[3])
    going_in = move(inner_rows, over_lat(inward))
    going_across = move(inner_rows, across)
    out, third_o, third_i = interior(info, state, edges, winds_ext, (level_o, level_i), (one_o, one_i), smooths[2:])
    out = finish(False, info, out, winds_ext, raw_inner, late[0], going_out, going_across, level_i, third_i)
    return finish(True, info, out, winds_ext, raw_in, late[1], going_in, going_in, level_o, third_o)


def solution(mesh):
    in_specs = (P("lat", "lon", None), P("lat", "lon", None), P(), P())
    out_specs = P("lat", "lon", None)
    return jax.shard_map(
        per_device, mesh=mesh, in_specs=in_specs, out_specs=out_specs, check_vma=False
    )
```

time: 193 us -> 151 us (0.78)
  Pallas kernels: 62.2 us -> 43.1 us
  starting transfers between devices: 48.6 us -> 36.3 us
  other arithmetic: 21.2 us -> 9 us
  waiting for transfers between devices: 42.9 us -> 51.6 us
  local copies, waits for them, and re-layouts: 15.1 us -> 8.04 us
    ppermute x13 -> x18, starting transfers between devices: 47.8 us -> 35.5 us  [move(): return lax.ppermute(cells, axes, pairs)]
    pallas_call x4, Pallas kernels: 33.5 us -> 23.1 us  [the longest x2 12.5 us: border_rows(): pl.pallas_call(functools.partial(border_kernel, outer, rows, lon, ext), i...]
    concatenate x9 -> x5, other arithmetic: 14.2 us -> 5.14 us  [the longest x1 2.38 us: per_device(): sib = [move(jnp.concatenate(circles[:2], axis=0), over_lon(1)), None]]
    ppermute x13 -> x18, waiting for transfers between devices: 42.9 us -> 51.6 us  [move(): return lax.ppermute(cells, axes, pairs)]
    pallas_call x3 -> x4, Pallas kernels: 11.3 us -> 4.04 us  [smooth_piece(): pl.pallas_call(functools.partial(smooth_kernel, geo, len(extras)), grid=(...]
    unnamed x64 -> x16, local copies, waits for them, and re-layouts: 6.62 us -> 0.04 us
    convert_element_type x0 -> x2, local copies, waits for them, and re-layouts: none -> 6.33 us  [the longest x1 4 us: per_device(): rows_of(cells, i).astype(jnp.bfloat16)]
    slice x10 -> x1, local copies, waits for them, and re-layouts: 4.05 us -> 0.04 us  [border(): wind[:1]]
  transfers between devices with their start and end apart: 15 -> 20, of which waited for: 3 -> 5; matrix products, arithmetic and copies ran while one was open for 13% -> 9% of each run, Pallas kernels for 29% -> 25%
where the time goes in v2:
time: 151 us; the launch traced here: 149 us
  waiting for transfers between devices  51.6 us (34%)
  Pallas kernels  43.1 us (29%)
  starting transfers between devices  36.3 us (24%)
  other arithmetic  9 us (6%)
  local copies, waits for them, and re-layouts  8.04 us (5%)
    ppermute x18, waiting for transfers between devices, move(): return lax.ppermute(cells, axes, pairs)  51.6 us
    ppermute x18, starting transfers between devices, move(): return lax.ppermute(cells, axes, pairs)  35.5 us
    pallas_call x1, Pallas kernels, interior(): pl.pallas_call(functools.partial(interior_kernel, rows, lon, ext), in_spe...  16 us
    pallas_call x2, Pallas kernels, border_rows(): pl.pallas_call(functools.partial(border_kernel, outer, rows, lon, ext), i...  12.5 us
    pallas_call x2, Pallas kernels, finish(): pl.pallas_call(functools.partial(finish_kernel, outer, rows, lon, ext), i...  10.6 us
    pallas_call x4, Pallas kernels, smooth_piece(): pl.pallas_call(functools.partial(smooth_kernel, geo, len(extras)), grid=(...  4.04 us
    convert_element_type x1, local copies, waits for them, and re-layouts, per_device(): rows_of(cells, i).astype(jnp.bfloat16)  4 us
  transfers between devices with their start and end apart: 20, of which 5 were waited for; matrix products, arithmetic and copies ran while one was open for 9% of the time, Pallas kernels for 25%

profile of v2, /device:TPU:21, one launch (start us, length us, event | category | flops | bytes accessed | tf_op | source)
XLA Modules:
  0.0 148.8 jit_solution(15938140663734686208)
XLA Ops:
  0.0 3.0 %convert.10 = bf16[16,360,256]{2,1,0:T(8,128)(2,1)S(1)} convert(f32[16,360,256]{2,1,0:T(8,128)} %state_ref.5) | non-fusion elementwise | flops 1474560 | bytes 8847360 | tf_op jit(solution)/shard_map/convert.7
  4.6 2.3 %dynamic-slice_convert_fusion.4.refs_0_ = bf16[4,360,256]{2,1,0:T(8,128)(2,1)} fusion(f32[16,360,256]{2,1,0:T(8,128)} %state_ref.5, s32[]{:T(128)S(6)} %select_n.68), kind=kLoop, calls=%fused_computation.7 | loop fusion | bytes 1474564 | tf_op jit(solution)/shard_map/convert_element_type | solution.py:560
  7.0 1.5 %collective-permute-start.3 = (bf16[4,360,256]{2,1,0:T(8,128)(2,1)}, bf16[4,360,256]{2,1,0:T(8,128)(2,1)}, u32[]{:S(2)}, u32[]{:S(2)}) collective-permute-start(bf16[4,360,256]{2,1,0:T(8,128)(2,1)} %dynamic-slice_convert_fusion.4.refs_0_), channel_id=1, source_target_pairs={{0,2},{1,3},{2,0},{3,1},{4,6},{5,7},{6,4},{7,5},{24,26},{25,27},{2... | collective-permute-start | bytes 2211848 | tf_op jit(solution)/shard_map/ppermute | solution.py:532
  8.7 4.0 %dynamic-slice_convert_fusion = (bf16[4,360,256]{2,1,0:T(8,128)(2,1)S(1)}, bf16[4,360,256]{2,1,0:T(8,128)(2,1)}, bf16[4,360,256]{2,1,0:T(8,128)(2,1)S(1)}, bf16[4,360,256]{2,1,0:T(8,128)(2,1)S(1)}) fusion(f32[16,360,256]{2,1,0:T(8,128)} %state_ref.5, s32[]{:T(128)S(6)} %select_n.73, s32[]{:T(128)S(6)} %select_n.71, s32[]{:T(128)S(6)} %select_n.68, ...), kind=kLoop, calls=%fused_computation.3 | loop fusion | bytes 5898256 | tf_op jit(solution)/shard_map/convert_element_type | solution.py:563
  13.3 1.7 %maximum_maximum_fusion.2 = (bf16[5,384,256]{2,1,0:T(8,128)(2,1)}, bf16[5,384,256]{2,1,0:T(8,128)(2,1)}) fusion(bf16[1,384,128]{2,1,0:T(8,128)(2,1)S(1)} %get-tuple-element.81, bf16[1,384,128]{2,1,0:T(8,128)(2,1)S(1)} %get-tuple-element.79, bf16[4,8,256]{2,1,0:T(8,128)(2,1)S(1)} %get-tuple-element.87, bf16[4,360,256]{2,1,0:T(8,128)(2,1)S(1)} %get-tuple-element.42.refs_0_, ...), kind=kLoop, calls=%fused_computation.9 | loop fusion | flops 11304960 | bytes 3903232 | tf_op jit(solution)/shard_map/concatenate | solution.py:576
  15.0 2.4 %pad_maximum_fusion = bf16[8,360,256]{2,1,0:T(8,128)(2,1)} fusion(bf16[4,360,256]{2,1,0:T(8,128)(2,1)S(1)} %get-tuple-element.42.refs_0_, bf16[4,360,256]{2,1,0:T(8,128)(2,1)} %dynamic-slice_convert_fusion.4.refs_0_), kind=kLoop, calls=%fused_computation.1 | loop fusion | flops 737280 | bytes 2949120 | tf_op jit(solution)/shard_map/concatenate | solution.py:586
  17.4 1.8 %collective-permute-start.2 = (bf16[8,360,256]{2,1,0:T(8,128)(2,1)}, bf16[8,360,256]{2,1,0:T(8,128)(2,1)}, u32[]{:S(2)}, u32[]{:S(2)}) collective-permute-start(bf16[8,360,256]{2,1,0:T(8,128)(2,1)} %pad_maximum_fusion), channel_id=1, source_target_pairs={{0,1},{1,0},{2,3},{3,2},{4,5},{5,4},{6,7},{7,6},{24,25},{25,24},{2... | collective-permute-start | bytes 4423688 | tf_op jit(solution)/shard_map/ppermute | solution.py:532
  19.2 4.1 %collective-permute-start.6 = (bf16[5,384,256]{2,1,0:T(8,128)(2,1)}, bf16[5,384,256]{2,1,0:T(8,128)(2,1)}, u32[]{:S(2)}, u32[]{:S(2)}) collective-permute-start(bf16[5,384,256]{2,1,0:T(8,128)(2,1)} %get-tuple-element.90), channel_id=1, source_target_pairs={{8,4},{9,5},{10,6},{11,7},{12,8},{13,9},{14,10},{15,11},{16,20},{1... | collective-permute-start | bytes 2949128 | tf_op jit(solution)/shard_map/ppermute | solution.py:532
  25.6 1.3 collective-permute-start.10
  27.9 1.6 %smooth.4 = (f32[4,2,384,128]{3,2,1,0:T(8,128)S(1)}, bf16[5,384,256]{2,1,0:T(8,128)(2,1)S(1)}) custom-call(s32[7]{0:T(128)S(1)} %stack.55.info_ref, s32[4]{0:T(128)S(1)} %get-tuple-element.96.widths_ref, bf16[4,360,256]{2,1,0:T(8,128)(2,1)} %dynamic-slice_convert_fusion.4.refs_0_, bf16[8,360,256]{2,1,0:T(8,128)(2,1)} %collective-permute-done.2.refs_1_, ...), custom_call_target="tpu_custom_call" | custom-call | flops 1000 | bytes 1000 | tf_op jit(solution)/shard_map/smooth/pallas_call | solution.py:136
  30.3 11.8 %collective-permute-done.6 = bf16[5,384,256]{2,1,0:T(8,128)(2,1)} collective-permute-done((bf16[5,384,256]{2,1,0:T(8,128)(2,1)}, bf16[5,384,256]{2,1,0:T(8,128)(2,1)}, u32[]{:S(2)}, u32[]{:S(2)}) %collective-permute-start.6) | collective-permute-done | bytes 983072 | tf_op jit(solution)/shard_map/ppermute | solution.py:532
  46.6 4.3 %collective-permute-done.10.raw_ref = bf16[5,384,256]{2,1,0:T(8,128)(2,1)S(1)} collective-permute-done((bf16[5,384,256]{2,1,0:T(8,128)(2,1)}, bf16[5,384,256]{2,1,0:T(8,128)(2,1)S(1)}, u32[]{:S(2)}, u32[]{:S(2)}) %collective-permute-start.10) | collective-permute-done | bytes 983072 | tf_op jit(solution)/shard_map/ppermute | solution.py:532
  52.4 1.9 %collective-permute-start.14 = (bf16[5,384,256]{2,1,0:T(8,128)(2,1)S(1)}, bf16[5,384,256]{2,1,0:T(8,128)(2,1)S(1)}, u32[]{:S(2)}, u32[]{:S(2)}) collective-permute-start(bf16[5,384,256]{2,1,0:T(8,128)(2,1)S(1)} %copy-done.2), channel_id=1, source_target_pairs={{12,16},{13,17},{14,18},{15,19},{16,12},{17,13},{18,14},{19,15}} | collective-permute-start | bytes 2949128 | tf_op jit(solution)/shard_map/ppermute | solution.py:532
  55.6 20.9 %collective-permute-done.14 = bf16[5,384,256]{2,1,0:T(8,128)(2,1)S(1)} collective-permute-done((bf16[5,384,256]{2,1,0:T(8,128)(2,1)S(1)}, bf16[5,384,256]{2,1,0:T(8,128)(2,1)S(1)}, u32[]{:S(2)}, u32[]{:S(2)}) %collective-permute-start.14) | collective-permute-done | bytes 983072 | tf_op jit(solution)/shard_map/ppermute | solution.py:532
  76.7 6.3 %border_outer.1 = (bf16[4,384,256]{2,1,0:T(8,128)(2,1)S(1)}, f32[4,2,384,128]{3,2,1,0:T(8,128)S(1)}, f32[4,2,384,128]{3,2,1,0:T(8,128)S(1)}) custom-call(s32[7]{0:T(128)S(1)} %stack.55.info_ref, f32[16,360,256]{2,1,0:T(8,128)S(1)} %bitcast.8, bf16[16,8,256]{2,1,0:T(8,128)(2,1)S(1)} %slice.52.edge_w_ref, bf16[16,8,256]{2,1,0:T(8,128)(2,1)S(1)} %slice.53.edge_e_ref, ...), custom_call_target="tpu_custom_call" | custom-call | flops 1000 | bytes 1000 | tf_op jit(solution)/shard_map/border_outer/pallas_call | solution.py:336
  82.9 14.4 %collective-permute-start.17 = (bf16[4,384,256]{2,1,0:T(8,128)(2,1)S(1)}, bf16[4,384,256]{2,1,0:T(8,128)(2,1)S(1)}, u32[]{:S(2)}, u32[]{:S(2)}) collective-permute-start(bf16[4,384,256]{2,1,0:T(8,128)(2,1)S(1)} %get-tuple-element.66), channel_id=1, source_target_pairs={{4,0},{5,1},{6,2},{7,3},{8,4},{9,5},{10,6},{11,7},{12,8},{13,9},{1... | collective-permute-start | bytes 2359304 | tf_op jit(solution)/shard_map/ppermute | solution.py:532
  97.9 6.3 %border_inner.1 = (bf16[4,384,256]{2,1,0:T(8,128)(2,1)S(1)}, f32[4,2,384,128]{3,2,1,0:T(8,128)S(1)}, f32[4,2,384,128]{3,2,1,0:T(8,128)S(1)}) custom-call(s32[7]{0:T(128)S(1)} %stack.55.info_ref, f32[16,360,256]{2,1,0:T(8,128)S(1)} %bitcast.8, bf16[16,8,256]{2,1,0:T(8,128)(2,1)S(1)} %slice.52.edge_w_ref, bf16[16,8,256]{2,1,0:T(8,128)(2,1)S(1)} %slice.53.edge_e_ref, ...), custom_call_target="tpu_custom_call" | custom-call | flops 1000 | bytes 1000 | tf_op jit(solution)/shard_map/border_inner/pallas_call | solution.py:336
  104.2 1.9 %collective-permute-start.18 = (bf16[4,384,256]{2,1,0:T(8,128)(2,1)S(1)}, bf16[4,384,256]{2,1,0:T(8,128)(2,1)S(1)}, u32[]{:S(2)}, u32[]{:S(2)}) collective-permute-start(bf16[4,384,256]{2,1,0:T(8,128)(2,1)S(1)} %get-tuple-element.67), channel_id=1, source_target_pairs={{12,16},{13,17},{14,18},{15,19},{16,12},{17,13},{18,14},{19,15}} | collective-permute-start | bytes 2359304 | tf_op jit(solution)/shard_map/ppermute | solution.py:532
  106.1 1.3 collective-permute-start.19
  107.4 16.0 %interior.1 = (bf16[16,360,256]{2,1,0:T(8,128)(2,1)}, f32[4,2,384,128]{3,2,1,0:T(8,128)S(1)}, f32[4,2,384,128]{3,2,1,0:T(8,128)S(1)}) custom-call(s32[7]{0:T(128)S(1)} %stack.55.info_ref, f32[16,360,256]{2,1,0:T(8,128)S(1)} %bitcast.8, bf16[16,8,256]{2,1,0:T(8,128)(2,1)S(1)} %slice.52.edge_w_ref, bf16[16,8,256]{2,1,0:T(8,128)(2,1)S(1)} %slice.53.edge_e_ref, ...), custom_call_target="tpu_custom_call" | custom-call | flops 1000 | bytes 1000 | tf_op jit(solution)/shard_map/interior/pallas_call | solution.py:420
  123.4 1.7 %collective-permute-done.18.across_ref = bf16[4,384,256]{2,1,0:T(8,128)(2,1)S(1)} collective-permute-done((bf16[4,384,256]{2,1,0:T(8,128)(2,1)S(1)}, bf16[4,384,256]{2,1,0:T(8,128)(2,1)S(1)}, u32[]{:S(2)}, u32[]{:S(2)}) %collective-permute-start.18) | collective-permute-done | bytes 786464 | tf_op jit(solution)/shard_map/ppermute | solution.py:532
  125.0 5.3 %finish_inner.1._ = bf16[16,360,256]{2,1,0:T(8,128)(2,1)} custom-call(bf16[16,360,256]{2,1,0:T(8,128)(2,1)} %get-tuple-element.65._, s32[7]{0:T(128)S(1)} %stack.55.info_ref, bf16[16,384,128]{2,1,0:T(8,128)(2,1)S(1)} %maximum_maximum_fusion.winds_ref, bf16[5,384,256]{2,1,0:T(8,128)(2,1)S(1)} %broadcast_select_fusion.raw_ref, ...), custom_call_target="tpu_custom_call", output_to_operand_aliasing={{}: (0, {})} | custom-call | flops 1000 | bytes 1000 | tf_op jit(solution)/shard_map/finish_inner/pallas_call | solution.py:472
  130.4 13.0 %collective-permute-done.19.border_ref.across_ref = bf16[4,384,256]{2,1,0:T(8,128)(2,1)S(1)} collective-permute-done((bf16[4,384,256]{2,1,0:T(8,128)(2,1)S(1)}, bf16[4,384,256]{2,1,0:T(8,128)(2,1)S(1)}, u32[]{:S(2)}, u32[]{:S(2)}) %collective-permute-start.19) | collective-permute-done | bytes 786464 | tf_op jit(solution)/shard_map/ppermute | solution.py:532
  143.3 5.3 %finish_outer.1 = bf16[16,360,256]{2,1,0:T(8,128)(2,1)} custom-call(bf16[16,360,256]{2,1,0:T(8,128)(2,1)} %finish_inner.1._, s32[7]{0:T(128)S(1)} %stack.55.info_ref, bf16[16,384,128]{2,1,0:T(8,128)(2,1)S(1)} %maximum_maximum_fusion.winds_ref, bf16[5,384,256]{2,1,0:T(8,128)(2,1)S(1)} %collective-permute-done.10.raw_ref, ...), custom_call_target="tpu_custom_call", output_to_operand_aliasing={{}: (0, {})} | custom-call | flops 1000 | bytes 1000 | tf_op jit(solution)/shard_map/finish_outer/pallas_call | solution.py:472
  (78 shorter events, 14.2 us)
Async XLA Ops:
  3.8 8.9 %collective-permute-start = (bf16[16,8,384]{2,1,0:T(8,128)(2,1)S(1)}, bf16[16,8,384]{2,1,0:T(8,128)(2,1)S(1)}, u32[]{:S(2)}, u32[]{:S(2)}) collective-permute-start(bf16[16,8,384]{2,1,0:T(8,128)(2,1)S(1)} %get-tuple-element.38), channel_id=1, source_target_pairs={{0,1},{1,2},{2,3},{3,0},{4,5},{5,6},{6,7},{7,4},{8,9},{9,10},{10,1... | collective-permute-start | bytes 294920 | tf_op jit(solution)/shard_map/ppermute | solution.py:557
  4.6 8.1 %collective-permute-start.1 = (bf16[16,8,384]{2,1,0:T(8,128)(2,1)S(1)}, bf16[16,8,384]{2,1,0:T(8,128)(2,1)S(1)}, u32[]{:S(2)}, u32[]{:S(2)}) collective-permute-start(bf16[16,8,384]{2,1,0:T(8,128)(2,1)S(1)} %get-tuple-element.39), channel_id=1, source_target_pairs={{1,0},{2,1},{3,2},{0,3},{5,4},{6,5},{7,6},{4,7},{9,8},{10,9},{11,1... | collective-permute-start | bytes 294920 | tf_op jit(solution)/shard_map/ppermute | solution.py:556
  7.0 17.6 %collective-permute-start.3 = (bf16[4,360,256]{2,1,0:T(8,128)(2,1)}, bf16[4,360,256]{2,1,0:T(8,128)(2,1)}, u32[]{:S(2)}, u32[]{:S(2)}) collective-permute-start(bf16[4,360,256]{2,1,0:T(8,128)(2,1)} %dynamic-slice_convert_fusion.4.refs_0_), channel_id=1, source_target_pairs={{0,2},{1,3},{2,0},{3,1},{4,6},{5,7},{6,4},{7,5},{24,26},{25,27},{2... | collective-permute-start | bytes 2211848 | tf_op jit(solution)/shard_map/ppermute | solution.py:532
  15.0 10.2 %copy-start.4 = (s32[128]{0:T(128)S(1)}, s32[128]{0:T(128)}, u32[]{:S(2)}) copy-start(s32[128]{0:T(128)} %param.7) | copy-start | bytes 1540
  17.4 10.5 %collective-permute-start.2 = (bf16[8,360,256]{2,1,0:T(8,128)(2,1)}, bf16[8,360,256]{2,1,0:T(8,128)(2,1)}, u32[]{:S(2)}, u32[]{:S(2)}) collective-permute-start(bf16[8,360,256]{2,1,0:T(8,128)(2,1)} %pad_maximum_fusion), channel_id=1, source_target_pairs={{0,1},{1,0},{2,3},{3,2},{4,5},{5,4},{6,7},{7,6},{24,25},{25,24},{2... | collective-permute-start | bytes 4423688 | tf_op jit(solution)/shard_map/ppermute | solution.py:532
  19.2 22.8 %collective-permute-start.6 = (bf16[5,384,256]{2,1,0:T(8,128)(2,1)}, bf16[5,384,256]{2,1,0:T(8,128)(2,1)}, u32[]{:S(2)}, u32[]{:S(2)}) collective-permute-start(bf16[5,384,256]{2,1,0:T(8,128)(2,1)} %get-tuple-element.90), channel_id=1, source_target_pairs={{8,4},{9,5},{10,6},{11,7},{12,8},{13,9},{14,10},{15,11},{16,20},{1... | collective-permute-start | bytes 2949128 | tf_op jit(solution)/shard_map/ppermute | solution.py:532
  23.8 5.7 %collective-permute-start.5 = (bf16[4,360,256]{2,1,0:T(8,128)(2,1)S(1)}, bf16[4,360,256]{2,1,0:T(8,128)(2,1)S(1)}, u32[]{:S(2)}, u32[]{:S(2)}) collective-permute-start(bf16[4,360,256]{2,1,0:T(8,128)(2,1)S(1)} %get-tuple-element.42.refs_0_), channel_id=1, source_target_pairs={{0,2},{1,3},{2,0},{3,1},{4,6},{5,7},{6,4},{7,5},{24,26},{25,27},{2... | collective-permute-start | bytes 2211848 | tf_op jit(solution)/shard_map/ppermute | solution.py:532
  24.6 3.3 %collective-permute-start.4 = (bf16[4,360,256]{2,1,0:T(8,128)(2,1)}, bf16[4,360,256]{2,1,0:T(8,128)(2,1)S(1)}, u32[]{:S(2)}, u32[]{:S(2)}) collective-permute-start(bf16[4,360,256]{2,1,0:T(8,128)(2,1)} %collective-permute-done.3.refs_2_), channel_id=1, source_target_pairs={{0,1},{1,0},{2,3},{3,2},{4,5},{5,4},{6,7},{7,6},{24,25},{25,24},{2... | collective-permute-start | bytes 2211848 | tf_op jit(solution)/shard_map/ppermute | solution.py:532
  25.6 25.3 %collective-permute-start.10 = (bf16[5,384,256]{2,1,0:T(8,128)(2,1)}, bf16[5,384,256]{2,1,0:T(8,128)(2,1)S(1)}, u32[]{:S(2)}, u32[]{:S(2)}) collective-permute-start(bf16[5,384,256]{2,1,0:T(8,128)(2,1)} %get-tuple-element.89), channel_id=1, source_target_pairs={{8,12},{9,13},{10,14},{11,15},{20,16},{21,17},{22,18},{23,19}} | collective-permute-start | bytes 2949128 | tf_op jit(solution)/shard_map/ppermute | solution.py:532
  27.9 14.9 %copy-start = (bf16[4,360,256]{2,1,0:T(8,128)(2,1)S(1)}, bf16[4,360,256]{2,1,0:T(8,128)(2,1)}, u32[]{:S(2)}) copy-start(bf16[4,360,256]{2,1,0:T(8,128)(2,1)} %get-tuple-element.50.refs_0_) | copy-start | bytes 2211844
  29.6 21.4 %collective-permute-start.9 = (bf16[5,384,256]{2,1,0:T(8,128)(2,1)S(1)}, bf16[5,384,256]{2,1,0:T(8,128)(2,1)S(1)}, u32[]{:S(2)}, u32[]{:S(2)}) collective-permute-start(bf16[5,384,256]{2,1,0:T(8,128)(2,1)S(1)} %get-tuple-element.52), channel_id=1, source_target_pairs={{4,0},{5,1},{6,2},{7,3},{24,28},{25,29},{26,30},{27,31}} | collective-permute-start | bytes 2949128 | tf_op jit(solution)/shard_map/ppermute | solution.py:532
  42.0 2.4 %collective-permute-start.7 = (bf16[4,360,256]{2,1,0:T(8,128)(2,1)S(1)}, bf16[4,360,256]{2,1,0:T(8,128)(2,1)S(1)}, u32[]{:S(2)}, u32[]{:S(2)}) collective-permute-start(bf16[4,360,256]{2,1,0:T(8,128)(2,1)S(1)} %collective-permute-done.5.refs_2_), channel_id=1, source_target_pairs={{0,1},{1,0},{2,3},{3,2},{4,5},{5,4},{6,7},{7,6},{24,25},{25,24},{2... | collective-permute-start | bytes 2211848 | tf_op jit(solution)/shard_map/ppermute | solution.py:532
  42.8 3.8 %collective-permute-start.8 = (bf16[4,360,256]{2,1,0:T(8,128)(2,1)S(1)}, bf16[4,360,256]{2,1,0:T(8,128)(2,1)S(1)}, u32[]{:S(2)}, u32[]{:S(2)}) collective-permute-start(bf16[4,360,256]{2,1,0:T(8,128)(2,1)S(1)} %copy-done), channel_id=1, source_target_pairs={{0,2},{1,3},{2,0},{3,1},{4,6},{5,7},{6,4},{7,5},{24,26},{25,27},{2... | collective-permute-start | bytes 2211848 | tf_op jit(solution)/shard_map/ppermute | solution.py:532
  43.6 10.7 %collective-permute-start.12 = (bf16[8,360,256]{2,1,0:T(8,128)(2,1)S(1)}, bf16[8,360,256]{2,1,0:T(8,128)(2,1)S(1)}, u32[]{:S(2)}, u32[]{:S(2)}) collective-permute-start(bf16[8,360,256]{2,1,0:T(8,128)(2,1)S(1)} %pad_maximum_fusion.1), channel_id=1, source_target_pairs={{0,1},{1,0},{2,3},{3,2},{4,5},{5,4},{6,7},{7,6},{24,25},{25,24},{2... | collective-permute-start | bytes 4423688 | tf_op jit(solution)/shard_map/ppermute | solution.py:532
  44.4 32.2 %slice-start = ((s8[5898240]{0:T(1024)(128)(4,1)}), s8[4194304]{0:T(1024)(128)(4,1)S(1)}, s32[]{:S(2)}) async-start(s8[5898240]{0:T(1024)(128)(4,1)} %bitcast.7), calls=%async_computation | async-start | bytes 8388608
  45.7 9.2 %collective-permute-start.11 = (bf16[5,384,256]{2,1,0:T(8,128)(2,1)S(1)}, bf16[5,384,256]{2,1,0:T(8,128)(2,1)S(1)}, u32[]{:S(2)}, u32[]{:S(2)}) collective-permute-start(bf16[5,384,256]{2,1,0:T(8,128)(2,1)S(1)} %get-tuple-element.54), channel_id=1, source_target_pairs={{0,4},{1,5},{2,6},{3,7},{4,8},{5,9},{6,10},{7,11},{24,20},{25,21},... | collective-permute-start | bytes 2949128 | tf_op jit(solution)/shard_map/ppermute | solution.py:532
  46.6 30.0 %slice-start.1 = ((s8[5898240]{0:T(1024)(128)(4,1)}), s8[1703936]{0:T(1024)(128)(4,1)S(1)}, s32[]{:S(2)}) async-start(s8[5898240]{0:T(1024)(128)(4,1)} %bitcast.7), calls=%async_computation.1 | async-start | bytes 3407872
  50.9 3.4 %collective-permute-start.13 = (bf16[4,360,256]{2,1,0:T(8,128)(2,1)S(1)}, bf16[4,360,256]{2,1,0:T(8,128)(2,1)S(1)}, u32[]{:S(2)}, u32[]{:S(2)}) collective-permute-start(bf16[4,360,256]{2,1,0:T(8,128)(2,1)S(1)} %collective-permute-done.8.refs_2_), channel_id=1, source_target_pairs={{0,1},{1,0},{2,3},{3,2},{4,5},{5,4},{6,7},{7,6},{24,25},{25,24},{2... | collective-permute-start | bytes 2211848 | tf_op jit(solution)/shard_map/ppermute | solution.py:532
  51.6 3.2 %collective-permute-start.15 = (bf16[4,360,256]{2,1,0:T(8,128)(2,1)S(1)}, bf16[4,360,256]{2,1,0:T(8,128)(2,1)S(1)}, u32[]{:S(2)}, u32[]{:S(2)}) collective-permute-start(bf16[4,360,256]{2,1,0:T(8,128)(2,1)S(1)} %get-tuple-element.55.refs_0_), channel_id=1, source_target_pairs={{0,2},{1,3},{2,0},{3,1},{4,6},{5,7},{6,4},{7,5},{24,26},{25,27},{2... | collective-permute-start | bytes 2211848 | tf_op jit(solution)/shard_map/ppermute | solution.py:532
  52.4 24.1 %collective-permute-start.14 = (bf16[5,384,256]{2,1,0:T(8,128)(2,1)S(1)}, bf16[5,384,256]{2,1,0:T(8,128)(2,1)S(1)}, u32[]{:S(2)}, u32[]{:S(2)}) collective-permute-start(bf16[5,384,256]{2,1,0:T(8,128)(2,1)S(1)} %copy-done.2), channel_id=1, source_target_pairs={{12,16},{13,17},{14,18},{15,19},{16,12},{17,13},{18,14},{19,15}} | collective-permute-start | bytes 2949128 | tf_op jit(solution)/shard_map/ppermute | solution.py:532
  54.9 42.4 %collective-permute-start.16 = (bf16[4,360,256]{2,1,0:T(8,128)(2,1)S(1)}, bf16[4,360,256]{2,1,0:T(8,128)(2,1)S(1)}, u32[]{:S(2)}, u32[]{:S(2)}) collective-permute-start(bf16[4,360,256]{2,1,0:T(8,128)(2,1)S(1)} %collective-permute-done.15.refs_2_), channel_id=1, source_target_pairs={{0,1},{1,0},{2,3},{3,2},{4,5},{5,4},{6,7},{7,6},{24,25},{25,24},{2... | collective-permute-start | bytes 2211848 | tf_op jit(solution)/shard_map/ppermute | solution.py:532
  82.9 40.4 %collective-permute-start.17 = (bf16[4,384,256]{2,1,0:T(8,128)(2,1)S(1)}, bf16[4,384,256]{2,1,0:T(8,128)(2,1)S(1)}, u32[]{:S(2)}, u32[]{:S(2)}) collective-permute-start(bf16[4,384,256]{2,1,0:T(8,128)(2,1)S(1)} %get-tuple-element.66), channel_id=1, source_target_pairs={{4,0},{5,1},{6,2},{7,3},{8,4},{9,5},{10,6},{11,7},{12,8},{13,9},{1... | collective-permute-start | bytes 2359304 | tf_op jit(solution)/shard_map/ppermute | solution.py:532
  104.2 20.9 %collective-permute-start.18 = (bf16[4,384,256]{2,1,0:T(8,128)(2,1)S(1)}, bf16[4,384,256]{2,1,0:T(8,128)(2,1)S(1)}, u32[]{:S(2)}, u32[]{:S(2)}) collective-permute-start(bf16[4,384,256]{2,1,0:T(8,128)(2,1)S(1)} %get-tuple-element.67), channel_id=1, source_target_pairs={{12,16},{13,17},{14,18},{15,19},{16,12},{17,13},{18,14},{19,15}} | collective-permute-start | bytes 2359304 | tf_op jit(solution)/shard_map/ppermute | solution.py:532
  106.1 37.2 %collective-permute-start.19 = (bf16[4,384,256]{2,1,0:T(8,128)(2,1)S(1)}, bf16[4,384,256]{2,1,0:T(8,128)(2,1)S(1)}, u32[]{:S(2)}, u32[]{:S(2)}) collective-permute-start(bf16[4,384,256]{2,1,0:T(8,128)(2,1)S(1)} %get-tuple-element.67), channel_id=1, source_target_pairs={{0,4},{1,5},{2,6},{3,7},{4,8},{5,9},{6,10},{7,11},{8,12},{9,13},{1... | collective-permute-start | bytes 2359304 | tf_op jit(solution)/shard_map/ppermute | solution.py:532
  (4 other events, 22.0 us)

commit v3 on v2

--- a/solution.py
+++ b/solution.py
@@ -14,7 +14,7 @@
 HMAX = 480
 LANES = 128
 MIB = 1024 * 1024
-ODD, POLAR, OUTER_LATE, INNER_LATE, ZERO, LOW_HALF, MIDDLE = range(7)
+ODD, POLAR, OUTER_FROM, INNER_FROM, ZERO, LOW_HALF = range(6)
 PAD = 8
 COLS = 48
 
@@ -27,8 +27,10 @@
     return -(-value // unit) * unit
 
 
-def smooth_kernel(geo, sends, info_ref, widths_ref, *refs):
-    ins, extra_refs, outs, scratch = refs[:8], refs[8:8 + sends], refs[8 + sends:9 + 2 * sends], refs[9 + 2 * sends:]
+def smooth_kernel(geo, sends, info_ref, widths_ref, own_ref, sib_ref, opp_ref, *refs):
+    diag_ref, refs = refs[0], refs[1:]
+    ins, extra_refs, outs, scratch = refs[:4], refs[4:4 + sends], refs[4 + sends:5 + 2 * sends], refs[5 + 2 * sends:]
+    ins = (own_ref, sib_ref, opp_ref, diag_ref) + ins
 
     @pl.when(info_ref[POLAR] == 1)
     def _():
@@ -121,7 +123,7 @@
         one_row(r, border_refs[0] if border_refs else None, r)
 
 
-def smooth_piece(piece, rows, ext, info, widths, own, sib, opp, diag, q, carry, far, scale, extras):
+def smooth_piece(piece, place, rows, ext, info, widths, own, sib, opp, diag, q, carry, far, scale, extras):
     lon, channels = own.shape[1:]
     tiles = channels // LANES
     back = round_up(HMAX + 1 + REACH, 8)
@@ -129,14 +131,15 @@
     seg = max(back + ext - REACH, span) // 8
     geo = (lon, back, 8 * seg, seg, ext)
     smem, vmem = pl.BlockSpec(memory_space=pltpu.SMEM), pl.BlockSpec(memory_space=pltpu.VMEM)
-    part = pl.BlockSpec((rows, lon, channels), lambda i: (piece % 2, 0, 0))
+    pair = pl.BlockSpec((rows, lon, channels), lambda i: (piece % 2, 0, 0))
+    part = pl.BlockSpec((rows, lon, channels), lambda i: (place, 0, 0))
     table = pl.BlockSpec((rows, 1, channels), lambda i: (piece, 0, 0))
     border = jax.ShapeDtypeStruct((HALO + 1, ext, channels), jnp.bfloat16)
     of_rows = slice(piece * rows, (piece + 1) * rows)
     return pl.pallas_call(
         functools.partial(smooth_kernel, geo, len(extras)),
         grid=(1,),
-        in_specs=[smem, smem, vmem, part, vmem, vmem, vmem, vmem, table, table] + [vmem] * len(extras),
+        in_specs=[smem, smem, part, pair, part, part, vmem, vmem, table, table] + [vmem] * len(extras),
         out_specs=[vmem] * (1 + len(extras)),
         out_shape=[jax.ShapeDtypeStruct((rows, tiles, ext, LANES), jnp.float32)] + [border] * len(extras),
         scratch_shapes=[
@@ -199,19 +202,15 @@
         copy.start()
         return copy
 
-    def either(self, flag, source, other, target):
+    def one_of(self, choice, sources, target):
         sem = self.sems.at[self.used]
         self.used += 1
-
-        @pl.when(flag)
-        def _():
-            pltpu.make_async_copy(source, target, sem).start()
-
-        @pl.when(jnp.logical_not(flag))
-        def _():
-            pltpu.make_async_copy(other, target, sem).start()
-
-        return pltpu.make_async_copy(source, target, sem)
+        for i, source in enumerate(sources):
+            @pl.when(choice == i)
+            def _(source=source):
+                pltpu.make_async_copy(source, target, sem).start()
+
+        return pltpu.make_async_copy(sources[0], target, sem)
 
 
 def store_in(field):
@@ -275,11 +274,8 @@
     return field.at[pl.ds(base, HALO), :, pl.ds(PAD, ext), :]
 
 
-def winds_beyond(copies, is_late, late_ref, raw_ref, winds, row):
-    def part(ref, i):
-        return ref.at[HALO, :, pl.ds(i * LANES, LANES)]
-
-    return [copies.either(is_late, part(late_ref, i), part(raw_ref, i), winds.at[row + i]) for i in range(2)]
+def winds_beyond(copies, origin, refs, winds, row):
+    return [copies.one_of(origin, [ref.at[HALO, :, pl.ds(i * LANES, LANES)] for ref in refs], winds.at[row + i]) for i in range(2)]
 
 
 def on_side(info_ref, outer, body):
@@ -292,10 +288,10 @@
         body(outer)
 
 
-def border_kernel(outer, rows, lon, ext, info_ref, state_ref, edge_w_ref, edge_e_ref, winds_ref, raw_ref, late_ref,
+def border_kernel(outer, rows, lon, ext, info_ref, state_ref, edge_w_ref, edge_e_ref, winds_ref, late_ref, raw_ref, across_ref,
                   near_ref, far_ref, border_ref, level_ref, one_ref, field_a, field_b, halo_rows, winds, own_sem, sems):
     zero = info_ref[ZERO]
-    is_late = info_ref[OUTER_LATE if outer else INNER_LATE] == 1
+    origin, origins = info_ref[OUTER_FROM if outer else INNER_FROM], (late_ref, raw_ref, across_ref)
 
     def store_both(r, t, c, count, value):
         level_ref[r, t, pl.ds(c, count), :] = value
@@ -305,11 +301,11 @@
         halo, own, first = (2 * HALO, 0, rows - 2 * HALO) if north else (0, HALO, 0)
         parts = ((far_ref, 0), (near_ref, 0)) if north else ((near_ref, 0), (far_ref, 0))
         copies = Copies(sems)
-        halo_copy = copies.either(is_late, late_ref.at[pl.ds(0, HALO)], raw_ref.at[pl.ds(0, HALO)], halo_rows)
+        halo_copy = copies.one_of(origin, [ref.at[pl.ds(0, HALO)] for ref in origins], halo_rows)
         mine = OwnRows(info_ref[POLAR] == 1, lon, ext, state_ref, edge_w_ref, edge_e_ref, parts, field_a, own, first, own_sem)
         wind_copies = [
             copies.start(winds_ref.at[pl.ds(first + 2 if north else 0, HALO + 2)], winds.at[pl.ds(0 if north else 2, HALO + 2)]),
-            *winds_beyond(copies, is_late, late_ref, raw_ref, winds, HALO + 2 if north else 0),
+            *winds_beyond(copies, origin, origins, winds, HALO + 2 if north else 0),
         ]
         halo_copy.wait()
         put_rows(field_a, halo_rows, halo, HALO, ext)
@@ -327,7 +323,7 @@
     pltpu.make_async_copy(strip(field_b, 0, ext), one_ref, sems.at[4]).wait()
 
 
-def border_rows(outer, info, state, edges, winds, raw, late, near, far):
+def border_rows(outer, info, state, edges, winds, origins, near, far):
     rows, lon, channels = state.shape
     ext = winds.shape[1]
     tiles = channels // LANES
@@ -335,7 +331,7 @@
     level = jax.ShapeDtypeStruct((HALO, tiles, ext, LANES), jnp.float32)
     return pl.pallas_call(
         functools.partial(border_kernel, outer, rows, lon, ext),
-        in_specs=[pl.BlockSpec(memory_space=pltpu.SMEM), hbm, vmem, vmem] + [hbm] * 5,
+        in_specs=[pl.BlockSpec(memory_space=pltpu.SMEM), hbm, vmem, vmem] + [hbm] * 6,
         out_specs=[vmem, vmem, hbm],
         out_shape=[jax.ShapeDtypeStruct((HALO, ext, channels), jnp.bfloat16), level, level],
         scratch_shapes=[
@@ -346,7 +342,7 @@
         compiler_params=pltpu.CompilerParams(vmem_limit_bytes=20 * MIB),
         cost_estimate=pl.CostEstimate(flops=1000, bytes_accessed=1000, transcendentals=0),
         name="border_outer" if outer else "border_inner",
-    )(info, state, *edges, winds, raw, late, near, far)
+    )(info, state, *edges, winds, *origins, near, far)
 
 
 def interior_kernel(rows, lon, ext, info_ref, state_ref, edge_w_ref, edge_e_ref, winds_ref, level_o_ref, level_i_ref,
@@ -433,19 +429,20 @@
     )(info, state, *edges, winds, *levels, *ones, *smooths)
 
 
-def finish_kernel(outer, rows, lon, ext, _, info_ref, winds_ref, raw_ref, late_ref, border_ref, across_ref, level_ref, third_ref,
+def finish_kernel(outer, rows, lon, ext, _, info_ref, winds_ref, late_ref, raw_ref, across_raw_ref, border_ref, across_ref, level_ref, third_ref,
                   out_ref, near, last, winds, halo_rows, part_ref, in_sem, out_sem):
     zero = info_ref[ZERO]
 
     def body(north):
         mine, other = (0, HALO) if north else (HALO, 0)
         copies = Copies(in_sem)
-        halo_copy = copies.either(info_ref[MIDDLE] == 1, across_ref, border_ref, halo_rows)
+        origin = info_ref[OUTER_FROM if outer else INNER_FROM]
+        halo_copy = copies.one_of(origin, (border_ref, border_ref, across_ref), halo_rows)
         incoming = [
             copies.start(level_ref, strip(near, mine, ext)),
             copies.start(third_ref, strip(last, mine, ext)),
             copies.start(winds_ref.at[pl.ds(rows - HALO if north else 0, HALO)], winds.at[pl.ds(0 if north else 2, HALO)]),
-            *winds_beyond(copies, info_ref[OUTER_LATE if outer else INNER_LATE] == 1, late_ref, raw_ref, winds, HALO if north else 0),
+            *winds_beyond(copies, origin, (late_ref, raw_ref, across_raw_ref), winds, HALO if north else 0),
         ]
         halo_copy.wait()
         put_rows(near, halo_rows, other, HALO, ext)
@@ -464,14 +461,14 @@
     on_side(info_ref, outer, body)
 
 
-def finish(outer, info, out, winds, raw, late, border, across, level, third):
+def finish(outer, info, out, winds, origins, border, across, level, third):
     rows, lon, channels = out.shape
     ext = winds.shape[1]
     tiles = channels // LANES
     hbm = pl.BlockSpec(memory_space=pl.ANY)
     return pl.pallas_call(
         functools.partial(finish_kernel, outer, rows, lon, ext),
-        in_specs=[hbm, pl.BlockSpec(memory_space=pltpu.SMEM)] + [hbm] * 7,
+        in_specs=[hbm, pl.BlockSpec(memory_space=pltpu.SMEM)] + [hbm] * 8,
         out_specs=hbm,
         out_shape=jax.ShapeDtypeStruct(out.shape, out.dtype),
         input_output_aliases={0: 0},
@@ -484,7 +481,7 @@
         compiler_params=pltpu.CompilerParams(vmem_limit_bytes=16 * MIB),
         cost_estimate=pl.CostEstimate(flops=1000, bytes_accessed=1000, transcendentals=0),
         name="finish_outer" if outer else "finish_inner",
-    )(out, info, winds, raw, late, border, across, level, third)
+    )(out, info, winds, *origins, border, across, level, third)
 
 
 def half_of(rows, ext, channels):
@@ -534,9 +531,10 @@
     low_half = lat < middle
     at_middle = (lat == middle - 1) | (lat == middle)
     polar = (lat < quarter) | (lat >= bands - quarter)
-    outer_late = (lat <= quarter) | (lat >= bands - quarter - 1)
-    inner_late = (lat < quarter - 1) | (lat > bands - quarter)
-    info = jnp.stack([lon_at % 2, polar, outer_late, inner_late, lat < 0, low_half, at_middle]).astype(jnp.int32)
+    outer_from = jnp.where((lat <= quarter) | (lat >= bands - quarter - 1), 0, 1)
+    inner_from = jnp.where((lat < quarter - 1) | (lat > bands - quarter), 0, jnp.where(at_middle, 2, 1))
+    numbers = [lon_at % 2, polar, outer_from, inner_from, lat < 0, low_half]
+    info = jnp.stack([jnp.asarray(n, jnp.int32) for n in numbers])
 
     count = HALO
     starts = [jnp.where(low_half, f, rows - count - f) for f in (0, rows - count, count, rows - 2 * count)]
@@ -583,7 +581,7 @@
     behind = outer_rows[HALO:], inner_rows[HALO:]
 
     circles[1], outer_rows = tie(circles[1], outer_rows)
-    sib = [move(jnp.concatenate(circles[:2], axis=0), over_lon(1)), None]
+    sib = move(jnp.concatenate(circles[:2], axis=0), over_lon(1))
     opp[1] = move(circles[1], over_lon(2))
 
     own_widths = ordered(lax.dynamic_slice_in_dim(widths, lat * rows, rows))
@@ -599,39 +597,41 @@
 
     edges = edge_w, edge_e
     smooths, late = [], []
-    for i in range(len(starts)):
+
+    def smoothed(i, place, own, sib, opp, diag):
+        return smooth_piece(i, place, count, ext, info, own_widths, own, sib, opp, diag, q, carry, far, scale, behind[i:i + 1])
+
+    for i in range(2):
+        if i == 0:
+            opp[0], last_two = tie(opp[0], jnp.concatenate(circles[2:], axis=0))
+            last_opp = move(last_two, over_lon(2))
+        diag = move(opp[i], over_lon(1))
+        smooth, ends = smoothed(i, 0, circles[i], sib, opp[i], diag)
+        smooths.append(smooth)
         if i == 1:
-            opp[i], raw_out = tie(opp[i], raw_out)
-        if i == 2:
-            opp[i], late[0], raw_in = tie(opp[i], late[0], raw_in)
-        if i == 3:
-            opp[i], late[1] = tie(opp[i], late[1])
-        if i + 2 < len(starts):
-            opp[i], circles[i + 2] = tie(opp[i], circles[i + 2])
-            opp[i + 2] = move(circles[i + 2], over_lon(2))
-        diag = move(opp[i], over_lon(1))
-        if i == 1:
-            sib[1] = move(jnp.concatenate(circles[2:], axis=0), over_lon(1))
-        smooth, *ends = smooth_piece(i, count, ext, info, own_widths, circles[i], sib[i // 2], opp[i], diag,
-                                     q, carry, far, scale, behind[i:i + 1])
-        smooths.append(smooth)
-        if i + 1 < len(starts):
-            smooth, opp[i + 1] = tie(smooth, opp[i + 1])
-        if ends:
-            late.append(move(ends[0], over_lat((outward, inward)[i], is_polar)))
-        if i == 2:
-            outer_rows, level_o, one_o = border_rows(
-                True, info, state, edges, winds_ext, raw_in, late[1], smooths[0], smooths[2])
-            going_out = move(outer_rows, over_lat(outward))
-
-    raw_inner = jnp.where(at_middle, raw_across, raw_out)
+            ends, raw_out = tie(ends, raw_out)
+        late.append(move(ends, over_lat((outward, inward)[i], is_polar)))
+        if i == 0:
+            smooth, opp[1] = tie(smooth, opp[1])
+        else:
+            smooth, last_opp = tie(smooth, last_opp)
+
+    last_opp, late[0], late[1], raw_in = tie(last_opp, late[0], late[1], raw_in)
+    last_sib = move(last_two, over_lon(1))
+    diag = move(last_opp, over_lon(1))
+    smooths += smoothed(2, 0, last_two, last_sib, last_opp, diag)
+    outer_rows, level_o, one_o = border_rows(
+        True, info, state, edges, winds_ext, (late[1], raw_in, raw_in), smooths[0], smooths[2])
+    going_out = move(outer_rows, over_lat(outward))
+    smooths += smoothed(3, 1, last_two, last_sib, last_opp, diag)
+    inner_origins, outer_origins = (late[0], raw_out, raw_across), (late[1], raw_in, raw_in)
     inner_rows, level_i, one_i = border_rows(
-        False, info, state, edges, winds_ext, raw_inner, late[0], smooths[1], smooths[3])
+        False, info, state, edges, winds_ext, inner_origins, smooths[1], smooths[3])
     going_in = move(inner_rows, over_lat(inward))
     going_across = move(inner_rows, across)
     out, third_o, third_i = interior(info, state, edges, winds_ext, (level_o, level_i), (one_o, one_i), smooths[2:])
-    out = finish(False, info, out, winds_ext, raw_inner, late[0], going_out, going_across, level_i, third_i)
-    return finish(True, info, out, winds_ext, raw_in, late[1], going_in, going_in, level_o, third_o)
+    out = finish(False, info, out, winds_ext, inner_origins, going_out, going_across, level_i, third_i)
+    return finish(True, info, out, winds_ext, outer_origins, going_in, going_in, level_o, third_o)
 
 
 def solution(mesh):

time: 151 us -> 145 us (0.960)
  waiting for transfers between devices: 51.6 us -> 41.9 us
  starting transfers between devices: 36.3 us -> 42.9 us
    ppermute x18 -> x16, waiting for transfers between devices: 51.6 us -> 41.9 us  [move(): return lax.ppermute(cells, axes, pairs)]
    ppermute x18 -> x16, starting transfers between devices: 35.5 us -> 42.1 us  [move(): return lax.ppermute(cells, axes, pairs)]
  transfers between devices with their start and end apart: 20 -> 18, of which waited for: 5 -> 4; matrix products, arithmetic and copies ran while one was open for 9% -> 8% of each run, Pallas kernels for 25% -> 26%
where the time goes in v3:
time: 145 us; the launch traced here: 144 us
  starting transfers between devices  42.9 us (30%)
  Pallas kernels  42.9 us (30%)
  waiting for transfers between devices  41.9 us (29%)
  other arithmetic  8.34 us (6%)
  local copies, waits for them, and re-layouts  7.4 us (5%)
    ppermute x16, starting transfers between devices, move(): return lax.ppermute(cells, axes, pairs)  42.1 us
    ppermute x16, waiting for transfers between devices, move(): return lax.ppermute(cells, axes, pairs)  41.9 us
    pallas_call x1, Pallas kernels, interior(): pl.pallas_call(functools.partial(interior_kernel, rows, lon, ext), in_spe...  16 us
    pallas_call x2, Pallas kernels, border_rows(): pl.pallas_call(functools.partial(border_kernel, outer, rows, lon, ext), i...  12.5 us
    pallas_call x2, Pallas kernels, finish(): pl.pallas_call(functools.partial(finish_kernel, outer, rows, lon, ext), i...  10.6 us
    convert_element_type x1, local copies, waits for them, and re-layouts, per_device(): rows_of(cells, i).astype(jnp.bfloat16)  4.25 us
    pallas_call x4, Pallas kernels, smooth_piece(): pl.pallas_call(functools.partial(smooth_kernel, geo, len(extras)), grid=(...  3.76 us
    another operation x1, other arithmetic  2.96 us
  transfers between devices with their start and end apart: 18, of which 4 were waited for; matrix products, arithmetic and copies ran while one was open for 8% of the time, Pallas kernels for 26%

profile of v3, /device:TPU:21, one launch (start us, length us, event | category | flops | bytes accessed | tf_op | source)
XLA Modules:
  0.0 144.1 jit_solution(11618291531601597420)
XLA Ops:
  0.8 3.0 %convert.7 = bf16[16,360,256]{2,1,0:T(8,128)(2,1)S(1)} convert(f32[16,360,256]{2,1,0:T(8,128)} %state_ref.5) | non-fusion elementwise | flops 1474560 | bytes 8847360 | tf_op jit(solution)/shard_map/convert.4
  4.6 1.4 %dynamic-slice_convert_fusion.4.own_ref = bf16[4,360,256]{2,1,0:T(8,128)(2,1)S(1)} fusion(f32[16,360,256]{2,1,0:T(8,128)} %state_ref.5, s32[]{:T(128)S(6)} %select_n.73), kind=kLoop, calls=%fused_computation.7 | loop fusion | bytes 1474564 | tf_op jit(solution)/shard_map/convert_element_type | solution.py:558
  6.1 1.5 %collective-permute-start.3 = (bf16[4,360,256]{2,1,0:T(8,128)(2,1)S(1)}, bf16[4,360,256]{2,1,0:T(8,128)(2,1)}, u32[]{:S(2)}, u32[]{:S(2)}) collective-permute-start(bf16[4,360,256]{2,1,0:T(8,128)(2,1)S(1)} %dynamic-slice_convert_fusion.4.own_ref), channel_id=1, source_target_pairs={{0,2},{1,3},{2,0},{3,1},{4,6},{5,7},{6,4},{7,5},{24,26},{25,27},{2... | collective-permute-start | bytes 2211848 | tf_op jit(solution)/shard_map/ppermute | solution.py:529
  7.8 4.2 %dynamic-slice_convert_fusion.1 = (bf16[4,360,256]{2,1,0:T(8,128)(2,1)}, bf16[4,360,256]{2,1,0:T(8,128)(2,1)}, bf16[4,360,256]{2,1,0:T(8,128)(2,1)S(1)}, bf16[4,360,256]{2,1,0:T(8,128)(2,1)S(1)}) fusion(f32[16,360,256]{2,1,0:T(8,128)} %state_ref.5, s32[]{:T(128)S(6)} %select_n.76, s32[]{:T(128)S(6)} %select_n.77, s32[]{:T(128)S(6)} %select_n.73, s32[]{:T(128)S(6)} %select_n.69), kind=kLoop, calls=%fused_computation.4 | loop fusion | bytes 5898256 | tf_op jit(solution)/shard_map/convert_element_type | solution.py:561
  12.7 1.8 %maximum_maximum_fusion.2 = (bf16[5,384,256]{2,1,0:T(8,128)(2,1)}, bf16[5,384,256]{2,1,0:T(8,128)(2,1)}) fusion(bf16[1,384,128]{2,1,0:T(8,128)(2,1)S(1)} %get-tuple-element.73, bf16[1,384,128]{2,1,0:T(8,128)(2,1)S(1)} %get-tuple-element.71, bf16[4,8,256]{2,1,0:T(8,128)(2,1)S(1)} %get-tuple-element.79, bf16[4,360,256]{2,1,0:T(8,128)(2,1)S(1)} %get-tuple-element.38.own_ref, ...), kind=kLoop, calls=%fused_computation.9 | loop fusion | flops 11304960 | bytes 3903232 | tf_op jit(solution)/shard_map/concatenate | solution.py:574
  14.4 1.2 pad_maximum_fusion
  15.7 1.9 %collective-permute-start.2 = (bf16[8,360,256]{2,1,0:T(8,128)(2,1)}, bf16[8,360,256]{2,1,0:T(8,128)(2,1)}, u32[]{:S(2)}, u32[]{:S(2)}) collective-permute-start(bf16[8,360,256]{2,1,0:T(8,128)(2,1)} %pad_maximum_fusion), channel_id=1, source_target_pairs={{0,1},{1,0},{2,3},{3,2},{4,5},{5,4},{6,7},{7,6},{24,25},{25,24},{2... | collective-permute-start | bytes 4423688 | tf_op jit(solution)/shard_map/ppermute | solution.py:529
  18.2 1.6 %pad_maximum_fusion.1.own_ref = bf16[8,360,256]{2,1,0:T(8,128)(2,1)S(1)} fusion(bf16[4,360,256]{2,1,0:T(8,128)(2,1)} %get-tuple-element.66, bf16[4,360,256]{2,1,0:T(8,128)(2,1)} %get-tuple-element.65), kind=kLoop, calls=%fused_computation.2 | loop fusion | flops 737280 | bytes 2949120 | tf_op jit(solution)/shard_map/concatenate | solution.py:606
  21.4 3.2 %collective-permute-start.9 = (bf16[5,384,256]{2,1,0:T(8,128)(2,1)S(1)}, bf16[5,384,256]{2,1,0:T(8,128)(2,1)S(1)}, u32[]{:S(2)}, u32[]{:S(2)}) collective-permute-start(bf16[5,384,256]{2,1,0:T(8,128)(2,1)S(1)} %copy-done.2), channel_id=1, source_target_pairs={{8,4},{9,5},{10,6},{11,7},{12,8},{13,9},{14,10},{15,11},{16,20},{1... | collective-permute-start | bytes 2949128 | tf_op jit(solution)/shard_map/ppermute | solution.py:529
  24.8 1.5 %smooth.4 = (f32[4,2,384,128]{3,2,1,0:T(8,128)S(1)}, bf16[5,384,256]{2,1,0:T(8,128)(2,1)S(1)}) custom-call(s32[6]{0:T(128)S(1)} %stack.39.info_ref, s32[4]{0:T(128)S(1)} %get-tuple-element.88.widths_ref, bf16[4,360,256]{2,1,0:T(8,128)(2,1)S(1)} %dynamic-slice_convert_fusion.4.own_ref, bf16[8,360,256]{2,1,0:T(8,128)(2,1)} %collective-permute-done.2.sib_ref, ...), custom_call_target="tpu_custom_call" | custom-call | flops 1000 | bytes 1000 | tf_op jit(solution)/shard_map/smooth/pallas_call | solution.py:139
  28.0 1.3 collective-permute-start.11
  31.4 12.5 %collective-permute-done.9.raw_ref = bf16[5,384,256]{2,1,0:T(8,128)(2,1)S(1)} collective-permute-done((bf16[5,384,256]{2,1,0:T(8,128)(2,1)S(1)}, bf16[5,384,256]{2,1,0:T(8,128)(2,1)S(1)}, u32[]{:S(2)}, u32[]{:S(2)}) %collective-permute-start.9) | collective-permute-done | bytes 983072 | tf_op jit(solution)/shard_map/ppermute | solution.py:529
  45.4 14.7 %collective-permute-done.11.raw_ref.across_ref.across_raw_ref = bf16[5,384,256]{2,1,0:T(8,128)(2,1)S(1)} collective-permute-done((bf16[5,384,256]{2,1,0:T(8,128)(2,1)S(1)}, bf16[5,384,256]{2,1,0:T(8,128)(2,1)S(1)}, u32[]{:S(2)}, u32[]{:S(2)}) %collective-permute-start.11) | collective-permute-done | bytes 983072 | tf_op jit(solution)/shard_map/ppermute | solution.py:529
  60.9 1.9 %collective-permute-start.14 = (bf16[5,384,256]{2,1,0:T(8,128)(2,1)S(1)}, bf16[5,384,256]{2,1,0:T(8,128)(2,1)S(1)}, u32[]{:S(2)}, u32[]{:S(2)}) collective-permute-start(bf16[5,384,256]{2,1,0:T(8,128)(2,1)S(1)} %copy-done.1), channel_id=1, source_target_pairs={{12,16},{13,17},{14,18},{15,19},{16,12},{17,13},{18,14},{19,15}} | collective-permute-start | bytes 2949128 | tf_op jit(solution)/shard_map/ppermute | solution.py:529
  63.4 6.3 %border_outer.1 = (bf16[4,384,256]{2,1,0:T(8,128)(2,1)S(1)}, f32[4,2,384,128]{3,2,1,0:T(8,128)S(1)}, f32[4,2,384,128]{3,2,1,0:T(8,128)S(1)}) custom-call(s32[6]{0:T(128)S(1)} %stack.39.info_ref, f32[16,360,256]{2,1,0:T(8,128)S(1)} %bitcast.7, bf16[16,8,256]{2,1,0:T(8,128)(2,1)S(1)} %slice.52.edge_w_ref, bf16[16,8,256]{2,1,0:T(8,128)(2,1)S(1)} %slice.53.edge_e_ref, ...), custom_call_target="tpu_custom_call" | custom-call | flops 1000 | bytes 1000 | tf_op jit(solution)/shard_map/border_outer/pallas_call | solution.py:332
  69.7 22.9 %collective-permute-start.15 = (bf16[4,384,256]{2,1,0:T(8,128)(2,1)S(1)}, bf16[4,384,256]{2,1,0:T(8,128)(2,1)S(1)}, u32[]{:S(2)}, u32[]{:S(2)}) collective-permute-start(bf16[4,384,256]{2,1,0:T(8,128)(2,1)S(1)} %get-tuple-element.59), channel_id=1, source_target_pairs={{4,0},{5,1},{6,2},{7,3},{8,4},{9,5},{10,6},{11,7},{12,8},{13,9},{1... | collective-permute-start | bytes 2359304 | tf_op jit(solution)/shard_map/ppermute | solution.py:529
  93.2 6.3 %border_inner.1 = (bf16[4,384,256]{2,1,0:T(8,128)(2,1)S(1)}, f32[4,2,384,128]{3,2,1,0:T(8,128)S(1)}, f32[4,2,384,128]{3,2,1,0:T(8,128)S(1)}) custom-call(s32[6]{0:T(128)S(1)} %stack.39.info_ref, f32[16,360,256]{2,1,0:T(8,128)S(1)} %bitcast.7, bf16[16,8,256]{2,1,0:T(8,128)(2,1)S(1)} %slice.52.edge_w_ref, bf16[16,8,256]{2,1,0:T(8,128)(2,1)S(1)} %slice.53.edge_e_ref, ...), custom_call_target="tpu_custom_call" | custom-call | flops 1000 | bytes 1000 | tf_op jit(solution)/shard_map/border_inner/pallas_call | solution.py:332
  99.5 1.9 %collective-permute-start.16 = (bf16[4,384,256]{2,1,0:T(8,128)(2,1)S(1)}, bf16[4,384,256]{2,1,0:T(8,128)(2,1)S(1)}, u32[]{:S(2)}, u32[]{:S(2)}) collective-permute-start(bf16[4,384,256]{2,1,0:T(8,128)(2,1)S(1)} %get-tuple-element.60), channel_id=1, source_target_pairs={{12,16},{13,17},{14,18},{15,19},{16,12},{17,13},{18,14},{19,15}} | collective-permute-start | bytes 2359304 | tf_op jit(solution)/shard_map/ppermute | solution.py:529
  101.4 1.3 collective-permute-start.17
  102.7 16.0 %interior.1 = (bf16[16,360,256]{2,1,0:T(8,128)(2,1)}, f32[4,2,384,128]{3,2,1,0:T(8,128)S(1)}, f32[4,2,384,128]{3,2,1,0:T(8,128)S(1)}) custom-call(s32[6]{0:T(128)S(1)} %stack.39.info_ref, f32[16,360,256]{2,1,0:T(8,128)S(1)} %bitcast.7, bf16[16,8,256]{2,1,0:T(8,128)(2,1)S(1)} %slice.52.edge_w_ref, bf16[16,8,256]{2,1,0:T(8,128)(2,1)S(1)} %slice.53.edge_e_ref, ...), custom_call_target="tpu_custom_call" | custom-call | flops 1000 | bytes 1000 | tf_op jit(solution)/shard_map/interior/pallas_call | solution.py:416
  118.7 1.3 collective-permute-done.16.across_ref
  119.9 5.3 %finish_inner.1._ = bf16[16,360,256]{2,1,0:T(8,128)(2,1)} custom-call(bf16[16,360,256]{2,1,0:T(8,128)(2,1)} %get-tuple-element.58._, s32[6]{0:T(128)S(1)} %stack.39.info_ref, bf16[16,384,128]{2,1,0:T(8,128)(2,1)S(1)} %maximum_maximum_fusion.winds_ref, bf16[5,384,256]{2,1,0:T(8,128)(2,1)S(1)} %collective-permute-done.8.late_ref, ...), custom_call_target="tpu_custom_call", output_to_operand_aliasing={{}: (0, {})} | custom-call | flops 1000 | bytes 1000 | tf_op jit(solution)/shard_map/finish_inner/pallas_call | solution.py:469
  125.3 13.3 %collective-permute-done.17.border_ref.across_ref = bf16[4,384,256]{2,1,0:T(8,128)(2,1)S(1)} collective-permute-done((bf16[4,384,256]{2,1,0:T(8,128)(2,1)S(1)}, bf16[4,384,256]{2,1,0:T(8,128)(2,1)S(1)}, u32[]{:S(2)}, u32[]{:S(2)}) %collective-permute-start.17) | collective-permute-done | bytes 786464 | tf_op jit(solution)/shard_map/ppermute | solution.py:529
  138.6 5.3 %finish_outer.1 = bf16[16,360,256]{2,1,0:T(8,128)(2,1)} custom-call(bf16[16,360,256]{2,1,0:T(8,128)(2,1)} %finish_inner.1._, s32[6]{0:T(128)S(1)} %stack.39.info_ref, bf16[16,384,128]{2,1,0:T(8,128)(2,1)S(1)} %maximum_maximum_fusion.winds_ref, bf16[5,384,256]{2,1,0:T(8,128)(2,1)S(1)} %collective-permute-done.10.late_ref, ...), custom_call_target="tpu_custom_call", output_to_operand_aliasing={{}: (0, {})} | custom-call | flops 1000 | bytes 1000 | tf_op jit(solution)/shard_map/finish_outer/pallas_call | solution.py:469
  (75 shorter events, 11.7 us)
Async XLA Ops:
  3.8 8.2 %collective-permute-start = (bf16[16,8,384]{2,1,0:T(8,128)(2,1)S(1)}, bf16[16,8,384]{2,1,0:T(8,128)(2,1)S(1)}, u32[]{:S(2)}, u32[]{:S(2)}) collective-permute-start(bf16[16,8,384]{2,1,0:T(8,128)(2,1)S(1)} %get-tuple-element.34), channel_id=1, source_target_pairs={{0,1},{1,2},{2,3},{3,0},{4,5},{5,6},{6,7},{7,4},{8,9},{9,10},{10,1... | collective-permute-start | bytes 294920 | tf_op jit(solution)/shard_map/ppermute | solution.py:555
  4.6 7.4 %collective-permute-start.1 = (bf16[16,8,384]{2,1,0:T(8,128)(2,1)S(1)}, bf16[16,8,384]{2,1,0:T(8,128)(2,1)S(1)}, u32[]{:S(2)}, u32[]{:S(2)}) collective-permute-start(bf16[16,8,384]{2,1,0:T(8,128)(2,1)S(1)} %get-tuple-element.35), channel_id=1, source_target_pairs={{1,0},{2,1},{3,2},{0,3},{5,4},{6,5},{7,6},{4,7},{9,8},{10,9},{11,1... | collective-permute-start | bytes 294920 | tf_op jit(solution)/shard_map/ppermute | solution.py:554
  6.1 14.4 %collective-permute-start.3 = (bf16[4,360,256]{2,1,0:T(8,128)(2,1)S(1)}, bf16[4,360,256]{2,1,0:T(8,128)(2,1)}, u32[]{:S(2)}, u32[]{:S(2)}) collective-permute-start(bf16[4,360,256]{2,1,0:T(8,128)(2,1)S(1)} %dynamic-slice_convert_fusion.4.own_ref), channel_id=1, source_target_pairs={{0,2},{1,3},{2,0},{3,1},{4,6},{5,7},{6,4},{7,5},{24,26},{25,27},{2... | collective-permute-start | bytes 2211848 | tf_op jit(solution)/shard_map/ppermute | solution.py:529
  7.8 4.4 %copy-start = (bf16[16,360,128]{2,1,0:T(8,128)(2,1)S(1)}, bf16[16,360,128]{2,1,0:T(8,128)(2,1)}, u32[]{:S(2)}) copy-start(bf16[16,360,128]{2,1,0:T(8,128)(2,1)} %param.5) | copy-start | bytes 4423684
  15.7 5.5 %copy-start.5 = (s32[128]{0:T(128)S(1)}, s32[128]{0:T(128)}, u32[]{:S(2)}) copy-start(s32[128]{0:T(128)} %param.7) | copy-start | bytes 1540
  15.7 9.1 %collective-permute-start.2 = (bf16[8,360,256]{2,1,0:T(8,128)(2,1)}, bf16[8,360,256]{2,1,0:T(8,128)(2,1)}, u32[]{:S(2)}, u32[]{:S(2)}) collective-permute-start(bf16[8,360,256]{2,1,0:T(8,128)(2,1)} %pad_maximum_fusion), channel_id=1, source_target_pairs={{0,1},{1,0},{2,3},{3,2},{4,5},{5,4},{6,7},{7,6},{24,25},{25,24},{2... | collective-permute-start | bytes 4423688 | tf_op jit(solution)/shard_map/ppermute | solution.py:529
  18.2 3.2 %copy-start.2 = (bf16[5,384,256]{2,1,0:T(8,128)(2,1)S(1)}, bf16[5,384,256]{2,1,0:T(8,128)(2,1)}, u32[]{:S(2)}) copy-start(bf16[5,384,256]{2,1,0:T(8,128)(2,1)} %get-tuple-element.82) | copy-start | bytes 2949124
  18.2 6.6 %copy-start.4 = (bf16[1,384,128]{2,1,0:T(8,128)(2,1)S(1)}, bf16[1,384,128]{2,1,0:T(8,128)(2,1)}, u32[]{:S(2)}) copy-start(bf16[1,384,128]{2,1,0:T(8,128)(2,1)} %copy-done.3) | copy-start | bytes 294916
  19.8 6.6 %collective-permute-start.5 = (bf16[4,360,256]{2,1,0:T(8,128)(2,1)S(1)}, bf16[4,360,256]{2,1,0:T(8,128)(2,1)S(1)}, u32[]{:S(2)}, u32[]{:S(2)}) collective-permute-start(bf16[4,360,256]{2,1,0:T(8,128)(2,1)S(1)} %get-tuple-element.38.own_ref), channel_id=1, source_target_pairs={{0,2},{1,3},{2,0},{3,1},{4,6},{5,7},{6,4},{7,5},{24,26},{25,27},{2... | collective-permute-start | bytes 2211848 | tf_op jit(solution)/shard_map/ppermute | solution.py:529
  20.5 4.3 %collective-permute-start.4 = (bf16[4,360,256]{2,1,0:T(8,128)(2,1)}, bf16[4,360,256]{2,1,0:T(8,128)(2,1)S(1)}, u32[]{:S(2)}, u32[]{:S(2)}) collective-permute-start(bf16[4,360,256]{2,1,0:T(8,128)(2,1)} %collective-permute-done.3.opp_ref), channel_id=1, source_target_pairs={{0,1},{1,0},{2,3},{3,2},{4,5},{5,4},{6,7},{7,6},{24,25},{25,24},{2... | collective-permute-start | bytes 2211848 | tf_op jit(solution)/shard_map/ppermute | solution.py:529
  21.4 22.5 %collective-permute-start.9 = (bf16[5,384,256]{2,1,0:T(8,128)(2,1)S(1)}, bf16[5,384,256]{2,1,0:T(8,128)(2,1)S(1)}, u32[]{:S(2)}, u32[]{:S(2)}) collective-permute-start(bf16[5,384,256]{2,1,0:T(8,128)(2,1)S(1)} %copy-done.2), channel_id=1, source_target_pairs={{8,4},{9,5},{10,6},{11,7},{12,8},{13,9},{14,10},{15,11},{16,20},{1... | collective-permute-start | bytes 2949128 | tf_op jit(solution)/shard_map/ppermute | solution.py:529
  24.8 38.5 %slice-start = ((s8[5898240]{0:T(1024)(128)(4,1)}), s8[4194304]{0:T(1024)(128)(4,1)S(1)}, s32[]{:S(2)}) async-start(s8[5898240]{0:T(1024)(128)(4,1)} %bitcast.6), calls=%async_computation | async-start | bytes 8388608
  26.4 3.8 %collective-permute-start.6 = (bf16[4,360,256]{2,1,0:T(8,128)(2,1)S(1)}, bf16[4,360,256]{2,1,0:T(8,128)(2,1)S(1)}, u32[]{:S(2)}, u32[]{:S(2)}) collective-permute-start(bf16[4,360,256]{2,1,0:T(8,128)(2,1)S(1)} %collective-permute-done.5.opp_ref), channel_id=1, source_target_pairs={{0,1},{1,0},{2,3},{3,2},{4,5},{5,4},{6,7},{7,6},{24,25},{25,24},{2... | collective-permute-start | bytes 2211848 | tf_op jit(solution)/shard_map/ppermute | solution.py:529
  27.2 18.2 %collective-permute-start.7 = (bf16[8,360,256]{2,1,0:T(8,128)(2,1)S(1)}, bf16[8,360,256]{2,1,0:T(8,128)(2,1)S(1)}, u32[]{:S(2)}, u32[]{:S(2)}) collective-permute-start(bf16[8,360,256]{2,1,0:T(8,128)(2,1)S(1)} %pad_maximum_fusion.1.own_ref), channel_id=1, source_target_pairs={{0,2},{1,3},{2,0},{3,1},{4,6},{5,7},{6,4},{7,5},{24,26},{25,27},{2... | collective-permute-start | bytes 4423688 | tf_op jit(solution)/shard_map/ppermute | solution.py:529
  28.0 32.1 %collective-permute-start.11 = (bf16[5,384,256]{2,1,0:T(8,128)(2,1)S(1)}, bf16[5,384,256]{2,1,0:T(8,128)(2,1)S(1)}, u32[]{:S(2)}, u32[]{:S(2)}) collective-permute-start(bf16[5,384,256]{2,1,0:T(8,128)(2,1)S(1)} %copy-done.1), channel_id=1, source_target_pairs={{8,12},{9,13},{10,14},{11,15},{20,16},{21,17},{22,18},{23,19}} | collective-permute-start | bytes 2949128 | tf_op jit(solution)/shard_map/ppermute | solution.py:529
  29.3 34.0 %slice-start.1 = ((s8[5898240]{0:T(1024)(128)(4,1)}), s8[1703936]{0:T(1024)(128)(4,1)S(1)}, s32[]{:S(2)}) async-start(s8[5898240]{0:T(1024)(128)(4,1)} %bitcast.6), calls=%async_computation.1 | async-start | bytes 3407872
  29.3 30.8 %collective-permute-start.8 = (bf16[5,384,256]{2,1,0:T(8,128)(2,1)S(1)}, bf16[5,384,256]{2,1,0:T(8,128)(2,1)S(1)}, u32[]{:S(2)}, u32[]{:S(2)}) collective-permute-start(bf16[5,384,256]{2,1,0:T(8,128)(2,1)S(1)} %get-tuple-element.46), channel_id=1, source_target_pairs={{4,0},{5,1},{6,2},{7,3},{24,28},{25,29},{26,30},{27,31}} | collective-permute-start | bytes 2949128 | tf_op jit(solution)/shard_map/ppermute | solution.py:529
  43.9 16.2 %collective-permute-start.10 = (bf16[5,384,256]{2,1,0:T(8,128)(2,1)S(1)}, bf16[5,384,256]{2,1,0:T(8,128)(2,1)S(1)}, u32[]{:S(2)}, u32[]{:S(2)}) collective-permute-start(bf16[5,384,256]{2,1,0:T(8,128)(2,1)S(1)} %get-tuple-element.48), channel_id=1, source_target_pairs={{0,4},{1,5},{2,6},{3,7},{4,8},{5,9},{6,10},{7,11},{24,20},{25,21},... | collective-permute-start | bytes 2949128 | tf_op jit(solution)/shard_map/ppermute | solution.py:529
  44.6 18.2 %collective-permute-start.12 = (bf16[8,360,256]{2,1,0:T(8,128)(2,1)S(1)}, bf16[8,360,256]{2,1,0:T(8,128)(2,1)S(1)}, u32[]{:S(2)}, u32[]{:S(2)}) collective-permute-start(bf16[8,360,256]{2,1,0:T(8,128)(2,1)S(1)} %pad_maximum_fusion.1.own_ref), channel_id=1, source_target_pairs={{0,1},{1,0},{2,3},{3,2},{4,5},{5,4},{6,7},{7,6},{24,25},{25,24},{2... | collective-permute-start | bytes 4423688 | tf_op jit(solution)/shard_map/ppermute | solution.py:529
  60.1 2.7 %collective-permute-start.13 = (bf16[8,360,256]{2,1,0:T(8,128)(2,1)S(1)}, bf16[8,360,256]{2,1,0:T(8,128)(2,1)S(1)}, u32[]{:S(2)}, u32[]{:S(2)}) collective-permute-start(bf16[8,360,256]{2,1,0:T(8,128)(2,1)S(1)} %collective-permute-done.7.opp_ref), channel_id=1, source_target_pairs={{0,1},{1,0},{2,3},{3,2},{4,5},{5,4},{6,7},{7,6},{24,25},{25,24},{2... | collective-permute-start | bytes 4423688 | tf_op jit(solution)/shard_map/ppermute | solution.py:529
  60.9 32.3 %collective-permute-start.14 = (bf16[5,384,256]{2,1,0:T(8,128)(2,1)S(1)}, bf16[5,384,256]{2,1,0:T(8,128)(2,1)S(1)}, u32[]{:S(2)}, u32[]{:S(2)}) collective-permute-start(bf16[5,384,256]{2,1,0:T(8,128)(2,1)S(1)} %copy-done.1), channel_id=1, source_target_pairs={{12,16},{13,17},{14,18},{15,19},{16,12},{17,13},{18,14},{19,15}} | collective-permute-start | bytes 2949128 | tf_op jit(solution)/shard_map/ppermute | solution.py:529
  69.7 49.0 %collective-permute-start.15 = (bf16[4,384,256]{2,1,0:T(8,128)(2,1)S(1)}, bf16[4,384,256]{2,1,0:T(8,128)(2,1)S(1)}, u32[]{:S(2)}, u32[]{:S(2)}) collective-permute-start(bf16[4,384,256]{2,1,0:T(8,128)(2,1)S(1)} %get-tuple-element.59), channel_id=1, source_target_pairs={{4,0},{5,1},{6,2},{7,3},{8,4},{9,5},{10,6},{11,7},{12,8},{13,9},{1... | collective-permute-start | bytes 2359304 | tf_op jit(solution)/shard_map/ppermute | solution.py:529
  99.5 20.5 %collective-permute-start.16 = (bf16[4,384,256]{2,1,0:T(8,128)(2,1)S(1)}, bf16[4,384,256]{2,1,0:T(8,128)(2,1)S(1)}, u32[]{:S(2)}, u32[]{:S(2)}) collective-permute-start(bf16[4,384,256]{2,1,0:T(8,128)(2,1)S(1)} %get-tuple-element.60), channel_id=1, source_target_pairs={{12,16},{13,17},{14,18},{15,19},{16,12},{17,13},{18,14},{19,15}} | collective-permute-start | bytes 2359304 | tf_op jit(solution)/shard_map/ppermute | solution.py:529
  101.4 37.2 %collective-permute-start.17 = (bf16[4,384,256]{2,1,0:T(8,128)(2,1)S(1)}, bf16[4,384,256]{2,1,0:T(8,128)(2,1)S(1)}, u32[]{:S(2)}, u32[]{:S(2)}) collective-permute-start(bf16[4,384,256]{2,1,0:T(8,128)(2,1)S(1)} %get-tuple-element.60), channel_id=1, source_target_pairs={{0,4},{1,5},{2,6},{3,7},{4,8},{5,9},{6,10},{7,11},{8,12},{9,13},{1... | collective-permute-start | bytes 2359304 | tf_op jit(solution)/shard_map/ppermute | solution.py:529
  (3 other events, 8.1 us)

commit v4 on v3

--- a/solution.py
+++ b/solution.py
@@ -399,12 +399,17 @@
     def _():
         hand_on(third_i_ref, third_o_ref)
 
-    step_rows(field_b, winds, zero, 0, inner - 4, 2, REACH, REACH + lon, store_out(part_ref))
-    copy = pltpu.make_async_copy(part_ref, out_ref.at[pl.ds(HALO, rows - 2 * HALO)], out_sem.at[2])
-    copy.start()
+    half = (rows - 2 * HALO) // 2
+    results = []
+    for i in range(2):
+        step_rows(field_b, winds, zero, i * half, (i + 1) * half, 2, REACH, REACH + lon, store_out(part_ref))
+        results.append(pltpu.make_async_copy(
+            part_ref.at[pl.ds(i * half, half)], out_ref.at[pl.ds(HALO + i * half, half)], out_sem.at[2 + i]))
+        results[i].start()
     for i in range(2):
         pltpu.make_async_copy(strip(field_b, 0, ext), third_o_ref, out_sem.at[i]).wait()
-    copy.wait()
+    for copy in results:
+        copy.wait()
 
 
 def interior(info, state, edges, winds, levels, ones, smooths):
@@ -421,7 +426,7 @@
         scratch_shapes=[
             cells_of(rows - 2 * HALO, tiles, ext), cells_of(rows - 4, tiles, ext), cells_of(rows, tiles, ext),
             half_of(rows - 2 * HALO, lon, channels), half_of(rows - 4, ext, LANES),
-            pltpu.SemaphoreType.DMA((2,)), pltpu.SemaphoreType.DMA((5,)), pltpu.SemaphoreType.DMA((3,)),
+            pltpu.SemaphoreType.DMA((2,)), pltpu.SemaphoreType.DMA((5,)), pltpu.SemaphoreType.DMA((4,)),
         ],
         compiler_params=pltpu.CompilerParams(vmem_limit_bytes=24 * MIB),
         cost_estimate=pl.CostEstimate(flops=1000, bytes_accessed=1000, transcendentals=0),
@@ -453,10 +458,14 @@
             last[r + other, t, pl.ds(PAD + c, count), :] = value
 
         step_rows(near, winds, zero, 0, HALO, 2 if north else 0, 0, ext, store)
-        step_rows(last, winds, zero, 0, HALO, 0 if north else 2, REACH, REACH + lon, store_out(part_ref))
-        copy = pltpu.make_async_copy(part_ref, out_ref.at[pl.ds(rows - HALO if north else 0, HALO)], out_sem.at[0])
-        copy.start()
-        copy.wait()
+        results, half = [], HALO // 2
+        for i in range(2):
+            step_rows(last, winds, zero, i * half, (i + 1) * half, 0 if north else 2, REACH, REACH + lon, store_out(part_ref))
+            place = out_ref.at[pl.ds((rows - HALO if north else 0) + i * half, half)]
+            results.append(pltpu.make_async_copy(part_ref.at[pl.ds(i * half, half)], place, out_sem.at[i]))
+            results[i].start()
+        for copy in results:
+            copy.wait()
 
     on_side(info_ref, outer, body)
 
@@ -476,7 +485,7 @@
             cells_of(2 * HALO, tiles, ext), cells_of(2 * HALO, tiles, ext),
             half_of(HALO + 2, ext, LANES), half_of(HALO, ext, channels), half_of(HALO, lon, channels),
             pltpu.SemaphoreType.DMA((6,)),
-            pltpu.SemaphoreType.DMA((1,)),
+            pltpu.SemaphoreType.DMA((2,)),
         ],
         compiler_params=pltpu.CompilerParams(vmem_limit_bytes=16 * MIB),
         cost_estimate=pl.CostEstimate(flops=1000, bytes_accessed=1000, transcendentals=0),
@@ -545,12 +554,14 @@
     def ordered(values):
         return jnp.concatenate([rows_of(values, i) for i in range(len(starts))], axis=0)
 
-    def joined(cols):
-        return jnp.concatenate([state[:, cols].astype(jnp.bfloat16), winds[:, cols]], axis=2)
+    def joined(cells, cols):
+        return jnp.concatenate([cells.astype(jnp.bfloat16), winds[:, cols]], axis=2)
 
     east = [(l, (l + 1) % tiles) for l in range(tiles)]
     west = [((l + 1) % tiles, l) for l in range(tiles)]
-    head, rear, cells = tie(joined(slice(0, REACH)), joined(slice(lon - REACH, lon)), state)
+    first, last = slice(0, REACH), slice(lon - REACH, lon)
+    head, rear = tie(state[:, first], state[:, last])
+    head, rear, cells = tie(joined(head, first), joined(rear, last), state)
     from_east = lax.ppermute(head, "lon", west)
     from_west = lax.ppermute(rear, "lon", east)
 

time: 145 us -> 143 us (0.986)
  other arithmetic: 8.34 us -> 5.38 us
    another operation x1 -> x0, other arithmetic: 2.96 us -> none
where the time goes in v4:
time: 143 us; the launch traced here: 142 us
  starting transfers between devices  42.9 us (30%)
  Pallas kernels  42.4 us (30%)
  waiting for transfers between devices  42.2 us (30%)
  local copies, waits for them, and re-layouts  8.37 us (6%)
  other arithmetic  5.38 us (4%)
    ppermute x16, waiting for transfers between devices, move(): return lax.ppermute(cells, axes, pairs)  42.2 us
    ppermute x16, starting transfers between devices, move(): return lax.ppermute(cells, axes, pairs)  42.1 us
    pallas_call x1, Pallas kernels, interior(): pl.pallas_call(functools.partial(interior_kernel, rows, lon, ext), in_spe...  15.7 us
    pallas_call x2, Pallas kernels, border_rows(): pl.pallas_call(functools.partial(border_kernel, outer, rows, lon, ext), i...  12.5 us
    pallas_call x2, Pallas kernels, finish(): pl.pallas_call(functools.partial(finish_kernel, outer, rows, lon, ext), i...  10.4 us
    convert_element_type x1, local copies, waits for them, and re-layouts, per_device(): rows_of(cells, i).astype(jnp.bfloat16)  4.25 us
    pallas_call x4, Pallas kernels, smooth_piece(): pl.pallas_call(functools.partial(smooth_kernel, geo, len(extras)), grid=(...  3.76 us
  transfers between devices with their start and end apart: 18, of which 4 were waited for; matrix products, arithmetic and copies ran while one was open for 8% of the time, Pallas kernels for 26%

profile of v4, /device:TPU:21, one launch (start us, length us, event | category | flops | bytes accessed | tf_op | source)
XLA Modules:
  0.0 141.9 jit_solution(15862936412723086432)
XLA Ops:
  2.6 1.4 %dynamic-slice_convert_fusion.4.own_ref = bf16[4,360,256]{2,1,0:T(8,128)(2,1)S(1)} fusion(f32[16,360,256]{2,1,0:T(8,128)} %state_ref.5, s32[]{:T(128)S(6)} %select_n.73), kind=kLoop, calls=%fused_computation.7 | loop fusion | bytes 1474564 | tf_op jit(solution)/shard_map/convert_element_type | solution.py:569
  4.1 1.5 %collective-permute-start.3 = (bf16[4,360,256]{2,1,0:T(8,128)(2,1)S(1)}, bf16[4,360,256]{2,1,0:T(8,128)(2,1)}, u32[]{:S(2)}, u32[]{:S(2)}) collective-permute-start(bf16[4,360,256]{2,1,0:T(8,128)(2,1)S(1)} %dynamic-slice_convert_fusion.4.own_ref), channel_id=1, source_target_pairs={{0,2},{1,3},{2,0},{3,1},{4,6},{5,7},{6,4},{7,5},{24,26},{25,27},{2... | collective-permute-start | bytes 2211848 | tf_op jit(solution)/shard_map/ppermute | solution.py:538
  5.8 4.2 %dynamic-slice_convert_fusion.1 = (bf16[4,360,256]{2,1,0:T(8,128)(2,1)}, bf16[4,360,256]{2,1,0:T(8,128)(2,1)}, bf16[4,360,256]{2,1,0:T(8,128)(2,1)S(1)}, bf16[4,360,256]{2,1,0:T(8,128)(2,1)S(1)}) fusion(f32[16,360,256]{2,1,0:T(8,128)} %state_ref.5, s32[]{:T(128)S(6)} %select_n.76, s32[]{:T(128)S(6)} %select_n.77, s32[]{:T(128)S(6)} %select_n.73, s32[]{:T(128)S(6)} %select_n.69), kind=kLoop, calls=%fused_computation.4 | loop fusion | bytes 5898256 | tf_op jit(solution)/shard_map/convert_element_type | solution.py:572
  10.7 1.8 %maximum_maximum_fusion.2 = (bf16[5,384,256]{2,1,0:T(8,128)(2,1)}, bf16[5,384,256]{2,1,0:T(8,128)(2,1)}) fusion(bf16[1,384,128]{2,1,0:T(8,128)(2,1)S(1)} %get-tuple-element.77, bf16[1,384,128]{2,1,0:T(8,128)(2,1)S(1)} %get-tuple-element.75, bf16[4,8,256]{2,1,0:T(8,128)(2,1)S(1)} %get-tuple-element.83, bf16[4,360,256]{2,1,0:T(8,128)(2,1)S(1)} %get-tuple-element.42.own_ref, ...), kind=kLoop, calls=%fused_computation.9 | loop fusion | flops 11304960 | bytes 3903232 | tf_op jit(solution)/shard_map/concatenate | solution.py:585
  12.4 1.2 pad_maximum_fusion
  13.7 1.9 %collective-permute-start.2 = (bf16[8,360,256]{2,1,0:T(8,128)(2,1)}, bf16[8,360,256]{2,1,0:T(8,128)(2,1)}, u32[]{:S(2)}, u32[]{:S(2)}) collective-permute-start(bf16[8,360,256]{2,1,0:T(8,128)(2,1)} %pad_maximum_fusion), channel_id=1, source_target_pairs={{0,1},{1,0},{2,3},{3,2},{4,5},{5,4},{6,7},{7,6},{24,25},{25,24},{2... | collective-permute-start | bytes 4423688 | tf_op jit(solution)/shard_map/ppermute | solution.py:538
  16.2 1.6 %pad_maximum_fusion.1.own_ref = bf16[8,360,256]{2,1,0:T(8,128)(2,1)S(1)} fusion(bf16[4,360,256]{2,1,0:T(8,128)(2,1)} %get-tuple-element.70, bf16[4,360,256]{2,1,0:T(8,128)(2,1)} %get-tuple-element.69), kind=kLoop, calls=%fused_computation.2 | loop fusion | flops 737280 | bytes 2949120 | tf_op jit(solution)/shard_map/concatenate | solution.py:617
  19.4 3.2 %collective-permute-start.9 = (bf16[5,384,256]{2,1,0:T(8,128)(2,1)S(1)}, bf16[5,384,256]{2,1,0:T(8,128)(2,1)S(1)}, u32[]{:S(2)}, u32[]{:S(2)}) collective-permute-start(bf16[5,384,256]{2,1,0:T(8,128)(2,1)S(1)} %copy-done.2), channel_id=1, source_target_pairs={{8,4},{9,5},{10,6},{11,7},{12,8},{13,9},{14,10},{15,11},{16,20},{1... | collective-permute-start | bytes 2949128 | tf_op jit(solution)/shard_map/ppermute | solution.py:538
  22.9 1.5 %smooth.4 = (f32[4,2,384,128]{3,2,1,0:T(8,128)S(1)}, bf16[5,384,256]{2,1,0:T(8,128)(2,1)S(1)}) custom-call(s32[6]{0:T(128)S(1)} %stack.39.info_ref, s32[4]{0:T(128)S(1)} %get-tuple-element.92.widths_ref, bf16[4,360,256]{2,1,0:T(8,128)(2,1)S(1)} %dynamic-slice_convert_fusion.4.own_ref, bf16[8,360,256]{2,1,0:T(8,128)(2,1)} %collective-permute-done.2.sib_ref, ...), custom_call_target="tpu_custom_call" | custom-call | flops 1000 | bytes 1000 | tf_op jit(solution)/shard_map/smooth/pallas_call | solution.py:139
  26.0 1.3 collective-permute-start.11
  28.2 1.1 smooth.5
  29.4 12.5 %collective-permute-done.9.raw_ref = bf16[5,384,256]{2,1,0:T(8,128)(2,1)S(1)} collective-permute-done((bf16[5,384,256]{2,1,0:T(8,128)(2,1)S(1)}, bf16[5,384,256]{2,1,0:T(8,128)(2,1)S(1)}, u32[]{:S(2)}, u32[]{:S(2)}) %collective-permute-start.9) | collective-permute-done | bytes 983072 | tf_op jit(solution)/shard_map/ppermute | solution.py:538
  43.4 14.7 %collective-permute-done.11.raw_ref.across_ref.across_raw_ref = bf16[5,384,256]{2,1,0:T(8,128)(2,1)S(1)} collective-permute-done((bf16[5,384,256]{2,1,0:T(8,128)(2,1)S(1)}, bf16[5,384,256]{2,1,0:T(8,128)(2,1)S(1)}, u32[]{:S(2)}, u32[]{:S(2)}) %collective-permute-start.11) | collective-permute-done | bytes 983072 | tf_op jit(solution)/shard_map/ppermute | solution.py:538
  58.9 1.9 %collective-permute-start.14 = (bf16[5,384,256]{2,1,0:T(8,128)(2,1)S(1)}, bf16[5,384,256]{2,1,0:T(8,128)(2,1)S(1)}, u32[]{:S(2)}, u32[]{:S(2)}) collective-permute-start(bf16[5,384,256]{2,1,0:T(8,128)(2,1)S(1)} %copy-done.1), channel_id=1, source_target_pairs={{12,16},{13,17},{14,18},{15,19},{16,12},{17,13},{18,14},{19,15}} | collective-permute-start | bytes 2949128 | tf_op jit(solution)/shard_map/ppermute | solution.py:538
  61.4 6.3 %border_outer.1 = (bf16[4,384,256]{2,1,0:T(8,128)(2,1)S(1)}, f32[4,2,384,128]{3,2,1,0:T(8,128)S(1)}, f32[4,2,384,128]{3,2,1,0:T(8,128)S(1)}) custom-call(s32[6]{0:T(128)S(1)} %stack.39.info_ref, f32[16,360,256]{2,1,0:T(8,128)S(1)} %bitcast.7, bf16[16,8,256]{2,1,0:T(8,128)(2,1)S(1)} %slice.48.edge_w_ref, bf16[16,8,256]{2,1,0:T(8,128)(2,1)S(1)} %slice.49.edge_e_ref, ...), custom_call_target="tpu_custom_call" | custom-call | flops 1000 | bytes 1000 | tf_op jit(solution)/shard_map/border_outer/pallas_call | solution.py:332
  67.7 22.9 %collective-permute-start.15 = (bf16[4,384,256]{2,1,0:T(8,128)(2,1)S(1)}, bf16[4,384,256]{2,1,0:T(8,128)(2,1)S(1)}, u32[]{:S(2)}, u32[]{:S(2)}) collective-permute-start(bf16[4,384,256]{2,1,0:T(8,128)(2,1)S(1)} %get-tuple-element.63), channel_id=1, source_target_pairs={{4,0},{5,1},{6,2},{7,3},{8,4},{9,5},{10,6},{11,7},{12,8},{13,9},{1... | collective-permute-start | bytes 2359304 | tf_op jit(solution)/shard_map/ppermute | solution.py:538
  91.2 6.3 %border_inner.1 = (bf16[4,384,256]{2,1,0:T(8,128)(2,1)S(1)}, f32[4,2,384,128]{3,2,1,0:T(8,128)S(1)}, f32[4,2,384,128]{3,2,1,0:T(8,128)S(1)}) custom-call(s32[6]{0:T(128)S(1)} %stack.39.info_ref, f32[16,360,256]{2,1,0:T(8,128)S(1)} %bitcast.7, bf16[16,8,256]{2,1,0:T(8,128)(2,1)S(1)} %slice.48.edge_w_ref, bf16[16,8,256]{2,1,0:T(8,128)(2,1)S(1)} %slice.49.edge_e_ref, ...), custom_call_target="tpu_custom_call" | custom-call | flops 1000 | bytes 1000 | tf_op jit(solution)/shard_map/border_inner/pallas_call | solution.py:332
  97.5 1.9 %collective-permute-start.16 = (bf16[4,384,256]{2,1,0:T(8,128)(2,1)S(1)}, bf16[4,384,256]{2,1,0:T(8,128)(2,1)S(1)}, u32[]{:S(2)}, u32[]{:S(2)}) collective-permute-start(bf16[4,384,256]{2,1,0:T(8,128)(2,1)S(1)} %get-tuple-element.64), channel_id=1, source_target_pairs={{12,16},{13,17},{14,18},{15,19},{16,12},{17,13},{18,14},{19,15}} | collective-permute-start | bytes 2359304 | tf_op jit(solution)/shard_map/ppermute | solution.py:538
  99.4 1.3 collective-permute-start.17
  100.7 15.7 %interior.1 = (bf16[16,360,256]{2,1,0:T(8,128)(2,1)}, f32[4,2,384,128]{3,2,1,0:T(8,128)S(1)}, f32[4,2,384,128]{3,2,1,0:T(8,128)S(1)}) custom-call(s32[6]{0:T(128)S(1)} %stack.39.info_ref, f32[16,360,256]{2,1,0:T(8,128)S(1)} %bitcast.7, bf16[16,8,256]{2,1,0:T(8,128)(2,1)S(1)} %slice.48.edge_w_ref, bf16[16,8,256]{2,1,0:T(8,128)(2,1)S(1)} %slice.49.edge_e_ref, ...), custom_call_target="tpu_custom_call" | custom-call | flops 1000 | bytes 1000 | tf_op jit(solution)/shard_map/interior/pallas_call | solution.py:421
  116.4 1.5 %collective-permute-done.16.across_ref = bf16[4,384,256]{2,1,0:T(8,128)(2,1)S(1)} collective-permute-done((bf16[4,384,256]{2,1,0:T(8,128)(2,1)S(1)}, bf16[4,384,256]{2,1,0:T(8,128)(2,1)S(1)}, u32[]{:S(2)}, u32[]{:S(2)}) %collective-permute-start.16) | collective-permute-done | bytes 786464 | tf_op jit(solution)/shard_map/ppermute | solution.py:538
  117.9 5.2 %finish_inner.1._ = bf16[16,360,256]{2,1,0:T(8,128)(2,1)} custom-call(bf16[16,360,256]{2,1,0:T(8,128)(2,1)} %get-tuple-element.62._, s32[6]{0:T(128)S(1)} %stack.39.info_ref, bf16[16,384,128]{2,1,0:T(8,128)(2,1)S(1)} %maximum_maximum_fusion.winds_ref, bf16[5,384,256]{2,1,0:T(8,128)(2,1)S(1)} %collective-permute-done.8.late_ref, ...), custom_call_target="tpu_custom_call", output_to_operand_aliasing={{}: (0, {})} | custom-call | flops 1000 | bytes 1000 | tf_op jit(solution)/shard_map/finish_inner/pallas_call | solution.py:478
  123.1 13.4 %collective-permute-done.17.border_ref.across_ref = bf16[4,384,256]{2,1,0:T(8,128)(2,1)S(1)} collective-permute-done((bf16[4,384,256]{2,1,0:T(8,128)(2,1)S(1)}, bf16[4,384,256]{2,1,0:T(8,128)(2,1)S(1)}, u32[]{:S(2)}, u32[]{:S(2)}) %collective-permute-start.17) | collective-permute-done | bytes 786464 | tf_op jit(solution)/shard_map/ppermute | solution.py:538
  136.6 5.2 %finish_outer.1 = bf16[16,360,256]{2,1,0:T(8,128)(2,1)} custom-call(bf16[16,360,256]{2,1,0:T(8,128)(2,1)} %finish_inner.1._, s32[6]{0:T(128)S(1)} %stack.39.info_ref, bf16[16,384,128]{2,1,0:T(8,128)(2,1)S(1)} %maximum_maximum_fusion.winds_ref, bf16[5,384,256]{2,1,0:T(8,128)(2,1)S(1)} %collective-permute-done.10.late_ref, ...), custom_call_target="tpu_custom_call", output_to_operand_aliasing={{}: (0, {})} | custom-call | flops 1000 | bytes 1000 | tf_op jit(solution)/shard_map/finish_outer/pallas_call | solution.py:478
  (74 shorter events, 11.6 us)
Async XLA Ops:
  1.8 8.2 %collective-permute-start = (bf16[16,8,384]{2,1,0:T(8,128)(2,1)S(1)}, bf16[16,8,384]{2,1,0:T(8,128)(2,1)S(1)}, u32[]{:S(2)}, u32[]{:S(2)}) collective-permute-start(bf16[16,8,384]{2,1,0:T(8,128)(2,1)S(1)} %get-tuple-element.38), channel_id=1, source_target_pairs={{0,1},{1,2},{2,3},{3,0},{4,5},{5,6},{6,7},{7,4},{8,9},{9,10},{10,1... | collective-permute-start | bytes 294920 | tf_op jit(solution)/shard_map/ppermute | solution.py:566
  2.6 7.4 %collective-permute-start.1 = (bf16[16,8,384]{2,1,0:T(8,128)(2,1)S(1)}, bf16[16,8,384]{2,1,0:T(8,128)(2,1)S(1)}, u32[]{:S(2)}, u32[]{:S(2)}) collective-permute-start(bf16[16,8,384]{2,1,0:T(8,128)(2,1)S(1)} %get-tuple-element.39), channel_id=1, source_target_pairs={{1,0},{2,1},{3,2},{0,3},{5,4},{6,5},{7,6},{4,7},{9,8},{10,9},{11,1... | collective-permute-start | bytes 294920 | tf_op jit(solution)/shard_map/ppermute | solution.py:565
  4.1 14.4 %collective-permute-start.3 = (bf16[4,360,256]{2,1,0:T(8,128)(2,1)S(1)}, bf16[4,360,256]{2,1,0:T(8,128)(2,1)}, u32[]{:S(2)}, u32[]{:S(2)}) collective-permute-start(bf16[4,360,256]{2,1,0:T(8,128)(2,1)S(1)} %dynamic-slice_convert_fusion.4.own_ref), channel_id=1, source_target_pairs={{0,2},{1,3},{2,0},{3,1},{4,6},{5,7},{6,4},{7,5},{24,26},{25,27},{2... | collective-permute-start | bytes 2211848 | tf_op jit(solution)/shard_map/ppermute | solution.py:538
  5.8 4.4 %copy-start = (bf16[16,360,128]{2,1,0:T(8,128)(2,1)S(1)}, bf16[16,360,128]{2,1,0:T(8,128)(2,1)}, u32[]{:S(2)}) copy-start(bf16[16,360,128]{2,1,0:T(8,128)(2,1)} %param.5) | copy-start | bytes 4423684
  13.7 5.5 %copy-start.5 = (s32[128]{0:T(128)S(1)}, s32[128]{0:T(128)}, u32[]{:S(2)}) copy-start(s32[128]{0:T(128)} %param.7) | copy-start | bytes 1540
  13.7 9.1 %collective-permute-start.2 = (bf16[8,360,256]{2,1,0:T(8,128)(2,1)}, bf16[8,360,256]{2,1,0:T(8,128)(2,1)}, u32[]{:S(2)}, u32[]{:S(2)}) collective-permute-start(bf16[8,360,256]{2,1,0:T(8,128)(2,1)} %pad_maximum_fusion), channel_id=1, source_target_pairs={{0,1},{1,0},{2,3},{3,2},{4,5},{5,4},{6,7},{7,6},{24,25},{25,24},{2... | collective-permute-start | bytes 4423688 | tf_op jit(solution)/shard_map/ppermute | solution.py:538
  16.2 3.2 %copy-start.2 = (bf16[5,384,256]{2,1,0:T(8,128)(2,1)S(1)}, bf16[5,384,256]{2,1,0:T(8,128)(2,1)}, u32[]{:S(2)}) copy-start(bf16[5,384,256]{2,1,0:T(8,128)(2,1)} %get-tuple-element.86) | copy-start | bytes 2949124
  16.2 6.6 %copy-start.4 = (bf16[1,384,128]{2,1,0:T(8,128)(2,1)S(1)}, bf16[1,384,128]{2,1,0:T(8,128)(2,1)}, u32[]{:S(2)}) copy-start(bf16[1,384,128]{2,1,0:T(8,128)(2,1)} %copy-done.3) | copy-start | bytes 294916
  17.8 6.6 %collective-permute-start.5 = (bf16[4,360,256]{2,1,0:T(8,128)(2,1)S(1)}, bf16[4,360,256]{2,1,0:T(8,128)(2,1)S(1)}, u32[]{:S(2)}, u32[]{:S(2)}) collective-permute-start(bf16[4,360,256]{2,1,0:T(8,128)(2,1)S(1)} %get-tuple-element.42.own_ref), channel_id=1, source_target_pairs={{0,2},{1,3},{2,0},{3,1},{4,6},{5,7},{6,4},{7,5},{24,26},{25,27},{2... | collective-permute-start | bytes 2211848 | tf_op jit(solution)/shard_map/ppermute | solution.py:538
  18.5 4.3 %collective-permute-start.4 = (bf16[4,360,256]{2,1,0:T(8,128)(2,1)}, bf16[4,360,256]{2,1,0:T(8,128)(2,1)S(1)}, u32[]{:S(2)}, u32[]{:S(2)}) collective-permute-start(bf16[4,360,256]{2,1,0:T(8,128)(2,1)} %collective-permute-done.3.opp_ref), channel_id=1, source_target_pairs={{0,1},{1,0},{2,3},{3,2},{4,5},{5,4},{6,7},{7,6},{24,25},{25,24},{2... | collective-permute-start | bytes 2211848 | tf_op jit(solution)/shard_map/ppermute | solution.py:538
  19.4 22.5 %collective-permute-start.9 = (bf16[5,384,256]{2,1,0:T(8,128)(2,1)S(1)}, bf16[5,384,256]{2,1,0:T(8,128)(2,1)S(1)}, u32[]{:S(2)}, u32[]{:S(2)}) collective-permute-start(bf16[5,384,256]{2,1,0:T(8,128)(2,1)S(1)} %copy-done.2), channel_id=1, source_target_pairs={{8,4},{9,5},{10,6},{11,7},{12,8},{13,9},{14,10},{15,11},{16,20},{1... | collective-permute-start | bytes 2949128 | tf_op jit(solution)/shard_map/ppermute | solution.py:538
  22.8 38.5 %slice-start = ((s8[5898240]{0:T(1024)(128)(4,1)}), s8[4194304]{0:T(1024)(128)(4,1)S(1)}, s32[]{:S(2)}) async-start(s8[5898240]{0:T(1024)(128)(4,1)} %bitcast.6), calls=%async_computation | async-start | bytes 8388608
  24.4 3.8 %collective-permute-start.6 = (bf16[4,360,256]{2,1,0:T(8,128)(2,1)S(1)}, bf16[4,360,256]{2,1,0:T(8,128)(2,1)S(1)}, u32[]{:S(2)}, u32[]{:S(2)}) collective-permute-start(bf16[4,360,256]{2,1,0:T(8,128)(2,1)S(1)} %collective-permute-done.5.opp_ref), channel_id=1, source_target_pairs={{0,1},{1,0},{2,3},{3,2},{4,5},{5,4},{6,7},{7,6},{24,25},{25,24},{2... | collective-permute-start | bytes 2211848 | tf_op jit(solution)/shard_map/ppermute | solution.py:538
  25.2 18.2 %collective-permute-start.7 = (bf16[8,360,256]{2,1,0:T(8,128)(2,1)S(1)}, bf16[8,360,256]{2,1,0:T(8,128)(2,1)S(1)}, u32[]{:S(2)}, u32[]{:S(2)}) collective-permute-start(bf16[8,360,256]{2,1,0:T(8,128)(2,1)S(1)} %pad_maximum_fusion.1.own_ref), channel_id=1, source_target_pairs={{0,2},{1,3},{2,0},{3,1},{4,6},{5,7},{6,4},{7,5},{24,26},{25,27},{2... | collective-permute-start | bytes 4423688 | tf_op jit(solution)/shard_map/ppermute | solution.py:538
  26.0 32.1 %collective-permute-start.11 = (bf16[5,384,256]{2,1,0:T(8,128)(2,1)S(1)}, bf16[5,384,256]{2,1,0:T(8,128)(2,1)S(1)}, u32[]{:S(2)}, u32[]{:S(2)}) collective-permute-start(bf16[5,384,256]{2,1,0:T(8,128)(2,1)S(1)} %copy-done.1), channel_id=1, source_target_pairs={{8,12},{9,13},{10,14},{11,15},{20,16},{21,17},{22,18},{23,19}} | collective-permute-start | bytes 2949128 | tf_op jit(solution)/shard_map/ppermute | solution.py:538
  27.3 34.0 %slice-start.1 = ((s8[5898240]{0:T(1024)(128)(4,1)}), s8[1703936]{0:T(1024)(128)(4,1)S(1)}, s32[]{:S(2)}) async-start(s8[5898240]{0:T(1024)(128)(4,1)} %bitcast.6), calls=%async_computation.1 | async-start | bytes 3407872
  27.3 30.8 %collective-permute-start.8 = (bf16[5,384,256]{2,1,0:T(8,128)(2,1)S(1)}, bf16[5,384,256]{2,1,0:T(8,128)(2,1)S(1)}, u32[]{:S(2)}, u32[]{:S(2)}) collective-permute-start(bf16[5,384,256]{2,1,0:T(8,128)(2,1)S(1)} %get-tuple-element.50), channel_id=1, source_target_pairs={{4,0},{5,1},{6,2},{7,3},{24,28},{25,29},{26,30},{27,31}} | collective-permute-start | bytes 2949128 | tf_op jit(solution)/shard_map/ppermute | solution.py:538
  41.9 16.2 %collective-permute-start.10 = (bf16[5,384,256]{2,1,0:T(8,128)(2,1)S(1)}, bf16[5,384,256]{2,1,0:T(8,128)(2,1)S(1)}, u32[]{:S(2)}, u32[]{:S(2)}) collective-permute-start(bf16[5,384,256]{2,1,0:T(8,128)(2,1)S(1)} %get-tuple-element.52), channel_id=1, source_target_pairs={{0,4},{1,5},{2,6},{3,7},{4,8},{5,9},{6,10},{7,11},{24,20},{25,21},... | collective-permute-start | bytes 2949128 | tf_op jit(solution)/shard_map/ppermute | solution.py:538
  42.6 18.2 %collective-permute-start.12 = (bf16[8,360,256]{2,1,0:T(8,128)(2,1)S(1)}, bf16[8,360,256]{2,1,0:T(8,128)(2,1)S(1)}, u32[]{:S(2)}, u32[]{:S(2)}) collective-permute-start(bf16[8,360,256]{2,1,0:T(8,128)(2,1)S(1)} %pad_maximum_fusion.1.own_ref), channel_id=1, source_target_pairs={{0,1},{1,0},{2,3},{3,2},{4,5},{5,4},{6,7},{7,6},{24,25},{25,24},{2... | collective-permute-start | bytes 4423688 | tf_op jit(solution)/shard_map/ppermute | solution.py:538
  58.1 2.7 %collective-permute-start.13 = (bf16[8,360,256]{2,1,0:T(8,128)(2,1)S(1)}, bf16[8,360,256]{2,1,0:T(8,128)(2,1)S(1)}, u32[]{:S(2)}, u32[]{:S(2)}) collective-permute-start(bf16[8,360,256]{2,1,0:T(8,128)(2,1)S(1)} %collective-permute-done.7.opp_ref), channel_id=1, source_target_pairs={{0,1},{1,0},{2,3},{3,2},{4,5},{5,4},{6,7},{7,6},{24,25},{25,24},{2... | collective-permute-start | bytes 4423688 | tf_op jit(solution)/shard_map/ppermute | solution.py:538
  58.9 32.3 %collective-permute-start.14 = (bf16[5,384,256]{2,1,0:T(8,128)(2,1)S(1)}, bf16[5,384,256]{2,1,0:T(8,128)(2,1)S(1)}, u32[]{:S(2)}, u32[]{:S(2)}) collective-permute-start(bf16[5,384,256]{2,1,0:T(8,128)(2,1)S(1)} %copy-done.1), channel_id=1, source_target_pairs={{12,16},{13,17},{14,18},{15,19},{16,12},{17,13},{18,14},{19,15}} | collective-permute-start | bytes 2949128 | tf_op jit(solution)/shard_map/ppermute | solution.py:538
  67.7 48.7 %collective-permute-start.15 = (bf16[4,384,256]{2,1,0:T(8,128)(2,1)S(1)}, bf16[4,384,256]{2,1,0:T(8,128)(2,1)S(1)}, u32[]{:S(2)}, u32[]{:S(2)}) collective-permute-start(bf16[4,384,256]{2,1,0:T(8,128)(2,1)S(1)} %get-tuple-element.63), channel_id=1, source_target_pairs={{4,0},{5,1},{6,2},{7,3},{8,4},{9,5},{10,6},{11,7},{12,8},{13,9},{1... | collective-permute-start | bytes 2359304 | tf_op jit(solution)/shard_map/ppermute | solution.py:538
  97.5 20.5 %collective-permute-start.16 = (bf16[4,384,256]{2,1,0:T(8,128)(2,1)S(1)}, bf16[4,384,256]{2,1,0:T(8,128)(2,1)S(1)}, u32[]{:S(2)}, u32[]{:S(2)}) collective-permute-start(bf16[4,384,256]{2,1,0:T(8,128)(2,1)S(1)} %get-tuple-element.64), channel_id=1, source_target_pairs={{12,16},{13,17},{14,18},{15,19},{16,12},{17,13},{18,14},{19,15}} | collective-permute-start | bytes 2359304 | tf_op jit(solution)/shard_map/ppermute | solution.py:538
  99.4 37.2 %collective-permute-start.17 = (bf16[4,384,256]{2,1,0:T(8,128)(2,1)S(1)}, bf16[4,384,256]{2,1,0:T(8,128)(2,1)S(1)}, u32[]{:S(2)}, u32[]{:S(2)}) collective-permute-start(bf16[4,384,256]{2,1,0:T(8,128)(2,1)S(1)} %get-tuple-element.64), channel_id=1, source_target_pairs={{0,4},{1,5},{2,6},{3,7},{4,8},{5,9},{6,10},{7,11},{8,12},{9,13},{1... | collective-permute-start | bytes 2359304 | tf_op jit(solution)/shard_map/ppermute | solution.py:538
  (3 other events, 8.1 us)

commit v5 on v4

--- a/solution.py
+++ b/solution.py
@@ -16,7 +16,7 @@
 MIB = 1024 * 1024
 ODD, POLAR, OUTER_FROM, INNER_FROM, ZERO, LOW_HALF = range(6)
 PAD = 8
-COLS = 48
+COLS = 32
 
 
 def tie(*values):

time: 143 us -> 143 us (level)
  no operation moved by 1% of the time
where the time goes in v5:
time: 143 us; the launch traced here: 142 us
  starting transfers between devices  42.9 us (30%)
  Pallas kernels  42.4 us (30%)
  waiting for transfers between devices  42.2 us (30%)
  local copies, waits for them, and re-layouts  8.37 us (6%)
  other arithmetic  5.38 us (4%)
    ppermute x16, waiting for transfers between devices, move(): return lax.ppermute(cells, axes, pairs)  42.2 us
    ppermute x16, starting transfers between devices, move(): return lax.ppermute(cells, axes, pairs)  42.1 us
    pallas_call x1, Pallas kernels, interior(): pl.pallas_call(functools.partial(interior_kernel, rows, lon, ext), in_spe...  15.7 us
    pallas_call x2, Pallas kernels, border_rows(): pl.pallas_call(functools.partial(border_kernel, outer, rows, lon, ext), i...  12.5 us
    pallas_call x2, Pallas kernels, finish(): pl.pallas_call(functools.partial(finish_kernel, outer, rows, lon, ext), i...  10.4 us
    convert_element_type x1, local copies, waits for them, and re-layouts, per_device(): rows_of(cells, i).astype(jnp.bfloat16)  4.25 us
    pallas_call x4, Pallas kernels, smooth_piece(): pl.pallas_call(functools.partial(smooth_kernel, geo, len(extras)), grid=(...  3.76 us
  transfers between devices with their start and end apart: 18, of which 4 were waited for; matrix products, arithmetic and copies ran while one was open for 8% of the time, Pallas kernels for 26%

profile of v5, /device:TPU:21, one launch (start us, length us, event | category | flops | bytes accessed | tf_op | source)
XLA Modules:
  0.0 141.9 jit_solution(1484903965089619699)
XLA Ops:
  2.6 1.4 %dynamic-slice_convert_fusion.4.own_ref = bf16[4,360,256]{2,1,0:T(8,128)(2,1)S(1)} fusion(f32[16,360,256]{2,1,0:T(8,128)} %state_ref.5, s32[]{:T(128)S(6)} %select_n.73), kind=kLoop, calls=%fused_computation.7 | loop fusion | bytes 1474564 | tf_op jit(solution)/shard_map/convert_element_type | solution.py:569
  4.1 1.5 %collective-permute-start.3 = (bf16[4,360,256]{2,1,0:T(8,128)(2,1)S(1)}, bf16[4,360,256]{2,1,0:T(8,128)(2,1)}, u32[]{:S(2)}, u32[]{:S(2)}) collective-permute-start(bf16[4,360,256]{2,1,0:T(8,128)(2,1)S(1)} %dynamic-slice_convert_fusion.4.own_ref), channel_id=1, source_target_pairs={{0,2},{1,3},{2,0},{3,1},{4,6},{5,7},{6,4},{7,5},{24,26},{25,27},{2... | collective-permute-start | bytes 2211848 | tf_op jit(solution)/shard_map/ppermute | solution.py:538
  5.8 4.2 %dynamic-slice_convert_fusion.1 = (bf16[4,360,256]{2,1,0:T(8,128)(2,1)}, bf16[4,360,256]{2,1,0:T(8,128)(2,1)}, bf16[4,360,256]{2,1,0:T(8,128)(2,1)S(1)}, bf16[4,360,256]{2,1,0:T(8,128)(2,1)S(1)}) fusion(f32[16,360,256]{2,1,0:T(8,128)} %state_ref.5, s32[]{:T(128)S(6)} %select_n.76, s32[]{:T(128)S(6)} %select_n.77, s32[]{:T(128)S(6)} %select_n.73, s32[]{:T(128)S(6)} %select_n.69), kind=kLoop, calls=%fused_computation.4 | loop fusion | bytes 5898256 | tf_op jit(solution)/shard_map/convert_element_type | solution.py:572
  10.7 1.8 %maximum_maximum_fusion.2 = (bf16[5,384,256]{2,1,0:T(8,128)(2,1)}, bf16[5,384,256]{2,1,0:T(8,128)(2,1)}) fusion(bf16[1,384,128]{2,1,0:T(8,128)(2,1)S(1)} %get-tuple-element.77, bf16[1,384,128]{2,1,0:T(8,128)(2,1)S(1)} %get-tuple-element.75, bf16[4,8,256]{2,1,0:T(8,128)(2,1)S(1)} %get-tuple-element.83, bf16[4,360,256]{2,1,0:T(8,128)(2,1)S(1)} %get-tuple-element.42.own_ref, ...), kind=kLoop, calls=%fused_computation.9 | loop fusion | flops 11304960 | bytes 3903232 | tf_op jit(solution)/shard_map/concatenate | solution.py:585
  12.4 1.2 pad_maximum_fusion
  13.7 1.9 %collective-permute-start.2 = (bf16[8,360,256]{2,1,0:T(8,128)(2,1)}, bf16[8,360,256]{2,1,0:T(8,128)(2,1)}, u32[]{:S(2)}, u32[]{:S(2)}) collective-permute-start(bf16[8,360,256]{2,1,0:T(8,128)(2,1)} %pad_maximum_fusion), channel_id=1, source_target_pairs={{0,1},{1,0},{2,3},{3,2},{4,5},{5,4},{6,7},{7,6},{24,25},{25,24},{2... | collective-permute-start | bytes 4423688 | tf_op jit(solution)/shard_map/ppermute | solution.py:538
  16.2 1.6 %pad_maximum_fusion.1.own_ref = bf16[8,360,256]{2,1,0:T(8,128)(2,1)S(1)} fusion(bf16[4,360,256]{2,1,0:T(8,128)(2,1)} %get-tuple-element.70, bf16[4,360,256]{2,1,0:T(8,128)(2,1)} %get-tuple-element.69), kind=kLoop, calls=%fused_computation.2 | loop fusion | flops 737280 | bytes 2949120 | tf_op jit(solution)/shard_map/concatenate | solution.py:617
  19.4 3.2 %collective-permute-start.9 = (bf16[5,384,256]{2,1,0:T(8,128)(2,1)S(1)}, bf16[5,384,256]{2,1,0:T(8,128)(2,1)S(1)}, u32[]{:S(2)}, u32[]{:S(2)}) collective-permute-start(bf16[5,384,256]{2,1,0:T(8,128)(2,1)S(1)} %copy-done.2), channel_id=1, source_target_pairs={{8,4},{9,5},{10,6},{11,7},{12,8},{13,9},{14,10},{15,11},{16,20},{1... | collective-permute-start | bytes 2949128 | tf_op jit(solution)/shard_map/ppermute | solution.py:538
  22.9 1.5 %smooth.4 = (f32[4,2,384,128]{3,2,1,0:T(8,128)S(1)}, bf16[5,384,256]{2,1,0:T(8,128)(2,1)S(1)}) custom-call(s32[6]{0:T(128)S(1)} %stack.39.info_ref, s32[4]{0:T(128)S(1)} %get-tuple-element.92.widths_ref, bf16[4,360,256]{2,1,0:T(8,128)(2,1)S(1)} %dynamic-slice_convert_fusion.4.own_ref, bf16[8,360,256]{2,1,0:T(8,128)(2,1)} %collective-permute-done.2.sib_ref, ...), custom_call_target="tpu_custom_call" | custom-call | flops 1000 | bytes 1000 | tf_op jit(solution)/shard_map/smooth/pallas_call | solution.py:139
  26.0 1.3 collective-permute-start.11
  28.2 1.1 smooth.5
  29.4 12.5 %collective-permute-done.9.raw_ref = bf16[5,384,256]{2,1,0:T(8,128)(2,1)S(1)} collective-permute-done((bf16[5,384,256]{2,1,0:T(8,128)(2,1)S(1)}, bf16[5,384,256]{2,1,0:T(8,128)(2,1)S(1)}, u32[]{:S(2)}, u32[]{:S(2)}) %collective-permute-start.9) | collective-permute-done | bytes 983072 | tf_op jit(solution)/shard_map/ppermute | solution.py:538
  43.4 14.7 %collective-permute-done.11.raw_ref.across_ref.across_raw_ref = bf16[5,384,256]{2,1,0:T(8,128)(2,1)S(1)} collective-permute-done((bf16[5,384,256]{2,1,0:T(8,128)(2,1)S(1)}, bf16[5,384,256]{2,1,0:T(8,128)(2,1)S(1)}, u32[]{:S(2)}, u32[]{:S(2)}) %collective-permute-start.11) | collective-permute-done | bytes 983072 | tf_op jit(solution)/shard_map/ppermute | solution.py:538
  58.9 1.9 %collective-permute-start.14 = (bf16[5,384,256]{2,1,0:T(8,128)(2,1)S(1)}, bf16[5,384,256]{2,1,0:T(8,128)(2,1)S(1)}, u32[]{:S(2)}, u32[]{:S(2)}) collective-permute-start(bf16[5,384,256]{2,1,0:T(8,128)(2,1)S(1)} %copy-done.1), channel_id=1, source_target_pairs={{12,16},{13,17},{14,18},{15,19},{16,12},{17,13},{18,14},{19,15}} | collective-permute-start | bytes 2949128 | tf_op jit(solution)/shard_map/ppermute | solution.py:538
  61.4 6.3 %border_outer.1 = (bf16[4,384,256]{2,1,0:T(8,128)(2,1)S(1)}, f32[4,2,384,128]{3,2,1,0:T(8,128)S(1)}, f32[4,2,384,128]{3,2,1,0:T(8,128)S(1)}) custom-call(s32[6]{0:T(128)S(1)} %stack.39.info_ref, f32[16,360,256]{2,1,0:T(8,128)S(1)} %bitcast.7, bf16[16,8,256]{2,1,0:T(8,128)(2,1)S(1)} %slice.48.edge_w_ref, bf16[16,8,256]{2,1,0:T(8,128)(2,1)S(1)} %slice.49.edge_e_ref, ...), custom_call_target="tpu_custom_call" | custom-call | flops 1000 | bytes 1000 | tf_op jit(solution)/shard_map/border_outer/pallas_call | solution.py:332
  67.7 22.9 %collective-permute-start.15 = (bf16[4,384,256]{2,1,0:T(8,128)(2,1)S(1)}, bf16[4,384,256]{2,1,0:T(8,128)(2,1)S(1)}, u32[]{:S(2)}, u32[]{:S(2)}) collective-permute-start(bf16[4,384,256]{2,1,0:T(8,128)(2,1)S(1)} %get-tuple-element.63), channel_id=1, source_target_pairs={{4,0},{5,1},{6,2},{7,3},{8,4},{9,5},{10,6},{11,7},{12,8},{13,9},{1... | collective-permute-start | bytes 2359304 | tf_op jit(solution)/shard_map/ppermute | solution.py:538
  91.2 6.3 %border_inner.1 = (bf16[4,384,256]{2,1,0:T(8,128)(2,1)S(1)}, f32[4,2,384,128]{3,2,1,0:T(8,128)S(1)}, f32[4,2,384,128]{3,2,1,0:T(8,128)S(1)}) custom-call(s32[6]{0:T(128)S(1)} %stack.39.info_ref, f32[16,360,256]{2,1,0:T(8,128)S(1)} %bitcast.7, bf16[16,8,256]{2,1,0:T(8,128)(2,1)S(1)} %slice.48.edge_w_ref, bf16[16,8,256]{2,1,0:T(8,128)(2,1)S(1)} %slice.49.edge_e_ref, ...), custom_call_target="tpu_custom_call" | custom-call | flops 1000 | bytes 1000 | tf_op jit(solution)/shard_map/border_inner/pallas_call | solution.py:332
  97.5 1.9 %collective-permute-start.16 = (bf16[4,384,256]{2,1,0:T(8,128)(2,1)S(1)}, bf16[4,384,256]{2,1,0:T(8,128)(2,1)S(1)}, u32[]{:S(2)}, u32[]{:S(2)}) collective-permute-start(bf16[4,384,256]{2,1,0:T(8,128)(2,1)S(1)} %get-tuple-element.64), channel_id=1, source_target_pairs={{12,16},{13,17},{14,18},{15,19},{16,12},{17,13},{18,14},{19,15}} | collective-permute-start | bytes 2359304 | tf_op jit(solution)/shard_map/ppermute | solution.py:538
  99.4 1.3 collective-permute-start.17
  100.7 15.7 %interior.1 = (bf16[16,360,256]{2,1,0:T(8,128)(2,1)}, f32[4,2,384,128]{3,2,1,0:T(8,128)S(1)}, f32[4,2,384,128]{3,2,1,0:T(8,128)S(1)}) custom-call(s32[6]{0:T(128)S(1)} %stack.39.info_ref, f32[16,360,256]{2,1,0:T(8,128)S(1)} %bitcast.7, bf16[16,8,256]{2,1,0:T(8,128)(2,1)S(1)} %slice.48.edge_w_ref, bf16[16,8,256]{2,1,0:T(8,128)(2,1)S(1)} %slice.49.edge_e_ref, ...), custom_call_target="tpu_custom_call" | custom-call | flops 1000 | bytes 1000 | tf_op jit(solution)/shard_map/interior/pallas_call | solution.py:421
  116.4 1.5 %collective-permute-done.16.across_ref = bf16[4,384,256]{2,1,0:T(8,128)(2,1)S(1)} collective-permute-done((bf16[4,384,256]{2,1,0:T(8,128)(2,1)S(1)}, bf16[4,384,256]{2,1,0:T(8,128)(2,1)S(1)}, u32[]{:S(2)}, u32[]{:S(2)}) %collective-permute-start.16) | collective-permute-done | bytes 786464 | tf_op jit(solution)/shard_map/ppermute | solution.py:538
  117.9 5.2 %finish_inner.1._ = bf16[16,360,256]{2,1,0:T(8,128)(2,1)} custom-call(bf16[16,360,256]{2,1,0:T(8,128)(2,1)} %get-tuple-element.62._, s32[6]{0:T(128)S(1)} %stack.39.info_ref, bf16[16,384,128]{2,1,0:T(8,128)(2,1)S(1)} %maximum_maximum_fusion.winds_ref, bf16[5,384,256]{2,1,0:T(8,128)(2,1)S(1)} %collective-permute-done.8.late_ref, ...), custom_call_target="tpu_custom_call", output_to_operand_aliasing={{}: (0, {})} | custom-call | flops 1000 | bytes 1000 | tf_op jit(solution)/shard_map/finish_inner/pallas_call | solution.py:478
  123.1 13.4 %collective-permute-done.17.border_ref.across_ref = bf16[4,384,256]{2,1,0:T(8,128)(2,1)S(1)} collective-permute-done((bf16[4,384,256]{2,1,0:T(8,128)(2,1)S(1)}, bf16[4,384,256]{2,1,0:T(8,128)(2,1)S(1)}, u32[]{:S(2)}, u32[]{:S(2)}) %collective-permute-start.17) | collective-permute-done | bytes 786464 | tf_op jit(solution)/shard_map/ppermute | solution.py:538
  136.6 5.2 %finish_outer.1 = bf16[16,360,256]{2,1,0:T(8,128)(2,1)} custom-call(bf16[16,360,256]{2,1,0:T(8,128)(2,1)} %finish_inner.1._, s32[6]{0:T(128)S(1)} %stack.39.info_ref, bf16[16,384,128]{2,1,0:T(8,128)(2,1)S(1)} %maximum_maximum_fusion.winds_ref, bf16[5,384,256]{2,1,0:T(8,128)(2,1)S(1)} %collective-permute-done.10.late_ref, ...), custom_call_target="tpu_custom_call", output_to_operand_aliasing={{}: (0, {})} | custom-call | flops 1000 | bytes 1000 | tf_op jit(solution)/shard_map/finish_outer/pallas_call | solution.py:478
  (74 shorter events, 11.6 us)
Async XLA Ops:
  1.8 8.2 %collective-permute-start = (bf16[16,8,384]{2,1,0:T(8,128)(2,1)S(1)}, bf16[16,8,384]{2,1,0:T(8,128)(2,1)S(1)}, u32[]{:S(2)}, u32[]{:S(2)}) collective-permute-start(bf16[16,8,384]{2,1,0:T(8,128)(2,1)S(1)} %get-tuple-element.38), channel_id=1, source_target_pairs={{0,1},{1,2},{2,3},{3,0},{4,5},{5,6},{6,7},{7,4},{8,9},{9,10},{10,1... | collective-permute-start | bytes 294920 | tf_op jit(solution)/shard_map/ppermute | solution.py:566
  2.6 7.4 %collective-permute-start.1 = (bf16[16,8,384]{2,1,0:T(8,128)(2,1)S(1)}, bf16[16,8,384]{2,1,0:T(8,128)(2,1)S(1)}, u32[]{:S(2)}, u32[]{:S(2)}) collective-permute-start(bf16[16,8,384]{2,1,0:T(8,128)(2,1)S(1)} %get-tuple-element.39), channel_id=1, source_target_pairs={{1,0},{2,1},{3,2},{0,3},{5,4},{6,5},{7,6},{4,7},{9,8},{10,9},{11,1... | collective-permute-start | bytes 294920 | tf_op jit(solution)/shard_map/ppermute | solution.py:565
  4.1 14.4 %collective-permute-start.3 = (bf16[4,360,256]{2,1,0:T(8,128)(2,1)S(1)}, bf16[4,360,256]{2,1,0:T(8,128)(2,1)}, u32[]{:S(2)}, u32[]{:S(2)}) collective-permute-start(bf16[4,360,256]{2,1,0:T(8,128)(2,1)S(1)} %dynamic-slice_convert_fusion.4.own_ref), channel_id=1, source_target_pairs={{0,2},{1,3},{2,0},{3,1},{4,6},{5,7},{6,4},{7,5},{24,26},{25,27},{2... | collective-permute-start | bytes 2211848 | tf_op jit(solution)/shard_map/ppermute | solution.py:538
  5.8 4.4 %copy-start = (bf16[16,360,128]{2,1,0:T(8,128)(2,1)S(1)}, bf16[16,360,128]{2,1,0:T(8,128)(2,1)}, u32[]{:S(2)}) copy-start(bf16[16,360,128]{2,1,0:T(8,128)(2,1)} %param.5) | copy-start | bytes 4423684
  13.7 5.5 %copy-start.5 = (s32[128]{0:T(128)S(1)}, s32[128]{0:T(128)}, u32[]{:S(2)}) copy-start(s32[128]{0:T(128)} %param.7) | copy-start | bytes 1540
  13.7 9.1 %collective-permute-start.2 = (bf16[8,360,256]{2,1,0:T(8,128)(2,1)}, bf16[8,360,256]{2,1,0:T(8,128)(2,1)}, u32[]{:S(2)}, u32[]{:S(2)}) collective-permute-start(bf16[8,360,256]{2,1,0:T(8,128)(2,1)} %pad_maximum_fusion), channel_id=1, source_target_pairs={{0,1},{1,0},{2,3},{3,2},{4,5},{5,4},{6,7},{7,6},{24,25},{25,24},{2... | collective-permute-start | bytes 4423688 | tf_op jit(solution)/shard_map/ppermute | solution.py:538
  16.2 3.2 %copy-start.2 = (bf16[5,384,256]{2,1,0:T(8,128)(2,1)S(1)}, bf16[5,384,256]{2,1,0:T(8,128)(2,1)}, u32[]{:S(2)}) copy-start(bf16[5,384,256]{2,1,0:T(8,128)(2,1)} %get-tuple-element.86) | copy-start | bytes 2949124
  16.2 6.6 %copy-start.4 = (bf16[1,384,128]{2,1,0:T(8,128)(2,1)S(1)}, bf16[1,384,128]{2,1,0:T(8,128)(2,1)}, u32[]{:S(2)}) copy-start(bf16[1,384,128]{2,1,0:T(8,128)(2,1)} %copy-done.3) | copy-start | bytes 294916
  17.8 6.6 %collective-permute-start.5 = (bf16[4,360,256]{2,1,0:T(8,128)(2,1)S(1)}, bf16[4,360,256]{2,1,0:T(8,128)(2,1)S(1)}, u32[]{:S(2)}, u32[]{:S(2)}) collective-permute-start(bf16[4,360,256]{2,1,0:T(8,128)(2,1)S(1)} %get-tuple-element.42.own_ref), channel_id=1, source_target_pairs={{0,2},{1,3},{2,0},{3,1},{4,6},{5,7},{6,4},{7,5},{24,26},{25,27},{2... | collective-permute-start | bytes 2211848 | tf_op jit(solution)/shard_map/ppermute | solution.py:538
  18.5 4.3 %collective-permute-start.4 = (bf16[4,360,256]{2,1,0:T(8,128)(2,1)}, bf16[4,360,256]{2,1,0:T(8,128)(2,1)S(1)}, u32[]{:S(2)}, u32[]{:S(2)}) collective-permute-start(bf16[4,360,256]{2,1,0:T(8,128)(2,1)} %collective-permute-done.3.opp_ref), channel_id=1, source_target_pairs={{0,1},{1,0},{2,3},{3,2},{4,5},{5,4},{6,7},{7,6},{24,25},{25,24},{2... | collective-permute-start | bytes 2211848 | tf_op jit(solution)/shard_map/ppermute | solution.py:538
  19.4 22.5 %collective-permute-start.9 = (bf16[5,384,256]{2,1,0:T(8,128)(2,1)S(1)}, bf16[5,384,256]{2,1,0:T(8,128)(2,1)S(1)}, u32[]{:S(2)}, u32[]{:S(2)}) collective-permute-start(bf16[5,384,256]{2,1,0:T(8,128)(2,1)S(1)} %copy-done.2), channel_id=1, source_target_pairs={{8,4},{9,5},{10,6},{11,7},{12,8},{13,9},{14,10},{15,11},{16,20},{1... | collective-permute-start | bytes 2949128 | tf_op jit(solution)/shard_map/ppermute | solution.py:538
  22.8 38.5 %slice-start = ((s8[5898240]{0:T(1024)(128)(4,1)}), s8[4194304]{0:T(1024)(128)(4,1)S(1)}, s32[]{:S(2)}) async-start(s8[5898240]{0:T(1024)(128)(4,1)} %bitcast.6), calls=%async_computation | async-start | bytes 8388608
  24.4 3.8 %collective-permute-start.6 = (bf16[4,360,256]{2,1,0:T(8,128)(2,1)S(1)}, bf16[4,360,256]{2,1,0:T(8,128)(2,1)S(1)}, u32[]{:S(2)}, u32[]{:S(2)}) collective-permute-start(bf16[4,360,256]{2,1,0:T(8,128)(2,1)S(1)} %collective-permute-done.5.opp_ref), channel_id=1, source_target_pairs={{0,1},{1,0},{2,3},{3,2},{4,5},{5,4},{6,7},{7,6},{24,25},{25,24},{2... | collective-permute-start | bytes 2211848 | tf_op jit(solution)/shard_map/ppermute | solution.py:538
  25.2 18.2 %collective-permute-start.7 = (bf16[8,360,256]{2,1,0:T(8,128)(2,1)S(1)}, bf16[8,360,256]{2,1,0:T(8,128)(2,1)S(1)}, u32[]{:S(2)}, u32[]{:S(2)}) collective-permute-start(bf16[8,360,256]{2,1,0:T(8,128)(2,1)S(1)} %pad_maximum_fusion.1.own_ref), channel_id=1, source_target_pairs={{0,2},{1,3},{2,0},{3,1},{4,6},{5,7},{6,4},{7,5},{24,26},{25,27},{2... | collective-permute-start | bytes 4423688 | tf_op jit(solution)/shard_map/ppermute | solution.py:538
  26.0 32.1 %collective-permute-start.11 = (bf16[5,384,256]{2,1,0:T(8,128)(2,1)S(1)}, bf16[5,384,256]{2,1,0:T(8,128)(2,1)S(1)}, u32[]{:S(2)}, u32[]{:S(2)}) collective-permute-start(bf16[5,384,256]{2,1,0:T(8,128)(2,1)S(1)} %copy-done.1), channel_id=1, source_target_pairs={{8,12},{9,13},{10,14},{11,15},{20,16},{21,17},{22,18},{23,19}} | collective-permute-start | bytes 2949128 | tf_op jit(solution)/shard_map/ppermute | solution.py:538
  27.3 34.0 %slice-start.1 = ((s8[5898240]{0:T(1024)(128)(4,1)}), s8[1703936]{0:T(1024)(128)(4,1)S(1)}, s32[]{:S(2)}) async-start(s8[5898240]{0:T(1024)(128)(4,1)} %bitcast.6), calls=%async_computation.1 | async-start | bytes 3407872
  27.3 30.8 %collective-permute-start.8 = (bf16[5,384,256]{2,1,0:T(8,128)(2,1)S(1)}, bf16[5,384,256]{2,1,0:T(8,128)(2,1)S(1)}, u32[]{:S(2)}, u32[]{:S(2)}) collective-permute-start(bf16[5,384,256]{2,1,0:T(8,128)(2,1)S(1)} %get-tuple-element.50), channel_id=1, source_target_pairs={{4,0},{5,1},{6,2},{7,3},{24,28},{25,29},{26,30},{27,31}} | collective-permute-start | bytes 2949128 | tf_op jit(solution)/shard_map/ppermute | solution.py:538
  41.9 16.2 %collective-permute-start.10 = (bf16[5,384,256]{2,1,0:T(8,128)(2,1)S(1)}, bf16[5,384,256]{2,1,0:T(8,128)(2,1)S(1)}, u32[]{:S(2)}, u32[]{:S(2)}) collective-permute-start(bf16[5,384,256]{2,1,0:T(8,128)(2,1)S(1)} %get-tuple-element.52), channel_id=1, source_target_pairs={{0,4},{1,5},{2,6},{3,7},{4,8},{5,9},{6,10},{7,11},{24,20},{25,21},... | collective-permute-start | bytes 2949128 | tf_op jit(solution)/shard_map/ppermute | solution.py:538
  42.6 18.2 %collective-permute-start.12 = (bf16[8,360,256]{2,1,0:T(8,128)(2,1)S(1)}, bf16[8,360,256]{2,1,0:T(8,128)(2,1)S(1)}, u32[]{:S(2)}, u32[]{:S(2)}) collective-permute-start(bf16[8,360,256]{2,1,0:T(8,128)(2,1)S(1)} %pad_maximum_fusion.1.own_ref), channel_id=1, source_target_pairs={{0,1},{1,0},{2,3},{3,2},{4,5},{5,4},{6,7},{7,6},{24,25},{25,24},{2... | collective-permute-start | bytes 4423688 | tf_op jit(solution)/shard_map/ppermute | solution.py:538
  58.1 2.7 %collective-permute-start.13 = (bf16[8,360,256]{2,1,0:T(8,128)(2,1)S(1)}, bf16[8,360,256]{2,1,0:T(8,128)(2,1)S(1)}, u32[]{:S(2)}, u32[]{:S(2)}) collective-permute-start(bf16[8,360,256]{2,1,0:T(8,128)(2,1)S(1)} %collective-permute-done.7.opp_ref), channel_id=1, source_target_pairs={{0,1},{1,0},{2,3},{3,2},{4,5},{5,4},{6,7},{7,6},{24,25},{25,24},{2... | collective-permute-start | bytes 4423688 | tf_op jit(solution)/shard_map/ppermute | solution.py:538
  58.9 32.3 %collective-permute-start.14 = (bf16[5,384,256]{2,1,0:T(8,128)(2,1)S(1)}, bf16[5,384,256]{2,1,0:T(8,128)(2,1)S(1)}, u32[]{:S(2)}, u32[]{:S(2)}) collective-permute-start(bf16[5,384,256]{2,1,0:T(8,128)(2,1)S(1)} %copy-done.1), channel_id=1, source_target_pairs={{12,16},{13,17},{14,18},{15,19},{16,12},{17,13},{18,14},{19,15}} | collective-permute-start | bytes 2949128 | tf_op jit(solution)/shard_map/ppermute | solution.py:538
  67.7 48.7 %collective-permute-start.15 = (bf16[4,384,256]{2,1,0:T(8,128)(2,1)S(1)}, bf16[4,384,256]{2,1,0:T(8,128)(2,1)S(1)}, u32[]{:S(2)}, u32[]{:S(2)}) collective-permute-start(bf16[4,384,256]{2,1,0:T(8,128)(2,1)S(1)} %get-tuple-element.63), channel_id=1, source_target_pairs={{4,0},{5,1},{6,2},{7,3},{8,4},{9,5},{10,6},{11,7},{12,8},{13,9},{1... | collective-permute-start | bytes 2359304 | tf_op jit(solution)/shard_map/ppermute | solution.py:538
  97.5 20.5 %collective-permute-start.16 = (bf16[4,384,256]{2,1,0:T(8,128)(2,1)S(1)}, bf16[4,384,256]{2,1,0:T(8,128)(2,1)S(1)}, u32[]{:S(2)}, u32[]{:S(2)}) collective-permute-start(bf16[4,384,256]{2,1,0:T(8,128)(2,1)S(1)} %get-tuple-element.64), channel_id=1, source_target_pairs={{12,16},{13,17},{14,18},{15,19},{16,12},{17,13},{18,14},{19,15}} | collective-permute-start | bytes 2359304 | tf_op jit(solution)/shard_map/ppermute | solution.py:538
  99.4 37.2 %collective-permute-start.17 = (bf16[4,384,256]{2,1,0:T(8,128)(2,1)S(1)}, bf16[4,384,256]{2,1,0:T(8,128)(2,1)S(1)}, u32[]{:S(2)}, u32[]{:S(2)}) collective-permute-start(bf16[4,384,256]{2,1,0:T(8,128)(2,1)S(1)} %get-tuple-element.64), channel_id=1, source_target_pairs={{0,4},{1,5},{2,6},{3,7},{4,8},{5,9},{6,10},{7,11},{8,12},{9,13},{1... | collective-permute-start | bytes 2359304 | tf_op jit(solution)/shard_map/ppermute | solution.py:538
  (3 other events, 8.1 us)

commit v6 on v4

--- a/solution.py
+++ b/solution.py
@@ -143,9 +143,9 @@
         out_specs=[vmem] * (1 + len(extras)),
         out_shape=[jax.ShapeDtypeStruct((rows, tiles, ext, LANES), jnp.float32)] + [border] * len(extras),
         scratch_shapes=[
-            pltpu.VMEM((rows * tiles, back - REACH + 8 * seg, LANES), jnp.float32),
-            pltpu.VMEM((rows * tiles, 8 * seg, LANES), jnp.float32),
-            pltpu.VMEM((rows * tiles, 8 * seg, LANES), jnp.float32),
+            pltpu.VMEM((rows * tiles, round_up(back - REACH + 9 * seg, 8), LANES), jnp.float32),
+            pltpu.VMEM((rows * tiles, round_up(9 * seg, 8), LANES), jnp.float32),
+            pltpu.VMEM((rows * tiles, round_up(9 * seg, 8), LANES), jnp.float32),
         ],
         compiler_params=pltpu.CompilerParams(vmem_limit_bytes=28 * MIB),
         cost_estimate=pl.CostEstimate(flops=1000, bytes_accessed=1000, transcendentals=0),

time: 143 us -> 143 us (level)
  no operation moved by 1% of the time
where the time goes in v6:
time: 143 us; the launch traced here: 142 us
  starting transfers between devices  43.4 us (30%)
  Pallas kernels  42.4 us (30%)
  waiting for transfers between devices  42.2 us (30%)
  local copies, waits for them, and re-layouts  8.37 us (6%)
  other arithmetic  5.38 us (4%)
    ppermute x16, starting transfers between devices, move(): return lax.ppermute(cells, axes, pairs)  42.6 us
    ppermute x16, waiting for transfers between devices, move(): return lax.ppermute(cells, axes, pairs)  42.2 us
    pallas_call x1, Pallas kernels, interior(): pl.pallas_call(functools.partial(interior_kernel, rows, lon, ext), in_spe...  15.7 us
    pallas_call x2, Pallas kernels, border_rows(): pl.pallas_call(functools.partial(border_kernel, outer, rows, lon, ext), i...  12.5 us
    pallas_call x2, Pallas kernels, finish(): pl.pallas_call(functools.partial(finish_kernel, outer, rows, lon, ext), i...  10.4 us
    convert_element_type x1, local copies, waits for them, and re-layouts, per_device(): rows_of(cells, i).astype(jnp.bfloat16)  4.25 us
    pallas_call x4, Pallas kernels, smooth_piece(): pl.pallas_call(functools.partial(smooth_kernel, geo, len(extras)), grid=(...  3.76 us
  transfers between devices with their start and end apart: 18, of which 4 were waited for; matrix products, arithmetic and copies ran while one was open for 8% of the time, Pallas kernels for 26%

profile of v6, /device:TPU:21, one launch (start us, length us, event | category | flops | bytes accessed | tf_op | source)
XLA Modules:
  0.0 142.4 jit_solution(12189200410130487850)
XLA Ops:
  2.6 1.4 %dynamic-slice_convert_fusion.4.own_ref = bf16[4,360,256]{2,1,0:T(8,128)(2,1)S(1)} fusion(f32[16,360,256]{2,1,0:T(8,128)} %state_ref.5, s32[]{:T(128)S(6)} %select_n.73), kind=kLoop, calls=%fused_computation.7 | loop fusion | bytes 1474564 | tf_op jit(solution)/shard_map/convert_element_type | solution.py:569
  4.1 1.5 %collective-permute-start.3 = (bf16[4,360,256]{2,1,0:T(8,128)(2,1)S(1)}, bf16[4,360,256]{2,1,0:T(8,128)(2,1)}, u32[]{:S(2)}, u32[]{:S(2)}) collective-permute-start(bf16[4,360,256]{2,1,0:T(8,128)(2,1)S(1)} %dynamic-slice_convert_fusion.4.own_ref), channel_id=1, source_target_pairs={{0,2},{1,3},{2,0},{3,1},{4,6},{5,7},{6,4},{7,5},{24,26},{25,27},{2... | collective-permute-start | bytes 2211848 | tf_op jit(solution)/shard_map/ppermute | solution.py:538
  5.8 4.2 %dynamic-slice_convert_fusion.1 = (bf16[4,360,256]{2,1,0:T(8,128)(2,1)}, bf16[4,360,256]{2,1,0:T(8,128)(2,1)}, bf16[4,360,256]{2,1,0:T(8,128)(2,1)S(1)}, bf16[4,360,256]{2,1,0:T(8,128)(2,1)S(1)}) fusion(f32[16,360,256]{2,1,0:T(8,128)} %state_ref.5, s32[]{:T(128)S(6)} %select_n.76, s32[]{:T(128)S(6)} %select_n.77, s32[]{:T(128)S(6)} %select_n.73, s32[]{:T(128)S(6)} %select_n.69), kind=kLoop, calls=%fused_computation.4 | loop fusion | bytes 5898256 | tf_op jit(solution)/shard_map/convert_element_type | solution.py:572
  10.7 1.8 %maximum_maximum_fusion.2 = (bf16[5,384,256]{2,1,0:T(8,128)(2,1)}, bf16[5,384,256]{2,1,0:T(8,128)(2,1)}) fusion(bf16[1,384,128]{2,1,0:T(8,128)(2,1)S(1)} %get-tuple-element.77, bf16[1,384,128]{2,1,0:T(8,128)(2,1)S(1)} %get-tuple-element.75, bf16[4,8,256]{2,1,0:T(8,128)(2,1)S(1)} %get-tuple-element.83, bf16[4,360,256]{2,1,0:T(8,128)(2,1)S(1)} %get-tuple-element.42.own_ref, ...), kind=kLoop, calls=%fused_computation.9 | loop fusion | flops 11304960 | bytes 3903232 | tf_op jit(solution)/shard_map/concatenate | solution.py:585
  12.4 1.2 pad_maximum_fusion
  13.7 1.9 %collective-permute-start.2 = (bf16[8,360,256]{2,1,0:T(8,128)(2,1)}, bf16[8,360,256]{2,1,0:T(8,128)(2,1)}, u32[]{:S(2)}, u32[]{:S(2)}) collective-permute-start(bf16[8,360,256]{2,1,0:T(8,128)(2,1)} %pad_maximum_fusion), channel_id=1, source_target_pairs={{0,1},{1,0},{2,3},{3,2},{4,5},{5,4},{6,7},{7,6},{24,25},{25,24},{2... | collective-permute-start | bytes 4423688 | tf_op jit(solution)/shard_map/ppermute | solution.py:538
  16.2 1.6 %pad_maximum_fusion.1.own_ref = bf16[8,360,256]{2,1,0:T(8,128)(2,1)S(1)} fusion(bf16[4,360,256]{2,1,0:T(8,128)(2,1)} %get-tuple-element.70, bf16[4,360,256]{2,1,0:T(8,128)(2,1)} %get-tuple-element.69), kind=kLoop, calls=%fused_computation.2 | loop fusion | flops 737280 | bytes 2949120 | tf_op jit(solution)/shard_map/concatenate | solution.py:617
  19.4 3.2 %collective-permute-start.9 = (bf16[5,384,256]{2,1,0:T(8,128)(2,1)S(1)}, bf16[5,384,256]{2,1,0:T(8,128)(2,1)S(1)}, u32[]{:S(2)}, u32[]{:S(2)}) collective-permute-start(bf16[5,384,256]{2,1,0:T(8,128)(2,1)S(1)} %copy-done.2), channel_id=1, source_target_pairs={{8,4},{9,5},{10,6},{11,7},{12,8},{13,9},{14,10},{15,11},{16,20},{1... | collective-permute-start | bytes 2949128 | tf_op jit(solution)/shard_map/ppermute | solution.py:538
  22.9 1.5 %smooth.4 = (f32[4,2,384,128]{3,2,1,0:T(8,128)S(1)}, bf16[5,384,256]{2,1,0:T(8,128)(2,1)S(1)}) custom-call(s32[6]{0:T(128)S(1)} %stack.39.info_ref, s32[4]{0:T(128)S(1)} %get-tuple-element.92.widths_ref, bf16[4,360,256]{2,1,0:T(8,128)(2,1)S(1)} %dynamic-slice_convert_fusion.4.own_ref, bf16[8,360,256]{2,1,0:T(8,128)(2,1)} %collective-permute-done.2.sib_ref, ...), custom_call_target="tpu_custom_call" | custom-call | flops 1000 | bytes 1000 | tf_op jit(solution)/shard_map/smooth/pallas_call | solution.py:139
  26.0 1.3 collective-permute-start.11
  28.2 1.1 smooth.5
  29.4 12.5 %collective-permute-done.9.raw_ref = bf16[5,384,256]{2,1,0:T(8,128)(2,1)S(1)} collective-permute-done((bf16[5,384,256]{2,1,0:T(8,128)(2,1)S(1)}, bf16[5,384,256]{2,1,0:T(8,128)(2,1)S(1)}, u32[]{:S(2)}, u32[]{:S(2)}) %collective-permute-start.9) | collective-permute-done | bytes 983072 | tf_op jit(solution)/shard_map/ppermute | solution.py:538
  43.4 14.7 %collective-permute-done.11.raw_ref.across_ref.across_raw_ref = bf16[5,384,256]{2,1,0:T(8,128)(2,1)S(1)} collective-permute-done((bf16[5,384,256]{2,1,0:T(8,128)(2,1)S(1)}, bf16[5,384,256]{2,1,0:T(8,128)(2,1)S(1)}, u32[]{:S(2)}, u32[]{:S(2)}) %collective-permute-start.11) | collective-permute-done | bytes 983072 | tf_op jit(solution)/shard_map/ppermute | solution.py:538
  58.9 1.9 %collective-permute-start.14 = (bf16[5,384,256]{2,1,0:T(8,128)(2,1)S(1)}, bf16[5,384,256]{2,1,0:T(8,128)(2,1)S(1)}, u32[]{:S(2)}, u32[]{:S(2)}) collective-permute-start(bf16[5,384,256]{2,1,0:T(8,128)(2,1)S(1)} %copy-done.1), channel_id=1, source_target_pairs={{12,16},{13,17},{14,18},{15,19},{16,12},{17,13},{18,14},{19,15}} | collective-permute-start | bytes 2949128 | tf_op jit(solution)/shard_map/ppermute | solution.py:538
  61.4 6.3 %border_outer.1 = (bf16[4,384,256]{2,1,0:T(8,128)(2,1)S(1)}, f32[4,2,384,128]{3,2,1,0:T(8,128)S(1)}, f32[4,2,384,128]{3,2,1,0:T(8,128)S(1)}) custom-call(s32[6]{0:T(128)S(1)} %stack.39.info_ref, f32[16,360,256]{2,1,0:T(8,128)S(1)} %bitcast.7, bf16[16,8,256]{2,1,0:T(8,128)(2,1)S(1)} %slice.48.edge_w_ref, bf16[16,8,256]{2,1,0:T(8,128)(2,1)S(1)} %slice.49.edge_e_ref, ...), custom_call_target="tpu_custom_call" | custom-call | flops 1000 | bytes 1000 | tf_op jit(solution)/shard_map/border_outer/pallas_call | solution.py:332
  67.7 23.4 %collective-permute-start.15 = (bf16[4,384,256]{2,1,0:T(8,128)(2,1)S(1)}, bf16[4,384,256]{2,1,0:T(8,128)(2,1)S(1)}, u32[]{:S(2)}, u32[]{:S(2)}) collective-permute-start(bf16[4,384,256]{2,1,0:T(8,128)(2,1)S(1)} %get-tuple-element.63), channel_id=1, source_target_pairs={{4,0},{5,1},{6,2},{7,3},{8,4},{9,5},{10,6},{11,7},{12,8},{13,9},{1... | collective-permute-start | bytes 2359304 | tf_op jit(solution)/shard_map/ppermute | solution.py:538
  91.7 6.3 %border_inner.1 = (bf16[4,384,256]{2,1,0:T(8,128)(2,1)S(1)}, f32[4,2,384,128]{3,2,1,0:T(8,128)S(1)}, f32[4,2,384,128]{3,2,1,0:T(8,128)S(1)}) custom-call(s32[6]{0:T(128)S(1)} %stack.39.info_ref, f32[16,360,256]{2,1,0:T(8,128)S(1)} %bitcast.7, bf16[16,8,256]{2,1,0:T(8,128)(2,1)S(1)} %slice.48.edge_w_ref, bf16[16,8,256]{2,1,0:T(8,128)(2,1)S(1)} %slice.49.edge_e_ref, ...), custom_call_target="tpu_custom_call" | custom-call | flops 1000 | bytes 1000 | tf_op jit(solution)/shard_map/border_inner/pallas_call | solution.py:332
  98.0 1.9 %collective-permute-start.16 = (bf16[4,384,256]{2,1,0:T(8,128)(2,1)S(1)}, bf16[4,384,256]{2,1,0:T(8,128)(2,1)S(1)}, u32[]{:S(2)}, u32[]{:S(2)}) collective-permute-start(bf16[4,384,256]{2,1,0:T(8,128)(2,1)S(1)} %get-tuple-element.64), channel_id=1, source_target_pairs={{12,16},{13,17},{14,18},{15,19},{16,12},{17,13},{18,14},{19,15}} | collective-permute-start | bytes 2359304 | tf_op jit(solution)/shard_map/ppermute | solution.py:538
  99.9 1.3 collective-permute-start.17
  101.2 15.7 %interior.1 = (bf16[16,360,256]{2,1,0:T(8,128)(2,1)}, f32[4,2,384,128]{3,2,1,0:T(8,128)S(1)}, f32[4,2,384,128]{3,2,1,0:T(8,128)S(1)}) custom-call(s32[6]{0:T(128)S(1)} %stack.39.info_ref, f32[16,360,256]{2,1,0:T(8,128)S(1)} %bitcast.7, bf16[16,8,256]{2,1,0:T(8,128)(2,1)S(1)} %slice.48.edge_w_ref, bf16[16,8,256]{2,1,0:T(8,128)(2,1)S(1)} %slice.49.edge_e_ref, ...), custom_call_target="tpu_custom_call" | custom-call | flops 1000 | bytes 1000 | tf_op jit(solution)/shard_map/interior/pallas_call | solution.py:421
  116.9 1.5 %collective-permute-done.16.across_ref = bf16[4,384,256]{2,1,0:T(8,128)(2,1)S(1)} collective-permute-done((bf16[4,384,256]{2,1,0:T(8,128)(2,1)S(1)}, bf16[4,384,256]{2,1,0:T(8,128)(2,1)S(1)}, u32[]{:S(2)}, u32[]{:S(2)}) %collective-permute-start.16) | collective-permute-done | bytes 786464 | tf_op jit(solution)/shard_map/ppermute | solution.py:538
  118.4 5.2 %finish_inner.1._ = bf16[16,360,256]{2,1,0:T(8,128)(2,1)} custom-call(bf16[16,360,256]{2,1,0:T(8,128)(2,1)} %get-tuple-element.62._, s32[6]{0:T(128)S(1)} %stack.39.info_ref, bf16[16,384,128]{2,1,0:T(8,128)(2,1)S(1)} %maximum_maximum_fusion.winds_ref, bf16[5,384,256]{2,1,0:T(8,128)(2,1)S(1)} %collective-permute-done.8.late_ref, ...), custom_call_target="tpu_custom_call", output_to_operand_aliasing={{}: (0, {})} | custom-call | flops 1000 | bytes 1000 | tf_op jit(solution)/shard_map/finish_inner/pallas_call | solution.py:478
  123.6 13.4 %collective-permute-done.17.border_ref.across_ref = bf16[4,384,256]{2,1,0:T(8,128)(2,1)S(1)} collective-permute-done((bf16[4,384,256]{2,1,0:T(8,128)(2,1)S(1)}, bf16[4,384,256]{2,1,0:T(8,128)(2,1)S(1)}, u32[]{:S(2)}, u32[]{:S(2)}) %collective-permute-start.17) | collective-permute-done | bytes 786464 | tf_op jit(solution)/shard_map/ppermute | solution.py:538
  137.1 5.2 %finish_outer.1 = bf16[16,360,256]{2,1,0:T(8,128)(2,1)} custom-call(bf16[16,360,256]{2,1,0:T(8,128)(2,1)} %finish_inner.1._, s32[6]{0:T(128)S(1)} %stack.39.info_ref, bf16[16,384,128]{2,1,0:T(8,128)(2,1)S(1)} %maximum_maximum_fusion.winds_ref, bf16[5,384,256]{2,1,0:T(8,128)(2,1)S(1)} %collective-permute-done.10.late_ref, ...), custom_call_target="tpu_custom_call", output_to_operand_aliasing={{}: (0, {})} | custom-call | flops 1000 | bytes 1000 | tf_op jit(solution)/shard_map/finish_outer/pallas_call | solution.py:478
  (74 shorter events, 11.6 us)
Async XLA Ops:
  1.8 8.2 %collective-permute-start = (bf16[16,8,384]{2,1,0:T(8,128)(2,1)S(1)}, bf16[16,8,384]{2,1,0:T(8,128)(2,1)S(1)}, u32[]{:S(2)}, u32[]{:S(2)}) collective-permute-start(bf16[16,8,384]{2,1,0:T(8,128)(2,1)S(1)} %get-tuple-element.38), channel_id=1, source_target_pairs={{0,1},{1,2},{2,3},{3,0},{4,5},{5,6},{6,7},{7,4},{8,9},{9,10},{10,1... | collective-permute-start | bytes 294920 | tf_op jit(solution)/shard_map/ppermute | solution.py:566
  2.6 7.4 %collective-permute-start.1 = (bf16[16,8,384]{2,1,0:T(8,128)(2,1)S(1)}, bf16[16,8,384]{2,1,0:T(8,128)(2,1)S(1)}, u32[]{:S(2)}, u32[]{:S(2)}) collective-permute-start(bf16[16,8,384]{2,1,0:T(8,128)(2,1)S(1)} %get-tuple-element.39), channel_id=1, source_target_pairs={{1,0},{2,1},{3,2},{0,3},{5,4},{6,5},{7,6},{4,7},{9,8},{10,9},{11,1... | collective-permute-start | bytes 294920 | tf_op jit(solution)/shard_map/ppermute | solution.py:565
  4.1 14.4 %collective-permute-start.3 = (bf16[4,360,256]{2,1,0:T(8,128)(2,1)S(1)}, bf16[4,360,256]{2,1,0:T(8,128)(2,1)}, u32[]{:S(2)}, u32[]{:S(2)}) collective-permute-start(bf16[4,360,256]{2,1,0:T(8,128)(2,1)S(1)} %dynamic-slice_convert_fusion.4.own_ref), channel_id=1, source_target_pairs={{0,2},{1,3},{2,0},{3,1},{4,6},{5,7},{6,4},{7,5},{24,26},{25,27},{2... | collective-permute-start | bytes 2211848 | tf_op jit(solution)/shard_map/ppermute | solution.py:538
  5.8 4.4 %copy-start = (bf16[16,360,128]{2,1,0:T(8,128)(2,1)S(1)}, bf16[16,360,128]{2,1,0:T(8,128)(2,1)}, u32[]{:S(2)}) copy-start(bf16[16,360,128]{2,1,0:T(8,128)(2,1)} %param.5) | copy-start | bytes 4423684
  13.7 5.5 %copy-start.5 = (s32[128]{0:T(128)S(1)}, s32[128]{0:T(128)}, u32[]{:S(2)}) copy-start(s32[128]{0:T(128)} %param.7) | copy-start | bytes 1540
  13.7 9.1 %collective-permute-start.2 = (bf16[8,360,256]{2,1,0:T(8,128)(2,1)}, bf16[8,360,256]{2,1,0:T(8,128)(2,1)}, u32[]{:S(2)}, u32[]{:S(2)}) collective-permute-start(bf16[8,360,256]{2,1,0:T(8,128)(2,1)} %pad_maximum_fusion), channel_id=1, source_target_pairs={{0,1},{1,0},{2,3},{3,2},{4,5},{5,4},{6,7},{7,6},{24,25},{25,24},{2... | collective-permute-start | bytes 4423688 | tf_op jit(solution)/shard_map/ppermute | solution.py:538
  16.2 3.2 %copy-start.2 = (bf16[5,384,256]{2,1,0:T(8,128)(2,1)S(1)}, bf16[5,384,256]{2,1,0:T(8,128)(2,1)}, u32[]{:S(2)}) copy-start(bf16[5,384,256]{2,1,0:T(8,128)(2,1)} %get-tuple-element.86) | copy-start | bytes 2949124
  16.2 6.6 %copy-start.4 = (bf16[1,384,128]{2,1,0:T(8,128)(2,1)S(1)}, bf16[1,384,128]{2,1,0:T(8,128)(2,1)}, u32[]{:S(2)}) copy-start(bf16[1,384,128]{2,1,0:T(8,128)(2,1)} %copy-done.3) | copy-start | bytes 294916
  17.8 6.6 %collective-permute-start.5 = (bf16[4,360,256]{2,1,0:T(8,128)(2,1)S(1)}, bf16[4,360,256]{2,1,0:T(8,128)(2,1)S(1)}, u32[]{:S(2)}, u32[]{:S(2)}) collective-permute-start(bf16[4,360,256]{2,1,0:T(8,128)(2,1)S(1)} %get-tuple-element.42.own_ref), channel_id=1, source_target_pairs={{0,2},{1,3},{2,0},{3,1},{4,6},{5,7},{6,4},{7,5},{24,26},{25,27},{2... | collective-permute-start | bytes 2211848 | tf_op jit(solution)/shard_map/ppermute | solution.py:538
  18.5 4.3 %collective-permute-start.4 = (bf16[4,360,256]{2,1,0:T(8,128)(2,1)}, bf16[4,360,256]{2,1,0:T(8,128)(2,1)S(1)}, u32[]{:S(2)}, u32[]{:S(2)}) collective-permute-start(bf16[4,360,256]{2,1,0:T(8,128)(2,1)} %collective-permute-done.3.opp_ref), channel_id=1, source_target_pairs={{0,1},{1,0},{2,3},{3,2},{4,5},{5,4},{6,7},{7,6},{24,25},{25,24},{2... | collective-permute-start | bytes 2211848 | tf_op jit(solution)/shard_map/ppermute | solution.py:538
  19.4 22.5 %collective-permute-start.9 = (bf16[5,384,256]{2,1,0:T(8,128)(2,1)S(1)}, bf16[5,384,256]{2,1,0:T(8,128)(2,1)S(1)}, u32[]{:S(2)}, u32[]{:S(2)}) collective-permute-start(bf16[5,384,256]{2,1,0:T(8,128)(2,1)S(1)} %copy-done.2), channel_id=1, source_target_pairs={{8,4},{9,5},{10,6},{11,7},{12,8},{13,9},{14,10},{15,11},{16,20},{1... | collective-permute-start | bytes 2949128 | tf_op jit(solution)/shard_map/ppermute | solution.py:538
  22.8 38.5 %slice-start = ((s8[5898240]{0:T(1024)(128)(4,1)}), s8[4194304]{0:T(1024)(128)(4,1)S(1)}, s32[]{:S(2)}) async-start(s8[5898240]{0:T(1024)(128)(4,1)} %bitcast.6), calls=%async_computation | async-start | bytes 8388608
  24.4 3.8 %collective-permute-start.6 = (bf16[4,360,256]{2,1,0:T(8,128)(2,1)S(1)}, bf16[4,360,256]{2,1,0:T(8,128)(2,1)S(1)}, u32[]{:S(2)}, u32[]{:S(2)}) collective-permute-start(bf16[4,360,256]{2,1,0:T(8,128)(2,1)S(1)} %collective-permute-done.5.opp_ref), channel_id=1, source_target_pairs={{0,1},{1,0},{2,3},{3,2},{4,5},{5,4},{6,7},{7,6},{24,25},{25,24},{2... | collective-permute-start | bytes 2211848 | tf_op jit(solution)/shard_map/ppermute | solution.py:538
  25.2 18.2 %collective-permute-start.7 = (bf16[8,360,256]{2,1,0:T(8,128)(2,1)S(1)}, bf16[8,360,256]{2,1,0:T(8,128)(2,1)S(1)}, u32[]{:S(2)}, u32[]{:S(2)}) collective-permute-start(bf16[8,360,256]{2,1,0:T(8,128)(2,1)S(1)} %pad_maximum_fusion.1.own_ref), channel_id=1, source_target_pairs={{0,2},{1,3},{2,0},{3,1},{4,6},{5,7},{6,4},{7,5},{24,26},{25,27},{2... | collective-permute-start | bytes 4423688 | tf_op jit(solution)/shard_map/ppermute | solution.py:538
  26.0 32.1 %collective-permute-start.11 = (bf16[5,384,256]{2,1,0:T(8,128)(2,1)S(1)}, bf16[5,384,256]{2,1,0:T(8,128)(2,1)S(1)}, u32[]{:S(2)}, u32[]{:S(2)}) collective-permute-start(bf16[5,384,256]{2,1,0:T(8,128)(2,1)S(1)} %copy-done.1), channel_id=1, source_target_pairs={{8,12},{9,13},{10,14},{11,15},{20,16},{21,17},{22,18},{23,19}} | collective-permute-start | bytes 2949128 | tf_op jit(solution)/shard_map/ppermute | solution.py:538
  27.3 34.0 %slice-start.1 = ((s8[5898240]{0:T(1024)(128)(4,1)}), s8[1703936]{0:T(1024)(128)(4,1)S(1)}, s32[]{:S(2)}) async-start(s8[5898240]{0:T(1024)(128)(4,1)} %bitcast.6), calls=%async_computation.1 | async-start | bytes 3407872
  27.3 30.8 %collective-permute-start.8 = (bf16[5,384,256]{2,1,0:T(8,128)(2,1)S(1)}, bf16[5,384,256]{2,1,0:T(8,128)(2,1)S(1)}, u32[]{:S(2)}, u32[]{:S(2)}) collective-permute-start(bf16[5,384,256]{2,1,0:T(8,128)(2,1)S(1)} %get-tuple-element.50), channel_id=1, source_target_pairs={{4,0},{5,1},{6,2},{7,3},{24,28},{25,29},{26,30},{27,31}} | collective-permute-start | bytes 2949128 | tf_op jit(solution)/shard_map/ppermute | solution.py:538
  41.9 16.2 %collective-permute-start.10 = (bf16[5,384,256]{2,1,0:T(8,128)(2,1)S(1)}, bf16[5,384,256]{2,1,0:T(8,128)(2,1)S(1)}, u32[]{:S(2)}, u32[]{:S(2)}) collective-permute-start(bf16[5,384,256]{2,1,0:T(8,128)(2,1)S(1)} %get-tuple-element.52), channel_id=1, source_target_pairs={{0,4},{1,5},{2,6},{3,7},{4,8},{5,9},{6,10},{7,11},{24,20},{25,21},... | collective-permute-start | bytes 2949128 | tf_op jit(solution)/shard_map/ppermute | solution.py:538
  42.6 18.2 %collective-permute-start.12 = (bf16[8,360,256]{2,1,0:T(8,128)(2,1)S(1)}, bf16[8,360,256]{2,1,0:T(8,128)(2,1)S(1)}, u32[]{:S(2)}, u32[]{:S(2)}) collective-permute-start(bf16[8,360,256]{2,1,0:T(8,128)(2,1)S(1)} %pad_maximum_fusion.1.own_ref), channel_id=1, source_target_pairs={{0,1},{1,0},{2,3},{3,2},{4,5},{5,4},{6,7},{7,6},{24,25},{25,24},{2... | collective-permute-start | bytes 4423688 | tf_op jit(solution)/shard_map/ppermute | solution.py:538
  58.1 2.7 %collective-permute-start.13 = (bf16[8,360,256]{2,1,0:T(8,128)(2,1)S(1)}, bf16[8,360,256]{2,1,0:T(8,128)(2,1)S(1)}, u32[]{:S(2)}, u32[]{:S(2)}) collective-permute-start(bf16[8,360,256]{2,1,0:T(8,128)(2,1)S(1)} %collective-permute-done.7.opp_ref), channel_id=1, source_target_pairs={{0,1},{1,0},{2,3},{3,2},{4,5},{5,4},{6,7},{7,6},{24,25},{25,24},{2... | collective-permute-start | bytes 4423688 | tf_op jit(solution)/shard_map/ppermute | solution.py:538
  58.9 32.8 %collective-permute-start.14 = (bf16[5,384,256]{2,1,0:T(8,128)(2,1)S(1)}, bf16[5,384,256]{2,1,0:T(8,128)(2,1)S(1)}, u32[]{:S(2)}, u32[]{:S(2)}) collective-permute-start(bf16[5,384,256]{2,1,0:T(8,128)(2,1)S(1)} %copy-done.1), channel_id=1, source_target_pairs={{12,16},{13,17},{14,18},{15,19},{16,12},{17,13},{18,14},{19,15}} | collective-permute-start | bytes 2949128 | tf_op jit(solution)/shard_map/ppermute | solution.py:538
  67.7 49.2 %collective-permute-start.15 = (bf16[4,384,256]{2,1,0:T(8,128)(2,1)S(1)}, bf16[4,384,256]{2,1,0:T(8,128)(2,1)S(1)}, u32[]{:S(2)}, u32[]{:S(2)}) collective-permute-start(bf16[4,384,256]{2,1,0:T(8,128)(2,1)S(1)} %get-tuple-element.63), channel_id=1, source_target_pairs={{4,0},{5,1},{6,2},{7,3},{8,4},{9,5},{10,6},{11,7},{12,8},{13,9},{1... | collective-permute-start | bytes 2359304 | tf_op jit(solution)/shard_map/ppermute | solution.py:538
  98.0 20.5 %collective-permute-start.16 = (bf16[4,384,256]{2,1,0:T(8,128)(2,1)S(1)}, bf16[4,384,256]{2,1,0:T(8,128)(2,1)S(1)}, u32[]{:S(2)}, u32[]{:S(2)}) collective-permute-start(bf16[4,384,256]{2,1,0:T(8,128)(2,1)S(1)} %get-tuple-element.64), channel_id=1, source_target_pairs={{12,16},{13,17},{14,18},{15,19},{16,12},{17,13},{18,14},{19,15}} | collective-permute-start | bytes 2359304 | tf_op jit(solution)/shard_map/ppermute | solution.py:538
  99.9 37.2 %collective-permute-start.17 = (bf16[4,384,256]{2,1,0:T(8,128)(2,1)S(1)}, bf16[4,384,256]{2,1,0:T(8,128)(2,1)S(1)}, u32[]{:S(2)}, u32[]{:S(2)}) collective-permute-start(bf16[4,384,256]{2,1,0:T(8,128)(2,1)S(1)} %get-tuple-element.64), channel_id=1, source_target_pairs={{0,4},{1,5},{2,6},{3,7},{4,8},{5,9},{6,10},{7,11},{8,12},{9,13},{1... | collective-permute-start | bytes 2359304 | tf_op jit(solution)/shard_map/ppermute | solution.py:538
  (3 other events, 8.1 us)
